TPU v7x, 32 devices: a whole 2x2x4 slice. The times are simulated.
32 devices in a mesh: groups: 2 (over x), sites: 16 (over z, y, core).
Axes of the slice: x: 2, y: 2, z: 4, core: 2. Of those that a mesh axis runs over, the one named last changes fastest.
Arguments:
- tip_probs: bfloat16 [128, 20, 8192], P(('groups', 'sites')), parts along dimension 0, may hold values from 0.02 to 600, as said below
- leaf_order: int32 [128], P('groups'), parts along dimension 0, may hold values from 0 to 63, each once
- site_weights: int32 [16384], P(('groups', 'sites')), parts along dimension 0, may hold values from 1 to 10
- branch_length: float32 [252], P('groups'), parts along dimension 0, may hold values from 0.02 to 0.6
- direction: float32 [252], P('groups'), parts along dimension 0, may hold values from -6 to 6
Outputs:
- gradient: float32 [252], P('groups'), parts along dimension 0
- hess_vec: float32 [252], P('groups'), parts along dimension 0
There are 2 independent parts, one for each index of `groups`. A program takes and returns all parts, laid end to end along the dimension named above; each array names one. Nothing has to cross between parts.
Inputs may be any that keep to these rules, and one draw needn't show every extreme that they name: `tip_probs`: positive state likelihoods.
All inputs are finite; a program needn't handle non-finite values.
Results may differ from a plain program's by a relative error of at most 0.0003.
Values may be sent and summed in bfloat16 or wider, within the bound.
No kernel may reach another device: no remote copies, remote signals or barrier semaphores. Data moves between devices by JAX's collectives and lax.ppermute only.
A program may use at most 128 MiB of HBM per device.

v0:
```python
import functools
import jax
import jax.numpy as jnp
from jax import lax
from jax.experimental import pallas as pl
from jax.experimental.pallas import tpu as pltpu
from jax.sharding import PartitionSpec as P

F32 = jnp.float32
LANES = 128
ROWS = 8


def deal_kernel(tips_ref, out_ref, wide_ref):
    states, tips, span = tips_ref.shape
    per_row = span // LANES
    rows = states * per_row
    for state in range(states):
        for part in range(per_row):
            wide_ref[pl.ds(state * per_row + part, tips, rows), :] = tips_ref[
                state, :, part * LANES : (part + 1) * LANES
            ].astype(F32)
    out_ref[0] = wide_ref[...].astype(out_ref.dtype)


def deal(tip_probs, peers):
    states, tips, sites = tip_probs.shape
    span = sites // peers
    rows = states * span // LANES
    return pl.pallas_call(
        deal_kernel,
        grid=(peers,),
        in_specs=[pl.BlockSpec((states, tips, span), lambda i: (0, 0, i))],
        out_specs=pl.BlockSpec((1, tips * rows, LANES), lambda i: (i, 0, 0)),
        out_shape=jax.ShapeDtypeStruct((peers, tips * rows, LANES), tip_probs.dtype),
        scratch_shapes=[pltpu.VMEM((tips * rows, LANES), F32)],
        name="deal_tips",
    )(tip_probs)


def part_sum(x):
    return jnp.sum(x, axis=0)


def both(half):
    return half + pltpu.roll(half, half.shape[0] // 2, 0)


def prune_kernel(
    order_ref, x_ref, weight_ref, length_ref, toward_ref, out_ref,
    rate_ref, slope_ref, sums_ref, dsums_ref, y_ref, dy_ref, adj_ref, dadj_ref, norm_ref, grad_ref, curve_ref,
    *, tips, states,
):
    blocks = states * 4 // ROWS
    decay = states / (states - 1.0)
    branches = length_ref.shape[1]
    length = length_ref[...]
    toward = toward_ref[...]
    grow = jnp.exp(decay * length)
    pad = LANES - branches

    def column(row):
        wide = jnp.concatenate([row, jnp.zeros((1, pad), F32)], axis=1)
        return jnp.transpose(jnp.broadcast_to(wide, (LANES, LANES)))

    rate_ref[...] = column((grow - 1.0) / states)
    slope_ref[...] = column(decay * toward * grow / states)
    grad_ref[...] = jnp.zeros_like(grad_ref)
    curve_ref[...] = jnp.zeros_like(curve_ref)
    raw = weight_ref[...].astype(F32)
    quarter = [raw[:, part * LANES : (part + 1) * LANES] for part in range(4)]
    weight = jnp.concatenate(quarter + quarter, axis=0)

    offsets = [0]
    size = tips
    while size > 1:
        offsets.append(offsets[-1] + size)
        size //= 2

    def row(ref, at):
        return jnp.broadcast_to(ref[pl.ds(at, 1), :], (ROWS, LANES))

    def leaf(slot):
        tip = order_ref[slot]
        x = x_ref[tip].astype(F32).reshape(blocks, ROWS, LANES)
        total = both(part_sum(x))
        lift = row(rate_ref, tip) * total
        y = x + lift[None]
        y_ref[slot] = y
        sums_ref[slot] = total
        return y, row(slope_ref, tip) * total, total + states * lift

    def cherry(k):
        ya, qa, ta = leaf(2 * k)
        yb, qb, tb = leaf(2 * k + 1)
        z = ya * yb
        dz = qa[None] * yb + qb[None] * ya
        return z, dz, both(part_sum(z)), qa * tb + qb * ta

    def inner(at, z, dz, total, dtotal):
        rate, slope = row(rate_ref, at), row(slope_ref, at)
        y = z + (rate * total)[None]
        dy = dz + (rate * dtotal + slope * total)[None]
        y_ref[at] = y
        dy_ref[at - tips] = dy
        sums_ref[at] = total
        dsums_ref[at - tips] = dtotal
        return y, dy

    def join(left, right):
        (ya, dya), (yb, dyb) = left, right
        z = ya * yb
        dz = dya * yb + ya * dyb
        return z, dz, both(part_sum(z)), both(part_sum(dz))

    def climb(level, k, low):
        if level == 1:
            return cherry(k)
        kids = []
        for child in (2 * k, 2 * k + 1):
            kids.append(inner(offsets[level - 1] + child, *climb(level - 1, child, low)))
        return join(*kids)

    levels = len(offsets) - 1
    cut = 3

    def up(k, carry):
        z, dz, total, dtotal = climb(cut, k, 0)
        scale = states / total
        norm_ref[k] = scale
        inner(offsets[cut] + k, z * scale[None], dz * scale[None], jnp.full_like(total, states), dtotal * scale)
        return carry

    lax.fori_loop(0, tips >> cut, up, 0)

    def fetch(at):
        return y_ref[at], dy_ref[at - tips]

    def climb_top(level, k):
        if level == cut:
            return fetch(offsets[cut] + k)
        kids = [climb_top(level - 1, 2 * k), climb_top(level - 1, 2 * k + 1)]
        raw_values = join(*kids)
        if level == levels:
            return raw_values
        return inner(offsets[level] + k, *raw_values)

    _, _, total, dtotal = climb_top(levels, 0)
    seed = 1.0 / total
    dseed = -(dtotal * seed) * seed

    def record(at, grad, curve):
        grad_ref[pl.ds(at, 1), :] = jnp.sum(weight * grad, axis=0, keepdims=True)
        curve_ref[pl.ds(at, 1), :] = jnp.sum(weight * curve, axis=0, keepdims=True)

    def down(at, ybar, dybar):
        half, dhalf = part_sum(ybar), part_sum(dybar)
        total, dtotal = sums_ref[at], dsums_ref[at - tips]
        record(at, total * half, dtotal * half + total * dhalf)
        full, dfull = both(half), both(dhalf)
        rate, slope = row(rate_ref, at), row(slope_ref, at)
        xbar = ybar + (rate * full)[None]
        dxbar = dybar + (rate * dfull + slope * full)[None]
        return xbar, dxbar, full * (1.0 + states * rate)

    def split(level, k, zbar, dzbar, zsum, low, emit):
        first, second = 2 * k, 2 * k + 1
        for child, other in ((first, second), (second, first)):
            if level == 1:
                yb = y_ref[other]
                half, dhalf = part_sum(zbar * yb), part_sum(dzbar * yb)
                tip, mate = order_ref[child], order_ref[other]
                total = sums_ref[child]
                push = row(slope_ref, mate) * sums_ref[other]
                record(tip, total * half, total * (dhalf + 0.5 * (push * zsum)))
                continue
            at, mate = offsets[level - 1] + child, offsets[level - 1] + other
            yb, dyb = fetch(mate)
            xbar, dxbar, xsum = down(at, zbar * yb, dzbar * yb + zbar * dyb)
            if level - 1 == low:
                emit(child, xbar, dxbar)
            else:
                split(level - 1, child, xbar, dxbar, xsum, low, emit)

    def keep(k, xbar, dxbar):
        scale = norm_ref[k][None]
        adj_ref[k] = xbar * scale
        dadj_ref[k] = dxbar * scale

    wide = (blocks, ROWS, LANES)
    split(levels, 0, jnp.broadcast_to(seed[None], wide), jnp.broadcast_to(dseed[None], wide), None, cut, keep)

    def descend(k, carry):
        split(cut, k, adj_ref[k], dadj_ref[k], None, 0, None)
        return carry

    lax.fori_loop(0, tips >> cut, descend, 0)

    scale = decay * grow / states
    grad = jnp.sum(jnp.transpose(grad_ref[...]), axis=0, keepdims=True)[:, :branches] * scale
    curve = jnp.sum(jnp.transpose(curve_ref[...]), axis=0, keepdims=True)[:, :branches] * scale
    curve = curve + decay * toward * grad
    out_ref[...] = jnp.zeros_like(out_ref)
    out_ref[0:1, :branches] = grad
    out_ref[1:2, :branches] = curve
    out_ref[2:3, :] = jnp.broadcast_to(jnp.sum(0.5 * weight), (1, LANES))


def prune(arrived, leaf_order, site_weights, branch_length, direction):
    tips, rows, _ = arrived.shape
    states = rows // 4
    blocks = rows // ROWS
    branches = branch_length.shape[0]
    tops = branches - tips
    cut = tips >> 3
    vm = pl.BlockSpec(memory_space=pltpu.VMEM)
    vec = (blocks, ROWS, LANES)
    return pl.pallas_call(
        functools.partial(prune_kernel, tips=tips, states=states),
        in_specs=[pl.BlockSpec(memory_space=pltpu.SMEM), vm, vm, vm, vm],
        out_specs=vm,
        out_shape=jax.ShapeDtypeStruct((ROWS, LANES), F32),
        scratch_shapes=[
            pltpu.VMEM((LANES, LANES), F32),
            pltpu.VMEM((LANES, LANES), F32),
            pltpu.VMEM((branches, ROWS, LANES), F32),
            pltpu.VMEM((tops, ROWS, LANES), F32),
            pltpu.VMEM((branches, *vec), F32),
            pltpu.VMEM((tops, *vec), F32),
            pltpu.VMEM((cut, *vec), F32),
            pltpu.VMEM((cut, *vec), F32),
            pltpu.VMEM((cut, ROWS, LANES), F32),
            pltpu.VMEM((LANES, LANES), F32),
            pltpu.VMEM((LANES, LANES), F32),
        ],
        compiler_params=pltpu.CompilerParams(vmem_limit_bytes=32 * 1024 * 1024),
        name="prune",
    )(leaf_order, arrived, site_weights.reshape(1, -1), branch_length.reshape(1, -1), direction.reshape(1, -1))


def exchange(blocks):
    return lax.all_to_all(blocks, "sites", 0, 0, tiled=True)


def total_over_sites(part):
    peers = lax.axis_size("sites")
    step = 1
    while step < peers:
        part = part + lax.ppermute(part, "sites", [(i, i ^ step) for i in range(peers)])
        step *= 2
    return part


def local(tip_probs, leaf_order, site_weights, branch_length, direction):
    peers = lax.axis_size("sites")
    branches = branch_length.shape[0]
    states = tip_probs.shape[1]
    arrived = exchange(deal(jnp.transpose(tip_probs, (1, 0, 2)), peers))
    arrived = arrived.reshape(leaf_order.shape[0], -1, LANES)
    sums = total_over_sites(prune(arrived, leaf_order, site_weights, branch_length, direction))
    weight_total = sums[2, 0]
    gradient = sums[0, :branches] / weight_total - states / (states - 1.0)
    return gradient, sums[1, :branches] / weight_total


def solution(mesh):
    return jax.shard_map(
        local,
        mesh=mesh,
        in_specs=(
            P(("groups", "sites"), None, None),
            P("groups"),
            P(("groups", "sites")),
            P("groups"),
            P("groups"),
        ),
        out_specs=(P("groups"), P("groups")),
        check_vma=False,
    )
```

profile of v0, /device:TPU:0, one launch (start us, length us, event | category | flops | bytes accessed | tf_op | source)
XLA Modules:
  0.0 68.5 jit_solution(2635126594690785482)
XLA Ops:
  0.6 9.5 %deal_tips.1 = bf16[16,320,128]{2,1,0:T(8,128)(2,1)} custom-call(bf16[20,4,8192]{2,1,0:T(4,128)(2,1)} %bitcast.14), custom_call_target="tpu_custom_call" | custom-call | tf_op jit(solution)/shard_map/deal_tips/pallas_call | solution.py:30
  10.2 0.0 copy-start
  10.2 0.0 copy-start.1
  10.2 0.0 copy-start.2
  10.2 0.0 copy-start.3
  10.2 39.0 %all_to_all.5 = bf16[16,320,128]{2,1,0:T(8,128)(2,1)S(1)} all-to-all(bf16[16,320,128]{2,1,0:T(8,128)(2,1)} %deal_tips.1), channel_id=1, replica_groups=mesh['groups'=2,'sites'=16] {'sites'}, dimensions={0} | all-to-all | bytes 2621440 | tf_op jit(solution)/shard_map/all_to_all | solution.py:242
  49.2 0.0 copy-done
  49.2 0.0 copy-done.1
  49.2 0.0 copy-done.2
  49.2 0.0 copy-done.3
  49.2 4.1 %prune.1 = f32[8,128]{1,0:T(8,128)S(1)} custom-call(s32[64]{0:T(128)S(1)} %copy-done.1, bf16[64,80,128]{2,1,0:T(8,128)(2,1)S(1)} %bitcast.10, s32[1,512]{1,0:T(1,128)S(1)} %bitcast.11, f32[1,126]{1,0:T(1,128)S(1)} %bitcast.12, f32[1,126]{1,0:T(1,128)S(1)} %bitcast.13), custom_call_target="tpu_custom_call" | custom-call | tf_op jit(solution)/shard_map/prune/pallas_call | solution.py:218
  53.3 0.8 %collective-permute-start = (f32[8,128]{1,0:T(8,128)S(1)}, f32[8,128]{1,0:T(8,128)S(1)}, u32[]{:S(2)}, u32[]{:S(2)}) collective-permute-start(f32[8,128]{1,0:T(8,128)S(1)} %prune.1), channel_id=1, source_target_pairs={{0,1},{1,0},{2,3},{3,2},{4,5},{5,4},{6,7},{7,6},{8,9},{9,8},{10,11... | collective-permute-start | bytes 12296 | tf_op jit(solution)/shard_map/ppermute | solution.py:249
  54.1 0.8 %collective-permute-done = f32[8,128]{1,0:T(8,128)S(1)} collective-permute-done((f32[8,128]{1,0:T(8,128)S(1)}, f32[8,128]{1,0:T(8,128)S(1)}, u32[]{:S(2)}, u32[]{:S(2)}) %collective-permute-start) | collective-permute-done | bytes 4128 | tf_op jit(solution)/shard_map/ppermute | solution.py:249
  55.0 0.8 %collective-permute-start.1 = (f32[8,128]{1,0:T(8,128)S(1)}, f32[8,128]{1,0:T(8,128)S(1)}, u32[]{:S(2)}, u32[]{:S(2)}) collective-permute-start(f32[8,128]{1,0:T(8,128)S(1)} %add.14), channel_id=1, source_target_pairs={{0,2},{1,3},{2,0},{3,1},{4,6},{5,7},{6,4},{7,5},{8,10},{9,11},{10,... | collective-permute-start | bytes 12296 | tf_op jit(solution)/shard_map/ppermute | solution.py:249
  55.8 2.8 %collective-permute-done.1 = f32[8,128]{1,0:T(8,128)S(1)} collective-permute-done((f32[8,128]{1,0:T(8,128)S(1)}, f32[8,128]{1,0:T(8,128)S(1)}, u32[]{:S(2)}, u32[]{:S(2)}) %collective-permute-start.1) | collective-permute-done | bytes 4128 | tf_op jit(solution)/shard_map/ppermute | solution.py:249
  58.6 1.0 %collective-permute-start.2 = (f32[8,128]{1,0:T(8,128)S(1)}, f32[8,128]{1,0:T(8,128)S(1)}, u32[]{:S(2)}, u32[]{:S(2)}) collective-permute-start(f32[8,128]{1,0:T(8,128)S(1)} %add.15), channel_id=1, source_target_pairs={{0,4},{1,5},{2,6},{3,7},{4,0},{5,1},{6,2},{7,3},{8,12},{9,13},{10,... | collective-permute-start | bytes 12296 | tf_op jit(solution)/shard_map/ppermute | solution.py:249
  59.5 2.6 %collective-permute-done.2 = f32[8,128]{1,0:T(8,128)S(1)} collective-permute-done((f32[8,128]{1,0:T(8,128)S(1)}, f32[8,128]{1,0:T(8,128)S(1)}, u32[]{:S(2)}, u32[]{:S(2)}) %collective-permute-start.2) | collective-permute-done | bytes 4128 | tf_op jit(solution)/shard_map/ppermute | solution.py:249
  62.2 1.6 %collective-permute-start.3 = (f32[8,128]{1,0:T(8,128)S(1)}, f32[8,128]{1,0:T(8,128)S(1)}, u32[]{:S(2)}, u32[]{:S(2)}) collective-permute-start(f32[8,128]{1,0:T(8,128)S(1)} %add.16), channel_id=1, source_target_pairs={{0,8},{1,9},{2,10},{3,11},{4,12},{5,13},{6,14},{7,15},{8,0},{9,1},... | collective-permute-start | bytes 12296 | tf_op jit(solution)/shard_map/ppermute | solution.py:249
  63.8 2.9 %collective-permute-done.3 = f32[8,128]{1,0:T(8,128)S(1)} collective-permute-done((f32[8,128]{1,0:T(8,128)S(1)}, f32[8,128]{1,0:T(8,128)S(1)}, u32[]{:S(2)}, u32[]{:S(2)}) %collective-permute-start.3) | collective-permute-done | bytes 4128 | tf_op jit(solution)/shard_map/ppermute | solution.py:249
  66.7 0.6 slice.10
  67.3 1.2 %divide_bitcast_fusion = (f32[126]{0:T(128)}, f32[126]{0:T(128)}) fusion(f32[8,128]{1,0:T(8,128)S(1)} %add.17, f32[]{:T(128)} %bitcast.5), kind=kLoop, calls=%fused_computation | loop fusion | flops 378 | bytes 2020 | tf_op jit(solution)/shard_map/div | solution.py:263
  (4 shorter events, 0.0 us)
Async XLA Ops:
  10.2 39.1 %copy-start = (s32[512]{0:T(512)S(1)}, s32[512]{0:T(512)}, u32[]{:S(2)}) copy-start(s32[512]{0:T(512)} %param.7) | copy-start | bytes 6148
  10.2 39.1 %copy-start.1 = (s32[64]{0:T(128)S(1)}, s32[64]{0:T(128)}, u32[]{:S(2)}) copy-start(s32[64]{0:T(128)} %order_ref.1) | copy-start | bytes 772
  10.2 39.1 %copy-start.2 = (f32[126]{0:T(128)S(1)}, f32[126]{0:T(128)}, u32[]{:S(2)}) copy-start(f32[126]{0:T(128)} %param.8) | copy-start | bytes 1516
  10.2 39.1 %copy-start.3 = (f32[126]{0:T(128)S(1)}, f32[126]{0:T(128)}, u32[]{:S(2)}) copy-start(f32[126]{0:T(128)} %param.9) | copy-start | bytes 1516
  53.3 1.7 %collective-permute-start = (f32[8,128]{1,0:T(8,128)S(1)}, f32[8,128]{1,0:T(8,128)S(1)}, u32[]{:S(2)}, u32[]{:S(2)}) collective-permute-start(f32[8,128]{1,0:T(8,128)S(1)} %prune.1), channel_id=1, source_target_pairs={{0,1},{1,0},{2,3},{3,2},{4,5},{5,4},{6,7},{7,6},{8,9},{9,8},{10,11... | collective-permute-start | bytes 12296 | tf_op jit(solution)/shard_map/ppermute | solution.py:249
  55.0 3.6 %collective-permute-start.1 = (f32[8,128]{1,0:T(8,128)S(1)}, f32[8,128]{1,0:T(8,128)S(1)}, u32[]{:S(2)}, u32[]{:S(2)}) collective-permute-start(f32[8,128]{1,0:T(8,128)S(1)} %add.14), channel_id=1, source_target_pairs={{0,2},{1,3},{2,0},{3,1},{4,6},{5,7},{6,4},{7,5},{8,10},{9,11},{10,... | collective-permute-start | bytes 12296 | tf_op jit(solution)/shard_map/ppermute | solution.py:249
  58.6 3.6 %collective-permute-start.2 = (f32[8,128]{1,0:T(8,128)S(1)}, f32[8,128]{1,0:T(8,128)S(1)}, u32[]{:S(2)}, u32[]{:S(2)}) collective-permute-start(f32[8,128]{1,0:T(8,128)S(1)} %add.15), channel_id=1, source_target_pairs={{0,4},{1,5},{2,6},{3,7},{4,0},{5,1},{6,2},{7,3},{8,12},{9,13},{10,... | collective-permute-start | bytes 12296 | tf_op jit(solution)/shard_map/ppermute | solution.py:249
  62.2 4.5 %collective-permute-start.3 = (f32[8,128]{1,0:T(8,128)S(1)}, f32[8,128]{1,0:T(8,128)S(1)}, u32[]{:S(2)}, u32[]{:S(2)}) collective-permute-start(f32[8,128]{1,0:T(8,128)S(1)} %add.16), channel_id=1, source_target_pairs={{0,8},{1,9},{2,10},{3,11},{4,12},{5,13},{6,14},{7,15},{8,0},{9,1},... | collective-permute-start | bytes 12296 | tf_op jit(solution)/shard_map/ppermute | solution.py:249
where the time goes:
time: 69.2 us; the launch traced here: 68.5 us
  blocking collectives  39 us (56%)
  Pallas kernels  13.6 us (20%)
  waiting for transfers between devices  9.15 us (13%)
  starting transfers between devices  4.23 us (6%)
  other arithmetic  1.21 us (2%)
    all_to_all x1, blocking collectives, exchange(): return lax.all_to_all(blocks, 'sites', 0, 0, tiled=True)  39 us
    pallas_call x1, Pallas kernels, deal(): pl.pallas_call(deal_kernel, grid=(peers,), in_specs=[pl.BlockSpec((states...  9.53 us
    ppermute x4, waiting for transfers between devices, total_over_sites(): lax.ppermute(part, 'sites', [(i, i ^ step) for i in range(peers)])  9.15 us
    ppermute x4, starting transfers between devices, total_over_sites(): lax.ppermute(part, 'sites', [(i, i ^ step) for i in range(peers)])  4.23 us
    pallas_call x1, Pallas kernels, prune(): pl.pallas_call(functools.partial(prune_kernel, tips=tips, states=states),...  4.07 us
  transfers between devices with their start and end apart: 4, of which 4 were waited for; matrix products, arithmetic and copies ran while one was open for 0% of the time, Pallas kernels for 0%

commit v1 on v0

--- a/solution.py
+++ b/solution.py
@@ -11,33 +11,6 @@
 ROWS = 8
 
 
-def deal_kernel(tips_ref, out_ref, wide_ref):
-    states, tips, span = tips_ref.shape
-    per_row = span // LANES
-    rows = states * per_row
-    for state in range(states):
-        for part in range(per_row):
-            wide_ref[pl.ds(state * per_row + part, tips, rows), :] = tips_ref[
-                state, :, part * LANES : (part + 1) * LANES
-            ].astype(F32)
-    out_ref[0] = wide_ref[...].astype(out_ref.dtype)
-
-
-def deal(tip_probs, peers):
-    states, tips, sites = tip_probs.shape
-    span = sites // peers
-    rows = states * span // LANES
-    return pl.pallas_call(
-        deal_kernel,
-        grid=(peers,),
-        in_specs=[pl.BlockSpec((states, tips, span), lambda i: (0, 0, i))],
-        out_specs=pl.BlockSpec((1, tips * rows, LANES), lambda i: (i, 0, 0)),
-        out_shape=jax.ShapeDtypeStruct((peers, tips * rows, LANES), tip_probs.dtype),
-        scratch_shapes=[pltpu.VMEM((tips * rows, LANES), F32)],
-        name="deal_tips",
-    )(tip_probs)
-
-
 def part_sum(x):
     return jnp.sum(x, axis=0)
 
@@ -47,10 +20,16 @@
 
 
 def prune_kernel(
-    order_ref, x_ref, weight_ref, length_ref, toward_ref, out_ref,
-    rate_ref, slope_ref, sums_ref, dsums_ref, y_ref, dy_ref, adj_ref, dadj_ref, norm_ref, grad_ref, curve_ref,
-    *, tips, states,
+    order_ref, me_ref, *refs, unpack, held, tips, states, each
 ):
+    (weight_ref, length_ref, toward_ref), piece_refs = refs[:3], refs[3 : 3 + held]
+    out_ref, wide_ref, *refs = refs[3 + held :]
+    (
+        rate_ref, slope_ref, sums_ref, dsums_ref, y_ref, dy_ref, adj_ref, dadj_ref, norm_ref, grad_ref, curve_ref,
+    ) = refs
+    rows = states * 4
+    me = me_ref[0]
+    unpack(piece_refs, wide_ref, me, each * rows)
     blocks = states * 4 // ROWS
     decay = states / (states - 1.0)
     branches = length_ref.shape[1]
@@ -82,7 +61,8 @@
 
     def leaf(slot):
         tip = order_ref[slot]
-        x = x_ref[tip].astype(F32).reshape(blocks, ROWS, LANES)
+        first = ((tip // each) ^ me) * (each * rows) + tip % each
+        x = wide_ref[pl.ds(first, rows, each), :].reshape(blocks, ROWS, LANES)
         total = both(part_sum(x))
         lift = row(rate_ref, tip) * total
         y = x + lift[None]
@@ -206,21 +186,24 @@
     out_ref[2:3, :] = jnp.broadcast_to(jnp.sum(0.5 * weight), (1, LANES))
 
 
-def prune(arrived, leaf_order, site_weights, branch_length, direction):
-    tips, rows, _ = arrived.shape
-    states = rows // 4
-    blocks = rows // ROWS
+def prune(pieces, me, unpack, leaf_order, site_weights, branch_length, direction, states, each):
+    tips = leaf_order.shape[0]
+    blocks = states * 4 // ROWS
     branches = branch_length.shape[0]
     tops = branches - tips
     cut = tips >> 3
     vm = pl.BlockSpec(memory_space=pltpu.VMEM)
+    sm = pl.BlockSpec(memory_space=pltpu.SMEM)
     vec = (blocks, ROWS, LANES)
     return pl.pallas_call(
-        functools.partial(prune_kernel, tips=tips, states=states),
-        in_specs=[pl.BlockSpec(memory_space=pltpu.SMEM), vm, vm, vm, vm],
+        functools.partial(
+            prune_kernel, unpack=unpack, held=len(pieces), tips=tips, states=states, each=each
+        ),
+        in_specs=[sm, sm] + [vm] * (3 + len(pieces)),
         out_specs=vm,
         out_shape=jax.ShapeDtypeStruct((ROWS, LANES), F32),
         scratch_shapes=[
+            pltpu.VMEM((tips * states * 4, LANES), F32),
             pltpu.VMEM((LANES, LANES), F32),
             pltpu.VMEM((LANES, LANES), F32),
             pltpu.VMEM((branches, ROWS, LANES), F32),
@@ -235,11 +218,71 @@
         ],
         compiler_params=pltpu.CompilerParams(vmem_limit_bytes=32 * 1024 * 1024),
         name="prune",
-    )(leaf_order, arrived, site_weights.reshape(1, -1), branch_length.reshape(1, -1), direction.reshape(1, -1))
-
-
-def exchange(blocks):
-    return lax.all_to_all(blocks, "sites", 0, 0, tiled=True)
+    )(
+        leaf_order,
+        me.reshape(1),
+        site_weights.reshape(1, -1),
+        branch_length.reshape(1, -1),
+        direction.reshape(1, -1),
+        *pieces,
+    )
+
+
+def unpack_plain(piece_refs, wide_ref, me, rows):
+    (pieces,) = piece_refs
+    for number in range(pieces.shape[0]):
+        wide_ref[number * rows : (number + 1) * rows, :] = pieces[number].astype(F32)
+
+
+def unpack_pairs(piece_refs, wide_ref, me, rows):
+    own, *got, take = piece_refs
+    deep = own.shape[1]
+    here = pl.ds(pl.multiple_of(lax.rem(me, 2) * deep, deep), deep)
+
+    def put(number, block):
+        wide_ref[number * rows : (number + 1) * rows, :] = block.astype(F32).reshape(rows, LANES)
+
+    put(0, own[...])
+    for apart, block in enumerate(got, 1):
+        put(2 * apart, block[:, here, :])
+    for apart in range(len(got) + 1):
+        put(2 * apart + 1, take[apart])
+
+
+def by_tile(tip_probs):
+    tips, states, sites = tip_probs.shape
+    tiles = sites // LANES
+    shaped = tip_probs.transpose(1, 0, 2).reshape(states, tips, tiles, LANES)
+    return shaped.transpose(0, 2, 1, 3).reshape(states, tiles * tips, LANES)
+
+
+def exchange_plain(probs):
+    peers = lax.axis_size("sites")
+    states, rows, _ = probs.shape
+    blocks = probs.reshape(states, peers, rows // peers, LANES).transpose(1, 0, 2, 3)
+    arrived = lax.all_to_all(blocks, "sites", 0, 0, tiled=True)
+    return [arrived.reshape(peers, -1, LANES)]
+
+
+def exchange_pairs(probs):
+    peers = lax.axis_size("sites")
+    me = lax.axis_index("sites")
+    chips, chip, core = peers // 2, me // 2, me % 2
+    states, rows, _ = probs.shape
+    deep = rows // peers
+
+    def cut(block, first, count):
+        return lax.dynamic_slice(block, (0, first, 0), (states, count, LANES))
+
+    far_first = list(range(chips // 2, chips)) + list(range(1, chips // 2))
+    got = {}
+    for apart in far_first:
+        swap = [(i, i ^ (2 * apart)) for i in range(peers)]
+        got[apart] = lax.ppermute(cut(probs, 2 * deep * (chip ^ apart), 2 * deep), "sites", swap)
+    give = [cut(probs, deep * (me ^ 1), deep)]
+    give += [cut(got[apart], deep * (1 - core), deep) for apart in range(1, chips)]
+    take = lax.ppermute(jnp.stack(give), "sites", [(i, i ^ 1) for i in range(peers)])
+    return [cut(probs, deep * me, deep), *(got[apart] for apart in range(1, chips)), take]
 
 
 def total_over_sites(part):
@@ -252,15 +295,18 @@
 
 
 def local(tip_probs, leaf_order, site_weights, branch_length, direction):
-    peers = lax.axis_size("sites")
     branches = branch_length.shape[0]
-    states = tip_probs.shape[1]
-    arrived = exchange(deal(jnp.transpose(tip_probs, (1, 0, 2)), peers))
-    arrived = arrived.reshape(leaf_order.shape[0], -1, LANES)
-    sums = total_over_sites(prune(arrived, leaf_order, site_weights, branch_length, direction))
-    weight_total = sums[2, 0]
-    gradient = sums[0, :branches] / weight_total - states / (states - 1.0)
-    return gradient, sums[1, :branches] / weight_total
+    each, states, _ = tip_probs.shape
+    probs = by_tile(tip_probs)
+    if 4 * each % 16 == 0:
+        me = lax.axis_index("sites").astype(jnp.int32)
+        pieces, unpack = exchange_pairs(probs), unpack_pairs
+    else:
+        me = jnp.zeros((), jnp.int32)
+        pieces, unpack = exchange_plain(probs), unpack_plain
+    part = prune(pieces, me, unpack, leaf_order, site_weights, branch_length, direction, states, each)
+    sums = total_over_sites(part)[:, :branches]
+    return sums[0] / sums[2] - states / (states - 1.0), sums[1] / sums[2]
 
 
 def solution(mesh):

time: 69.2 us -> 58.8 us (0.85)
  blocking collectives: 39 us -> 0 us
  starting transfers between devices: 4.23 us -> 24.7 us
  waiting for transfers between devices: 9.15 us -> 24.8 us
  Pallas kernels: 13.6 us -> 4.17 us
  local copies, waits for them, and re-layouts: 0.6 us -> 3.57 us
    all_to_all x1 -> x0, blocking collectives: 39 us -> none  [exchange(): return lax.all_to_all(blocks, 'sites', 0, 0, tiled=True)]
    ppermute x0 -> x8, waiting for transfers between devices: none -> 17.7 us  [the longest x7 16.6 us: exchange_pairs(): lax.ppermute(cut(probs, 2 * deep * (chip ^ apart), 2 * deep), 'sites', swap)]
    ppermute x0 -> x8, starting transfers between devices: none -> 13.7 us  [the longest x7 13.7 us: exchange_pairs(): lax.ppermute(cut(probs, 2 * deep * (chip ^ apart), 2 * deep), 'sites', swap)]
    pallas_call x2 -> x1, Pallas kernels: 13.6 us -> 4.17 us  [prune(): pl.pallas_call(functools.partial(prune_kernel, unpack=unpack, held=len(pi...]
    ppermute x4, starting transfers between devices: 4.23 us -> 11 us  [total_over_sites(): lax.ppermute(part, 'sites', [(i, i ^ step) for i in range(peers)])]
    dynamic_slice x0 -> x2, local copies, waits for them, and re-layouts: none -> 2.54 us  [cut(): return lax.dynamic_slice(block, (0, first, 0), (states, count, LANES))]
    ppermute x4, waiting for transfers between devices: 9.15 us -> 7.05 us  [total_over_sites(): lax.ppermute(part, 'sites', [(i, i ^ step) for i in range(peers)])]
    unnamed x8 -> x15, local copies, waits for them, and re-layouts: 0.01 us -> 1.01 us
  transfers between devices with their start and end apart: 4 -> 12, of which waited for: 4 -> 8; matrix products, arithmetic and copies ran while one was open for 0% -> 3% of each run, Pallas kernels for 0% -> 0%
where the time goes in v1:
time: 58.8 us; the launch traced here: 58.6 us
  waiting for transfers between devices  24.8 us (42%)
  starting transfers between devices  24.7 us (42%)
  Pallas kernels  4.17 us (7%)
  local copies, waits for them, and re-layouts  3.57 us (6%)
  between operations  0.81 us (1%)
    ppermute x7, waiting for transfers between devices, exchange_pairs(): lax.ppermute(cut(probs, 2 * deep * (chip ^ apart), 2 * deep), 'sites', swap)  16.6 us
    ppermute x7, starting transfers between devices, exchange_pairs(): lax.ppermute(cut(probs, 2 * deep * (chip ^ apart), 2 * deep), 'sites', swap)  13.7 us
    ppermute x4, starting transfers between devices, total_over_sites(): lax.ppermute(part, 'sites', [(i, i ^ step) for i in range(peers)])  11 us
    ppermute x4, waiting for transfers between devices, total_over_sites(): lax.ppermute(part, 'sites', [(i, i ^ step) for i in range(peers)])  7.05 us
    pallas_call x1, Pallas kernels, prune(): pl.pallas_call(functools.partial(prune_kernel, unpack=unpack, held=len(pi...  4.17 us
    dynamic_slice x2, local copies, waits for them, and re-layouts, cut(): return lax.dynamic_slice(block, (0, first, 0), (states, count, LANES))  2.54 us
    ppermute x1, waiting for transfers between devices, exchange_pairs(): lax.ppermute(jnp.stack(give), 'sites', [(i, i ^ 1) for i in range(peers)])  1.18 us
  transfers between devices with their start and end apart: 12, of which 8 were waited for; matrix products, arithmetic and copies ran while one was open for 3% of the time, Pallas kernels for 0%

profile of v1, /device:TPU:0, one launch (start us, length us, event | category | flops | bytes accessed | tf_op | source)
XLA Modules:
  0.0 58.6 jit_solution(3930349606380675867)
XLA Ops:
  0.7 1.6 %constant_dynamic-slice_fusion = (bf16[20,32,128]{2,1,0:T(8,128)(2,1)S(1)}, bf16[20,32,128]{2,1,0:T(8,128)(2,1)S(1)}, bf16[20,32,128]{2,1,0:T(8,128)(2,1)S(1)}, ...) fusion(bf16[20,256,128]{2,1,0:T(8,128)(2,1)} %bitcast.34, ...), kind=kLoop, calls=%fused_computation.8 | loop fusion | bytes 2293788 | tf_op jit(solution)/shard_map/dynamic_slice | solution.py:275
  2.3 0.0 copy-start
  2.3 0.0 copy-start.1
  2.3 0.0 copy-start.2
  2.4 0.0 copy-start.3
  2.4 3.0 %collective-permute-start = (bf16[20,32,128]{2,1,0:T(8,128)(2,1)S(1)}, bf16[20,32,128]{2,1,0:T(8,128)(2,1)S(1)}, u32[]{:S(2)}, u32[]{:S(2)}) collective-permute-start(bf16[20,32,128]{2,1,0:T(8,128)(2,1)S(1)} %get-tuple-element.8), channel_id=1, source_target_pairs={{0,2},{1,3},{2,0},{3,1},{4,6},{5,7},{6,4},{7,5},{8,10},{9,11},{10,... | collective-permute-start | bytes 491528 | tf_op jit(solution)/shard_map/ppermute | solution.py:281
  5.4 1.6 %collective-permute-start.1 = (bf16[20,32,128]{2,1,0:T(8,128)(2,1)S(1)}, bf16[20,32,128]{2,1,0:T(8,128)(2,1)S(1)}, u32[]{:S(2)}, u32[]{:S(2)}) collective-permute-start(bf16[20,32,128]{2,1,0:T(8,128)(2,1)S(1)} %get-tuple-element.7), channel_id=1, source_target_pairs={{0,4},{1,5},{2,6},{3,7},{4,0},{5,1},{6,2},{7,3},{8,12},{9,13},{10,... | collective-permute-start | bytes 491528 | tf_op jit(solution)/shard_map/ppermute | solution.py:281
  7.0 0.0 collective-permute-start.2
  7.0 3.0 %collective-permute-start.3 = (bf16[20,32,128]{2,1,0:T(8,128)(2,1)S(1)}, bf16[20,32,128]{2,1,0:T(8,128)(2,1)S(1)}, u32[]{:S(2)}, u32[]{:S(2)}) collective-permute-start(bf16[20,32,128]{2,1,0:T(8,128)(2,1)S(1)} %get-tuple-element.5), channel_id=1, source_target_pairs={{0,8},{1,9},{2,10},{3,11},{4,12},{5,13},{6,14},{7,15},{8,0},{9,1},... | collective-permute-start | bytes 491528 | tf_op jit(solution)/shard_map/ppermute | solution.py:281
  10.0 1.3 %collective-permute-start.4 = (bf16[20,32,128]{2,1,0:T(8,128)(2,1)S(1)}, bf16[20,32,128]{2,1,0:T(8,128)(2,1)S(1)}, u32[]{:S(2)}, u32[]{:S(2)}) collective-permute-start(bf16[20,32,128]{2,1,0:T(8,128)(2,1)S(1)} %get-tuple-element.4), channel_id=1, source_target_pairs={{0,10},{1,11},{2,8},{3,9},{4,14},{5,15},{6,12},{7,13},{8,2},{9,3},... | collective-permute-start | bytes 491528 | tf_op jit(solution)/shard_map/ppermute | solution.py:281
  11.3 0.9 %bitcast_dynamic-update-slice_fusion.7 = bf16[8,20,16,128]{3,2,1,0:T(8,128)(2,1)S(1)} fusion(bf16[20,256,128]{2,1,0:T(8,128)(2,1)} %bitcast.35, s32[]{:T(128)S(6)} %select_n.56), kind=kLoop, calls=%fused_computation.7 | loop fusion | bytes 163844
  12.1 0.0 collective-permute-done.refs_4_
  12.2 3.7 %collective-permute-start.5 = (bf16[20,32,128]{2,1,0:T(8,128)(2,1)S(1)}, bf16[20,32,128]{2,1,0:T(8,128)(2,1)S(1)}, u32[]{:S(2)}, u32[]{:S(2)}) collective-permute-start(bf16[20,32,128]{2,1,0:T(8,128)(2,1)S(1)} %get-tuple-element.3), channel_id=1, source_target_pairs={{0,12},{1,13},{2,14},{3,15},{4,8},{5,9},{6,10},{7,11},{8,4},{9,5},... | collective-permute-start | bytes 491528 | tf_op jit(solution)/shard_map/ppermute | solution.py:281
  15.8 2.6 %collective-permute-done.1.refs_5_ = bf16[20,32,128]{2,1,0:T(8,128)(2,1)S(1)} collective-permute-done((bf16[20,32,128]{2,1,0:T(8,128)(2,1)S(1)}, bf16[20,32,128]{2,1,0:T(8,128)(2,1)S(1)}, u32[]{:S(2)}, u32[]{:S(2)}) %collective-permute-start.1) | collective-permute-done | bytes 163872 | tf_op jit(solution)/shard_map/ppermute | solution.py:281
  18.5 1.1 %collective-permute-start.6 = (bf16[20,32,128]{2,1,0:T(8,128)(2,1)S(1)}, bf16[20,32,128]{2,1,0:T(8,128)(2,1)S(1)}, u32[]{:S(2)}, u32[]{:S(2)}) collective-permute-start(bf16[20,32,128]{2,1,0:T(8,128)(2,1)S(1)} %get-tuple-element.2), channel_id=1, source_target_pairs={{0,14},{1,15},{2,12},{3,13},{4,10},{5,11},{6,8},{7,9},{8,6},{9,7},... | collective-permute-start | bytes 491528 | tf_op jit(solution)/shard_map/ppermute | solution.py:281
  19.6 0.3 collective-permute-done.2.refs_6_
  20.0 0.0 collective-permute-done.3.refs_7_
  20.0 13.6 %collective-permute-done.4.refs_8_ = bf16[20,32,128]{2,1,0:T(8,128)(2,1)S(1)} collective-permute-done((bf16[20,32,128]{2,1,0:T(8,128)(2,1)S(1)}, bf16[20,32,128]{2,1,0:T(8,128)(2,1)S(1)}, u32[]{:S(2)}, u32[]{:S(2)}) %collective-permute-start.4) | collective-permute-done | bytes 163872 | tf_op jit(solution)/shard_map/ppermute | solution.py:281
  33.6 0.0 collective-permute-done.5.refs_9_
  33.6 0.0 collective-permute-done.6.refs_10_
  33.7 0.1 collective-permute-start.7
  33.8 0.9 %constant_dynamic-slice_fusion.7.refs_3_ = bf16[20,16,128]{2,1,0:T(8,128)(2,1)S(1)} fusion(bf16[20,256,128]{2,1,0:T(8,128)(2,1)} %bitcast.36, s32[]{:T(128)S(6)} %select_n.47), kind=kLoop, calls=%fused_computation.15 | loop fusion | bytes 163844 | tf_op jit(solution)/shard_map/dynamic_slice | solution.py:275
  34.7 1.2 %collective-permute-done.7.refs_11_ = bf16[8,20,16,128]{3,2,1,0:T(8,128)(2,1)S(1)} collective-permute-done((bf16[8,20,16,128]{3,2,1,0:T(8,128)(2,1)S(1)}, bf16[8,20,16,128]{3,2,1,0:T(8,128)(2,1)S(1)}, u32[]{:S(2)}, u32[]{:S(2)}) %collective-permute-start.7) | collective-permute-done | bytes 655392 | tf_op jit(solution)/shard_map/ppermute | solution.py:284
  35.8 0.0 copy-done
  35.8 0.0 copy-done.1
  35.8 0.0 copy-done.2
  35.8 0.0 copy-done.3
  35.9 4.2 %prune.1 = f32[8,128]{1,0:T(8,128)S(1)} custom-call(s32[64]{0:T(128)S(1)} %copy-done.1, s32[1]{0:T(128)} %bitcast.me_ref, s32[1,512]{1,0:T(1,128)S(1)} %bitcast.31, f32[1,126]{1,0:T(1,128)S(1)} %bitcast.32, f32[1,126]{1,0:T(1,128)S(1)} %bitcast.33, bf16[20,16,128]{2,1,0:T(8,128)(2,1)S(1)} %constant_dynamic-slice_fusion.7.refs_3_, ...), custom_call_target="tpu_custom_call" | custom-call | tf_op jit(solution)/shard_map/prune/pallas_call | solution.py:198
  40.0 0.2 collective-permute-start.8
  40.2 1.0 %collective-permute-done.8 = f32[8,128]{1,0:T(8,128)S(1)} collective-permute-done((f32[8,128]{1,0:T(8,128)S(1)}, f32[8,128]{1,0:T(8,128)S(1)}, u32[]{:S(2)}, u32[]{:S(2)}) %collective-permute-start.8) | collective-permute-done | bytes 4128 | tf_op jit(solution)/shard_map/ppermute | solution.py:292
  41.3 0.8 %collective-permute-start.9 = (f32[8,128]{1,0:T(8,128)S(1)}, f32[8,128]{1,0:T(8,128)S(1)}, u32[]{:S(2)}, u32[]{:S(2)}) collective-permute-start(f32[8,128]{1,0:T(8,128)S(1)} %add.66), channel_id=1, source_target_pairs={{0,2},{1,3},{2,0},{3,1},{4,6},{5,7},{6,4},{7,5},{8,10},{9,11},{10,... | collective-permute-start | bytes 12296 | tf_op jit(solution)/shard_map/ppermute | solution.py:292
  42.0 2.8 %collective-permute-done.9 = f32[8,128]{1,0:T(8,128)S(1)} collective-permute-done((f32[8,128]{1,0:T(8,128)S(1)}, f32[8,128]{1,0:T(8,128)S(1)}, u32[]{:S(2)}, u32[]{:S(2)}) %collective-permute-start.9) | collective-permute-done | bytes 4128 | tf_op jit(solution)/shard_map/ppermute | solution.py:292
  44.9 6.0 %collective-permute-start.10 = (f32[8,128]{1,0:T(8,128)S(1)}, f32[8,128]{1,0:T(8,128)S(1)}, u32[]{:S(2)}, u32[]{:S(2)}) collective-permute-start(f32[8,128]{1,0:T(8,128)S(1)} %add.67), channel_id=1, source_target_pairs={{0,4},{1,5},{2,6},{3,7},{4,0},{5,1},{6,2},{7,3},{8,12},{9,13},{10,... | collective-permute-start | bytes 12296 | tf_op jit(solution)/shard_map/ppermute | solution.py:292
  50.9 1.6 %collective-permute-done.10 = f32[8,128]{1,0:T(8,128)S(1)} collective-permute-done((f32[8,128]{1,0:T(8,128)S(1)}, f32[8,128]{1,0:T(8,128)S(1)}, u32[]{:S(2)}, u32[]{:S(2)}) %collective-permute-start.10) | collective-permute-done | bytes 4128 | tf_op jit(solution)/shard_map/ppermute | solution.py:292
  52.5 4.0 %collective-permute-start.11 = (f32[8,128]{1,0:T(8,128)S(1)}, f32[8,128]{1,0:T(8,128)S(1)}, u32[]{:S(2)}, u32[]{:S(2)}) collective-permute-start(f32[8,128]{1,0:T(8,128)S(1)} %add.68), channel_id=1, source_target_pairs={{0,8},{1,9},{2,10},{3,11},{4,12},{5,13},{6,14},{7,15},{8,0},{9,1},... | collective-permute-start | bytes 12296 | tf_op jit(solution)/shard_map/ppermute | solution.py:292
  56.5 1.6 %collective-permute-done.11 = f32[8,128]{1,0:T(8,128)S(1)} collective-permute-done((f32[8,128]{1,0:T(8,128)S(1)}, f32[8,128]{1,0:T(8,128)S(1)}, u32[]{:S(2)}, u32[]{:S(2)}) %collective-permute-start.11) | collective-permute-done | bytes 4128 | tf_op jit(solution)/shard_map/ppermute | solution.py:292
  58.1 0.5 fusion
  (11 shorter events, 0.1 us)
Async XLA Ops:
  2.3 33.5 %copy-start = (s32[512]{0:T(512)S(1)}, s32[512]{0:T(512)}, u32[]{:S(2)}) copy-start(s32[512]{0:T(512)} %param.7) | copy-start | bytes 6148
  2.3 33.5 %copy-start.1 = (s32[64]{0:T(128)S(1)}, s32[64]{0:T(128)}, u32[]{:S(2)}) copy-start(s32[64]{0:T(128)} %order_ref.1) | copy-start | bytes 772
  2.3 33.5 %copy-start.2 = (f32[126]{0:T(128)S(1)}, f32[126]{0:T(128)}, u32[]{:S(2)}) copy-start(f32[126]{0:T(128)} %param.8) | copy-start | bytes 1516
  2.4 33.5 %copy-start.3 = (f32[126]{0:T(128)S(1)}, f32[126]{0:T(128)}, u32[]{:S(2)}) copy-start(f32[126]{0:T(128)} %param.9) | copy-start | bytes 1516
  2.4 9.8 %collective-permute-start = (bf16[20,32,128]{2,1,0:T(8,128)(2,1)S(1)}, bf16[20,32,128]{2,1,0:T(8,128)(2,1)S(1)}, u32[]{:S(2)}, u32[]{:S(2)}) collective-permute-start(bf16[20,32,128]{2,1,0:T(8,128)(2,1)S(1)} %get-tuple-element.8), channel_id=1, source_target_pairs={{0,2},{1,3},{2,0},{3,1},{4,6},{5,7},{6,4},{7,5},{8,10},{9,11},{10,... | collective-permute-start | bytes 491528 | tf_op jit(solution)/shard_map/ppermute | solution.py:281
  5.4 13.1 %collective-permute-start.1 = (bf16[20,32,128]{2,1,0:T(8,128)(2,1)S(1)}, bf16[20,32,128]{2,1,0:T(8,128)(2,1)S(1)}, u32[]{:S(2)}, u32[]{:S(2)}) collective-permute-start(bf16[20,32,128]{2,1,0:T(8,128)(2,1)S(1)} %get-tuple-element.7), channel_id=1, source_target_pairs={{0,4},{1,5},{2,6},{3,7},{4,0},{5,1},{6,2},{7,3},{8,12},{9,13},{10,... | collective-permute-start | bytes 491528 | tf_op jit(solution)/shard_map/ppermute | solution.py:281
  7.0 13.0 %collective-permute-start.2 = (bf16[20,32,128]{2,1,0:T(8,128)(2,1)S(1)}, bf16[20,32,128]{2,1,0:T(8,128)(2,1)S(1)}, u32[]{:S(2)}, u32[]{:S(2)}) collective-permute-start(bf16[20,32,128]{2,1,0:T(8,128)(2,1)S(1)} %get-tuple-element.6), channel_id=1, source_target_pairs={{0,6},{1,7},{2,4},{3,5},{4,2},{5,3},{6,0},{7,1},{8,14},{9,15},{10,... | collective-permute-start | bytes 491528 | tf_op jit(solution)/shard_map/ppermute | solution.py:281
  7.0 13.0 %collective-permute-start.3 = (bf16[20,32,128]{2,1,0:T(8,128)(2,1)S(1)}, bf16[20,32,128]{2,1,0:T(8,128)(2,1)S(1)}, u32[]{:S(2)}, u32[]{:S(2)}) collective-permute-start(bf16[20,32,128]{2,1,0:T(8,128)(2,1)S(1)} %get-tuple-element.5), channel_id=1, source_target_pairs={{0,8},{1,9},{2,10},{3,11},{4,12},{5,13},{6,14},{7,15},{8,0},{9,1},... | collective-permute-start | bytes 491528 | tf_op jit(solution)/shard_map/ppermute | solution.py:281
  10.0 23.6 %collective-permute-start.4 = (bf16[20,32,128]{2,1,0:T(8,128)(2,1)S(1)}, bf16[20,32,128]{2,1,0:T(8,128)(2,1)S(1)}, u32[]{:S(2)}, u32[]{:S(2)}) collective-permute-start(bf16[20,32,128]{2,1,0:T(8,128)(2,1)S(1)} %get-tuple-element.4), channel_id=1, source_target_pairs={{0,10},{1,11},{2,8},{3,9},{4,14},{5,15},{6,12},{7,13},{8,2},{9,3},... | collective-permute-start | bytes 491528 | tf_op jit(solution)/shard_map/ppermute | solution.py:281
  12.2 21.4 %collective-permute-start.5 = (bf16[20,32,128]{2,1,0:T(8,128)(2,1)S(1)}, bf16[20,32,128]{2,1,0:T(8,128)(2,1)S(1)}, u32[]{:S(2)}, u32[]{:S(2)}) collective-permute-start(bf16[20,32,128]{2,1,0:T(8,128)(2,1)S(1)} %get-tuple-element.3), channel_id=1, source_target_pairs={{0,12},{1,13},{2,14},{3,15},{4,8},{5,9},{6,10},{7,11},{8,4},{9,5},... | collective-permute-start | bytes 491528 | tf_op jit(solution)/shard_map/ppermute | solution.py:281
  18.5 15.2 %collective-permute-start.6 = (bf16[20,32,128]{2,1,0:T(8,128)(2,1)S(1)}, bf16[20,32,128]{2,1,0:T(8,128)(2,1)S(1)}, u32[]{:S(2)}, u32[]{:S(2)}) collective-permute-start(bf16[20,32,128]{2,1,0:T(8,128)(2,1)S(1)} %get-tuple-element.2), channel_id=1, source_target_pairs={{0,14},{1,15},{2,12},{3,13},{4,10},{5,11},{6,8},{7,9},{8,6},{9,7},... | collective-permute-start | bytes 491528 | tf_op jit(solution)/shard_map/ppermute | solution.py:281
  33.7 2.2 %collective-permute-start.7 = (bf16[8,20,16,128]{3,2,1,0:T(8,128)(2,1)S(1)}, bf16[8,20,16,128]{3,2,1,0:T(8,128)(2,1)S(1)}, u32[]{:S(2)}, u32[]{:S(2)}) collective-permute-start(bf16[8,20,16,128]{3,2,1,0:T(8,128)(2,1)S(1)} %bitcast_dynamic-update-slice_fusion), channel_id=1, source_target_pairs={{0,1},{1,0},{2,3},{3,2},{4,5},{5,4},{6,7},{7,6},{8,9},{9,8},{10,11... | collective-permute-start | bytes 1966088 | tf_op jit(solution)/shard_map/ppermute | solution.py:284
  40.0 1.2 %collective-permute-start.8 = (f32[8,128]{1,0:T(8,128)S(1)}, f32[8,128]{1,0:T(8,128)S(1)}, u32[]{:S(2)}, u32[]{:S(2)}) collective-permute-start(f32[8,128]{1,0:T(8,128)S(1)} %prune.1), channel_id=1, source_target_pairs={{0,1},{1,0},{2,3},{3,2},{4,5},{5,4},{6,7},{7,6},{8,9},{9,8},{10,11... | collective-permute-start | bytes 12296 | tf_op jit(solution)/shard_map/ppermute | solution.py:292
  41.3 3.6 %collective-permute-start.9 = (f32[8,128]{1,0:T(8,128)S(1)}, f32[8,128]{1,0:T(8,128)S(1)}, u32[]{:S(2)}, u32[]{:S(2)}) collective-permute-start(f32[8,128]{1,0:T(8,128)S(1)} %add.66), channel_id=1, source_target_pairs={{0,2},{1,3},{2,0},{3,1},{4,6},{5,7},{6,4},{7,5},{8,10},{9,11},{10,... | collective-permute-start | bytes 12296 | tf_op jit(solution)/shard_map/ppermute | solution.py:292
  44.9 7.6 %collective-permute-start.10 = (f32[8,128]{1,0:T(8,128)S(1)}, f32[8,128]{1,0:T(8,128)S(1)}, u32[]{:S(2)}, u32[]{:S(2)}) collective-permute-start(f32[8,128]{1,0:T(8,128)S(1)} %add.67), channel_id=1, source_target_pairs={{0,4},{1,5},{2,6},{3,7},{4,0},{5,1},{6,2},{7,3},{8,12},{9,13},{10,... | collective-permute-start | bytes 12296 | tf_op jit(solution)/shard_map/ppermute | solution.py:292
  52.5 5.6 %collective-permute-start.11 = (f32[8,128]{1,0:T(8,128)S(1)}, f32[8,128]{1,0:T(8,128)S(1)}, u32[]{:S(2)}, u32[]{:S(2)}) collective-permute-start(f32[8,128]{1,0:T(8,128)S(1)} %add.68), channel_id=1, source_target_pairs={{0,8},{1,9},{2,10},{3,11},{4,12},{5,13},{6,14},{7,15},{8,0},{9,1},... | collective-permute-start | bytes 12296 | tf_op jit(solution)/shard_map/ppermute | solution.py:292

commit v2 on v1

--- a/solution.py
+++ b/solution.py
@@ -234,7 +234,7 @@
         wide_ref[number * rows : (number + 1) * rows, :] = pieces[number].astype(F32)
 
 
-def unpack_pairs(piece_refs, wide_ref, me, rows):
+def unpack_pairs(piece_refs, wide_ref, me, rows, order):
     own, *got, take = piece_refs
     deep = own.shape[1]
     here = pl.ds(pl.multiple_of(lax.rem(me, 2) * deep, deep), deep)
@@ -243,10 +243,10 @@
         wide_ref[number * rows : (number + 1) * rows, :] = block.astype(F32).reshape(rows, LANES)
 
     put(0, own[...])
-    for apart, block in enumerate(got, 1):
+    put(1, take[0])
+    for number, (apart, block) in enumerate(zip(order, got), 1):
         put(2 * apart, block[:, here, :])
-    for apart in range(len(got) + 1):
-        put(2 * apart + 1, take[apart])
+        put(2 * apart + 1, take[number])
 
 
 def by_tile(tip_probs):
@@ -261,36 +261,44 @@
     states, rows, _ = probs.shape
     blocks = probs.reshape(states, peers, rows // peers, LANES).transpose(1, 0, 2, 3)
     arrived = lax.all_to_all(blocks, "sites", 0, 0, tiled=True)
-    return [arrived.reshape(peers, -1, LANES)]
+    return [arrived.reshape(peers, -1, LANES)], unpack_plain
 
 
 def exchange_pairs(probs):
     peers = lax.axis_size("sites")
-    me = lax.axis_index("sites")
-    chips, chip, core = peers // 2, me // 2, me % 2
+    chips, me = peers // 2, lax.axis_index("sites")
+    chip, core = me // 2, me % 2
     states, rows, _ = probs.shape
     deep = rows // peers
 
     def cut(block, first, count):
         return lax.dynamic_slice(block, (0, first, 0), (states, count, LANES))
 
-    far_first = list(range(chips // 2, chips)) + list(range(1, chips // 2))
-    got = {}
-    for apart in far_first:
+    far, near = range(chips // 2, chips), [*range(2, chips // 2), 1]
+    order = [far[0], *(apart for pair in zip(near, far[1:]) for apart in pair)]
+    got = []
+    for apart in order:
         swap = [(i, i ^ (2 * apart)) for i in range(peers)]
-        got[apart] = lax.ppermute(cut(probs, 2 * deep * (chip ^ apart), 2 * deep), "sites", swap)
-    give = [cut(probs, deep * (me ^ 1), deep)]
-    give += [cut(got[apart], deep * (1 - core), deep) for apart in range(1, chips)]
+        got.append(lax.ppermute(cut(probs, 2 * deep * (chip ^ apart), 2 * deep), "sites", swap))
+    give = [cut(probs, deep * (me ^ 1), deep)] + [cut(block, deep * (1 - core), deep) for block in got]
     take = lax.ppermute(jnp.stack(give), "sites", [(i, i ^ 1) for i in range(peers)])
-    return [cut(probs, deep * me, deep), *(got[apart] for apart in range(1, chips)), take]
+    return [cut(probs, deep * me, deep), *got, take], functools.partial(unpack_pairs, order=order)
 
 
 def total_over_sites(part):
     peers = lax.axis_size("sites")
-    step = 1
-    while step < peers:
-        part = part + lax.ppermute(part, "sites", [(i, i ^ step) for i in range(peers)])
-        step *= 2
+    rounds, bit = [[1], [3]], 4
+    while bit < peers:
+        if 2 * bit < peers:
+            rounds.append([bit + 1, 2 * bit + 1, 3 * bit + 1])
+        else:
+            rounds.append([bit + 1])
+        bit *= 4
+    for apart in rounds:
+        got = [lax.ppermute(part, "sites", [(i, i ^ step) for i in range(peers)]) for step in apart]
+        part = part + got[0]
+        if len(got) > 1:
+            part = part + (got[1] + got[2])
     return part
 
 
@@ -300,10 +308,10 @@
     probs = by_tile(tip_probs)
     if 4 * each % 16 == 0:
         me = lax.axis_index("sites").astype(jnp.int32)
-        pieces, unpack = exchange_pairs(probs), unpack_pairs
+        pieces, unpack = exchange_pairs(probs)
     else:
         me = jnp.zeros((), jnp.int32)
-        pieces, unpack = exchange_plain(probs), unpack_plain
+        pieces, unpack = exchange_plain(probs)
     part = prune(pieces, me, unpack, leaf_order, site_weights, branch_length, direction, states, each)
     sums = total_over_sites(part)[:, :branches]
     return sums[0] / sums[2] - states / (states - 1.0), sums[1] / sums[2]

time: 58.8 us -> 54.9 us (0.934)
  waiting for transfers between devices: 24.8 us -> 20.4 us
    ppermute x7, waiting for transfers between devices: 16.6 us -> 12.1 us  [exchange_pairs(): lax.ppermute(cut(probs, 2 * deep * (chip ^ apart), 2 * deep), 'sites', swap)]
    ppermute x7, starting transfers between devices: 13.7 us -> 15.6 us  [exchange_pairs(): lax.ppermute(cut(probs, 2 * deep * (chip ^ apart), 2 * deep), 'sites', swap)]
    ppermute x4 -> x5, starting transfers between devices: 11 us -> 9.48 us  [total_over_sites(): lax.ppermute(part, 'sites', [(i, i ^ step) for i in range(peers)])]
    ppermute x4 -> x5, waiting for transfers between devices: 7.05 us -> 7.15 us  [total_over_sites(): lax.ppermute(part, 'sites', [(i, i ^ step) for i in range(peers)])]
  transfers between devices with their start and end apart: 12 -> 13, of which waited for: 8 -> 9; matrix products, arithmetic and copies ran while one was open for 3% -> 3% of each run, Pallas kernels for 0% -> 0%
where the time goes in v2:
time: 54.9 us; the launch traced here: 54.7 us
  starting transfers between devices  25.1 us (46%)
  waiting for transfers between devices  20.4 us (37%)
  Pallas kernels  4.17 us (8%)
  local copies, waits for them, and re-layouts  3.56 us (6%)
  between operations  0.81 us (1%)
    ppermute x7, starting transfers between devices, exchange_pairs(): lax.ppermute(cut(probs, 2 * deep * (chip ^ apart), 2 * deep), 'sites', swap)  15.6 us
    ppermute x7, waiting for transfers between devices, exchange_pairs(): lax.ppermute(cut(probs, 2 * deep * (chip ^ apart), 2 * deep), 'sites', swap)  12.1 us
    ppermute x5, starting transfers between devices, total_over_sites(): lax.ppermute(part, 'sites', [(i, i ^ step) for i in range(peers)])  9.48 us
    ppermute x5, waiting for transfers between devices, total_over_sites(): lax.ppermute(part, 'sites', [(i, i ^ step) for i in range(peers)])  7.15 us
    pallas_call x1, Pallas kernels, prune(): pl.pallas_call(functools.partial(prune_kernel, unpack=unpack, held=len(pi...  4.17 us
    dynamic_slice x2, local copies, waits for them, and re-layouts, cut(): return lax.dynamic_slice(block, (0, first, 0), (states, count, LANES))  2.54 us
    ppermute x1, waiting for transfers between devices, exchange_pairs(): lax.ppermute(jnp.stack(give), 'sites', [(i, i ^ 1) for i in range(peers)])  1.18 us
  transfers between devices with their start and end apart: 13, of which 9 were waited for; matrix products, arithmetic and copies ran while one was open for 3% of the time, Pallas kernels for 0%

profile of v2, /device:TPU:0, one launch (start us, length us, event | category | flops | bytes accessed | tf_op | source)
XLA Modules:
  0.0 54.7 jit_solution(16801356591340900472)
XLA Ops:
  0.7 1.6 %constant_dynamic-slice_fusion = (bf16[20,32,128]{2,1,0:T(8,128)(2,1)S(1)}, bf16[20,32,128]{2,1,0:T(8,128)(2,1)S(1)}, bf16[20,32,128]{2,1,0:T(8,128)(2,1)S(1)}, ...) fusion(bf16[20,256,128]{2,1,0:T(8,128)(2,1)} %bitcast.34, ...), kind=kLoop, calls=%fused_computation.9 | loop fusion | bytes 2293788 | tf_op jit(solution)/shard_map/dynamic_slice | solution.py:275
  2.3 0.0 copy-start
  2.3 0.0 copy-start.1
  2.3 0.0 copy-start.2
  2.4 0.0 copy-start.3
  2.4 4.1 %collective-permute-start = (bf16[20,32,128]{2,1,0:T(8,128)(2,1)S(1)}, bf16[20,32,128]{2,1,0:T(8,128)(2,1)S(1)}, u32[]{:S(2)}, u32[]{:S(2)}) collective-permute-start(bf16[20,32,128]{2,1,0:T(8,128)(2,1)S(1)} %get-tuple-element.8), channel_id=1, source_target_pairs={{0,8},{1,9},{2,10},{3,11},{4,12},{5,13},{6,14},{7,15},{8,0},{9,1},... | collective-permute-start | bytes 491528 | tf_op jit(solution)/shard_map/ppermute | solution.py:282
  6.5 1.6 %collective-permute-start.1 = (bf16[20,32,128]{2,1,0:T(8,128)(2,1)S(1)}, bf16[20,32,128]{2,1,0:T(8,128)(2,1)S(1)}, u32[]{:S(2)}, u32[]{:S(2)}) collective-permute-start(bf16[20,32,128]{2,1,0:T(8,128)(2,1)S(1)} %get-tuple-element.7), channel_id=1, source_target_pairs={{0,4},{1,5},{2,6},{3,7},{4,0},{5,1},{6,2},{7,3},{8,12},{9,13},{10,... | collective-permute-start | bytes 491528 | tf_op jit(solution)/shard_map/ppermute | solution.py:282
  8.0 1.3 %collective-permute-start.2 = (bf16[20,32,128]{2,1,0:T(8,128)(2,1)S(1)}, bf16[20,32,128]{2,1,0:T(8,128)(2,1)S(1)}, u32[]{:S(2)}, u32[]{:S(2)}) collective-permute-start(bf16[20,32,128]{2,1,0:T(8,128)(2,1)S(1)} %get-tuple-element.6), channel_id=1, source_target_pairs={{0,10},{1,11},{2,8},{3,9},{4,14},{5,15},{6,12},{7,13},{8,2},{9,3},... | collective-permute-start | bytes 491528 | tf_op jit(solution)/shard_map/ppermute | solution.py:282
  9.3 0.1 collective-permute-start.3
  9.5 3.9 %collective-permute-start.4 = (bf16[20,32,128]{2,1,0:T(8,128)(2,1)S(1)}, bf16[20,32,128]{2,1,0:T(8,128)(2,1)S(1)}, u32[]{:S(2)}, u32[]{:S(2)}) collective-permute-start(bf16[20,32,128]{2,1,0:T(8,128)(2,1)S(1)} %get-tuple-element.4), channel_id=1, source_target_pairs={{0,12},{1,13},{2,14},{3,15},{4,8},{5,9},{6,10},{7,11},{8,4},{9,5},... | collective-permute-start | bytes 491528 | tf_op jit(solution)/shard_map/ppermute | solution.py:282
  13.3 0.9 %bitcast_dynamic-update-slice_fusion.7 = bf16[8,20,16,128]{3,2,1,0:T(8,128)(2,1)S(1)} fusion(bf16[20,256,128]{2,1,0:T(8,128)(2,1)} %bitcast.35, s32[]{:T(128)S(6)} %select_n.56), kind=kLoop, calls=%fused_computation.7 | loop fusion | bytes 163844
  14.2 1.7 %collective-permute-done.refs_4_ = bf16[20,32,128]{2,1,0:T(8,128)(2,1)S(1)} collective-permute-done((bf16[20,32,128]{2,1,0:T(8,128)(2,1)S(1)}, bf16[20,32,128]{2,1,0:T(8,128)(2,1)S(1)}, u32[]{:S(2)}, u32[]{:S(2)}) %collective-permute-start) | collective-permute-done | bytes 163872 | tf_op jit(solution)/shard_map/ppermute | solution.py:282
  15.9 3.5 %collective-permute-start.5 = (bf16[20,32,128]{2,1,0:T(8,128)(2,1)S(1)}, bf16[20,32,128]{2,1,0:T(8,128)(2,1)S(1)}, u32[]{:S(2)}, u32[]{:S(2)}) collective-permute-start(bf16[20,32,128]{2,1,0:T(8,128)(2,1)S(1)} %get-tuple-element.3), channel_id=1, source_target_pairs={{0,2},{1,3},{2,0},{3,1},{4,6},{5,7},{6,4},{7,5},{8,10},{9,11},{10,... | collective-permute-start | bytes 491528 | tf_op jit(solution)/shard_map/ppermute | solution.py:282
  19.4 0.0 collective-permute-done.1.refs_5_
  19.4 1.2 %collective-permute-start.6 = (bf16[20,32,128]{2,1,0:T(8,128)(2,1)S(1)}, bf16[20,32,128]{2,1,0:T(8,128)(2,1)S(1)}, u32[]{:S(2)}, u32[]{:S(2)}) collective-permute-start(bf16[20,32,128]{2,1,0:T(8,128)(2,1)S(1)} %get-tuple-element.2), channel_id=1, source_target_pairs={{0,14},{1,15},{2,12},{3,13},{4,10},{5,11},{6,8},{7,9},{8,6},{9,7},... | collective-permute-start | bytes 491528 | tf_op jit(solution)/shard_map/ppermute | solution.py:282
  20.6 3.3 %collective-permute-done.2.refs_6_ = bf16[20,32,128]{2,1,0:T(8,128)(2,1)S(1)} collective-permute-done((bf16[20,32,128]{2,1,0:T(8,128)(2,1)S(1)}, bf16[20,32,128]{2,1,0:T(8,128)(2,1)S(1)}, u32[]{:S(2)}, u32[]{:S(2)}) %collective-permute-start.2) | collective-permute-done | bytes 163872 | tf_op jit(solution)/shard_map/ppermute | solution.py:282
  23.9 0.0 collective-permute-done.3.refs_7_
  23.9 3.9 %collective-permute-done.4.refs_8_ = bf16[20,32,128]{2,1,0:T(8,128)(2,1)S(1)} collective-permute-done((bf16[20,32,128]{2,1,0:T(8,128)(2,1)S(1)}, bf16[20,32,128]{2,1,0:T(8,128)(2,1)S(1)}, u32[]{:S(2)}, u32[]{:S(2)}) %collective-permute-start.4) | collective-permute-done | bytes 163872 | tf_op jit(solution)/shard_map/ppermute | solution.py:282
  27.8 0.0 collective-permute-done.5.refs_9_
  27.9 3.3 %collective-permute-done.6.refs_10_ = bf16[20,32,128]{2,1,0:T(8,128)(2,1)S(1)} collective-permute-done((bf16[20,32,128]{2,1,0:T(8,128)(2,1)S(1)}, bf16[20,32,128]{2,1,0:T(8,128)(2,1)S(1)}, u32[]{:S(2)}, u32[]{:S(2)}) %collective-permute-start.6) | collective-permute-done | bytes 163872 | tf_op jit(solution)/shard_map/ppermute | solution.py:282
  31.1 0.1 collective-permute-start.7
  31.2 0.9 %constant_dynamic-slice_fusion.7.refs_3_ = bf16[20,16,128]{2,1,0:T(8,128)(2,1)S(1)} fusion(bf16[20,256,128]{2,1,0:T(8,128)(2,1)} %bitcast.36, s32[]{:T(128)S(6)} %select_n.47), kind=kLoop, calls=%fused_computation.16 | loop fusion | bytes 163844 | tf_op jit(solution)/shard_map/dynamic_slice | solution.py:275
  32.1 1.2 %collective-permute-done.7.refs_11_ = bf16[8,20,16,128]{3,2,1,0:T(8,128)(2,1)S(1)} collective-permute-done((bf16[8,20,16,128]{3,2,1,0:T(8,128)(2,1)S(1)}, bf16[8,20,16,128]{3,2,1,0:T(8,128)(2,1)S(1)}, u32[]{:S(2)}, u32[]{:S(2)}) %collective-permute-start.7) | collective-permute-done | bytes 655392 | tf_op jit(solution)/shard_map/ppermute | solution.py:284
  33.3 0.0 copy-done
  33.3 0.0 copy-done.1
  33.3 0.0 copy-done.2
  33.3 0.0 copy-done.3
  33.3 4.2 %prune.1 = f32[8,128]{1,0:T(8,128)S(1)} custom-call(s32[64]{0:T(128)S(1)} %copy-done.1, s32[1]{0:T(128)} %bitcast.me_ref, s32[1,512]{1,0:T(1,128)S(1)} %bitcast.31, f32[1,126]{1,0:T(1,128)S(1)} %bitcast.32, f32[1,126]{1,0:T(1,128)S(1)} %bitcast.33, bf16[20,16,128]{2,1,0:T(8,128)(2,1)S(1)} %constant_dynamic-slice_fusion.7.refs_3_, ...), custom_call_target="tpu_custom_call" | custom-call | tf_op jit(solution)/shard_map/prune/pallas_call | solution.py:198
  37.5 0.2 collective-permute-start.8
  37.7 1.0 %collective-permute-done.8 = f32[8,128]{1,0:T(8,128)S(1)} collective-permute-done((f32[8,128]{1,0:T(8,128)S(1)}, f32[8,128]{1,0:T(8,128)S(1)}, u32[]{:S(2)}, u32[]{:S(2)}) %collective-permute-start.8) | collective-permute-done | bytes 4128 | tf_op jit(solution)/shard_map/ppermute | solution.py:298
  38.7 0.3 collective-permute-start.9
  39.1 2.7 %collective-permute-done.9 = f32[8,128]{1,0:T(8,128)S(1)} collective-permute-done((f32[8,128]{1,0:T(8,128)S(1)}, f32[8,128]{1,0:T(8,128)S(1)}, u32[]{:S(2)}, u32[]{:S(2)}) %collective-permute-start.9) | collective-permute-done | bytes 4128 | tf_op jit(solution)/shard_map/ppermute | solution.py:298
  41.8 5.5 %collective-permute-start.10 = (f32[8,128]{1,0:T(8,128)S(1)}, f32[8,128]{1,0:T(8,128)S(1)}, u32[]{:S(2)}, u32[]{:S(2)}) collective-permute-start(f32[8,128]{1,0:T(8,128)S(1)} %add.70), channel_id=1, source_target_pairs={{0,5},{1,4},{2,7},{3,6},{4,1},{5,0},{6,3},{7,2},{8,13},{9,12},{10,... | collective-permute-start | bytes 12296 | tf_op jit(solution)/shard_map/ppermute | solution.py:298
  47.3 2.0 %collective-permute-start.11 = (f32[8,128]{1,0:T(8,128)S(1)}, f32[8,128]{1,0:T(8,128)S(1)}, u32[]{:S(2)}, u32[]{:S(2)}) collective-permute-start(f32[8,128]{1,0:T(8,128)S(1)} %add.70), channel_id=1, source_target_pairs={{0,9},{1,8},{2,11},{3,10},{4,13},{5,12},{6,15},{7,14},{8,1},{9,0},... | collective-permute-start | bytes 12296 | tf_op jit(solution)/shard_map/ppermute | solution.py:298
  49.3 1.4 %collective-permute-start.12 = (f32[8,128]{1,0:T(8,128)S(1)}, f32[8,128]{1,0:T(8,128)S(1)}, u32[]{:S(2)}, u32[]{:S(2)}) collective-permute-start(f32[8,128]{1,0:T(8,128)S(1)} %add.70), channel_id=1, source_target_pairs={{0,13},{1,12},{2,15},{3,14},{4,9},{5,8},{6,11},{7,10},{8,5},{9,4},... | collective-permute-start | bytes 12296 | tf_op jit(solution)/shard_map/ppermute | solution.py:298
  50.7 0.0 collective-permute-done.10
  50.7 0.5 collective-permute-done.11
  51.2 2.9 %collective-permute-done.12 = f32[8,128]{1,0:T(8,128)S(1)} collective-permute-done((f32[8,128]{1,0:T(8,128)S(1)}, f32[8,128]{1,0:T(8,128)S(1)}, u32[]{:S(2)}, u32[]{:S(2)}) %collective-permute-start.12) | collective-permute-done | bytes 4128 | tf_op jit(solution)/shard_map/ppermute | solution.py:298
  54.1 0.5 fusion
  (10 shorter events, 0.1 us)
Async XLA Ops:
  2.3 31.0 %copy-start = (s32[512]{0:T(512)S(1)}, s32[512]{0:T(512)}, u32[]{:S(2)}) copy-start(s32[512]{0:T(512)} %param.7) | copy-start | bytes 6148
  2.3 31.0 %copy-start.1 = (s32[64]{0:T(128)S(1)}, s32[64]{0:T(128)}, u32[]{:S(2)}) copy-start(s32[64]{0:T(128)} %order_ref.1) | copy-start | bytes 772
  2.3 31.0 %copy-start.2 = (f32[126]{0:T(128)S(1)}, f32[126]{0:T(128)}, u32[]{:S(2)}) copy-start(f32[126]{0:T(128)} %param.8) | copy-start | bytes 1516
  2.4 31.0 %copy-start.3 = (f32[126]{0:T(128)S(1)}, f32[126]{0:T(128)}, u32[]{:S(2)}) copy-start(f32[126]{0:T(128)} %param.9) | copy-start | bytes 1516
  2.4 13.6 %collective-permute-start = (bf16[20,32,128]{2,1,0:T(8,128)(2,1)S(1)}, bf16[20,32,128]{2,1,0:T(8,128)(2,1)S(1)}, u32[]{:S(2)}, u32[]{:S(2)}) collective-permute-start(bf16[20,32,128]{2,1,0:T(8,128)(2,1)S(1)} %get-tuple-element.8), channel_id=1, source_target_pairs={{0,8},{1,9},{2,10},{3,11},{4,12},{5,13},{6,14},{7,15},{8,0},{9,1},... | collective-permute-start | bytes 491528 | tf_op jit(solution)/shard_map/ppermute | solution.py:282
  6.5 12.9 %collective-permute-start.1 = (bf16[20,32,128]{2,1,0:T(8,128)(2,1)S(1)}, bf16[20,32,128]{2,1,0:T(8,128)(2,1)S(1)}, u32[]{:S(2)}, u32[]{:S(2)}) collective-permute-start(bf16[20,32,128]{2,1,0:T(8,128)(2,1)S(1)} %get-tuple-element.7), channel_id=1, source_target_pairs={{0,4},{1,5},{2,6},{3,7},{4,0},{5,1},{6,2},{7,3},{8,12},{9,13},{10,... | collective-permute-start | bytes 491528 | tf_op jit(solution)/shard_map/ppermute | solution.py:282
  8.0 15.8 %collective-permute-start.2 = (bf16[20,32,128]{2,1,0:T(8,128)(2,1)S(1)}, bf16[20,32,128]{2,1,0:T(8,128)(2,1)S(1)}, u32[]{:S(2)}, u32[]{:S(2)}) collective-permute-start(bf16[20,32,128]{2,1,0:T(8,128)(2,1)S(1)} %get-tuple-element.6), channel_id=1, source_target_pairs={{0,10},{1,11},{2,8},{3,9},{4,14},{5,15},{6,12},{7,13},{8,2},{9,3},... | collective-permute-start | bytes 491528 | tf_op jit(solution)/shard_map/ppermute | solution.py:282
  9.3 14.5 %collective-permute-start.3 = (bf16[20,32,128]{2,1,0:T(8,128)(2,1)S(1)}, bf16[20,32,128]{2,1,0:T(8,128)(2,1)S(1)}, u32[]{:S(2)}, u32[]{:S(2)}) collective-permute-start(bf16[20,32,128]{2,1,0:T(8,128)(2,1)S(1)} %get-tuple-element.5), channel_id=1, source_target_pairs={{0,6},{1,7},{2,4},{3,5},{4,2},{5,3},{6,0},{7,1},{8,14},{9,15},{10,... | collective-permute-start | bytes 491528 | tf_op jit(solution)/shard_map/ppermute | solution.py:282
  9.5 18.3 %collective-permute-start.4 = (bf16[20,32,128]{2,1,0:T(8,128)(2,1)S(1)}, bf16[20,32,128]{2,1,0:T(8,128)(2,1)S(1)}, u32[]{:S(2)}, u32[]{:S(2)}) collective-permute-start(bf16[20,32,128]{2,1,0:T(8,128)(2,1)S(1)} %get-tuple-element.4), channel_id=1, source_target_pairs={{0,12},{1,13},{2,14},{3,15},{4,8},{5,9},{6,10},{7,11},{8,4},{9,5},... | collective-permute-start | bytes 491528 | tf_op jit(solution)/shard_map/ppermute | solution.py:282
  15.9 11.9 %collective-permute-start.5 = (bf16[20,32,128]{2,1,0:T(8,128)(2,1)S(1)}, bf16[20,32,128]{2,1,0:T(8,128)(2,1)S(1)}, u32[]{:S(2)}, u32[]{:S(2)}) collective-permute-start(bf16[20,32,128]{2,1,0:T(8,128)(2,1)S(1)} %get-tuple-element.3), channel_id=1, source_target_pairs={{0,2},{1,3},{2,0},{3,1},{4,6},{5,7},{6,4},{7,5},{8,10},{9,11},{10,... | collective-permute-start | bytes 491528 | tf_op jit(solution)/shard_map/ppermute | solution.py:282
  19.4 11.7 %collective-permute-start.6 = (bf16[20,32,128]{2,1,0:T(8,128)(2,1)S(1)}, bf16[20,32,128]{2,1,0:T(8,128)(2,1)S(1)}, u32[]{:S(2)}, u32[]{:S(2)}) collective-permute-start(bf16[20,32,128]{2,1,0:T(8,128)(2,1)S(1)} %get-tuple-element.2), channel_id=1, source_target_pairs={{0,14},{1,15},{2,12},{3,13},{4,10},{5,11},{6,8},{7,9},{8,6},{9,7},... | collective-permute-start | bytes 491528 | tf_op jit(solution)/shard_map/ppermute | solution.py:282
  31.1 2.2 %collective-permute-start.7 = (bf16[8,20,16,128]{3,2,1,0:T(8,128)(2,1)S(1)}, bf16[8,20,16,128]{3,2,1,0:T(8,128)(2,1)S(1)}, u32[]{:S(2)}, u32[]{:S(2)}) collective-permute-start(bf16[8,20,16,128]{3,2,1,0:T(8,128)(2,1)S(1)} %bitcast_dynamic-update-slice_fusion), channel_id=1, source_target_pairs={{0,1},{1,0},{2,3},{3,2},{4,5},{5,4},{6,7},{7,6},{8,9},{9,8},{10,11... | collective-permute-start | bytes 1966088 | tf_op jit(solution)/shard_map/ppermute | solution.py:284
  37.5 1.2 %collective-permute-start.8 = (f32[8,128]{1,0:T(8,128)S(1)}, f32[8,128]{1,0:T(8,128)S(1)}, u32[]{:S(2)}, u32[]{:S(2)}) collective-permute-start(f32[8,128]{1,0:T(8,128)S(1)} %prune.1), channel_id=1, source_target_pairs={{0,1},{1,0},{2,3},{3,2},{4,5},{5,4},{6,7},{7,6},{8,9},{9,8},{10,11... | collective-permute-start | bytes 12296 | tf_op jit(solution)/shard_map/ppermute | solution.py:298
  38.7 3.0 %collective-permute-start.9 = (f32[8,128]{1,0:T(8,128)S(1)}, f32[8,128]{1,0:T(8,128)S(1)}, u32[]{:S(2)}, u32[]{:S(2)}) collective-permute-start(f32[8,128]{1,0:T(8,128)S(1)} %add.69), channel_id=1, source_target_pairs={{0,3},{1,2},{2,1},{3,0},{4,7},{5,6},{6,5},{7,4},{8,11},{9,10},{10,... | collective-permute-start | bytes 12296 | tf_op jit(solution)/shard_map/ppermute | solution.py:298
  41.8 9.0 %collective-permute-start.10 = (f32[8,128]{1,0:T(8,128)S(1)}, f32[8,128]{1,0:T(8,128)S(1)}, u32[]{:S(2)}, u32[]{:S(2)}) collective-permute-start(f32[8,128]{1,0:T(8,128)S(1)} %add.70), channel_id=1, source_target_pairs={{0,5},{1,4},{2,7},{3,6},{4,1},{5,0},{6,3},{7,2},{8,13},{9,12},{10,... | collective-permute-start | bytes 12296 | tf_op jit(solution)/shard_map/ppermute | solution.py:298
  47.3 3.9 %collective-permute-start.11 = (f32[8,128]{1,0:T(8,128)S(1)}, f32[8,128]{1,0:T(8,128)S(1)}, u32[]{:S(2)}, u32[]{:S(2)}) collective-permute-start(f32[8,128]{1,0:T(8,128)S(1)} %add.70), channel_id=1, source_target_pairs={{0,9},{1,8},{2,11},{3,10},{4,13},{5,12},{6,15},{7,14},{8,1},{9,0},... | collective-permute-start | bytes 12296 | tf_op jit(solution)/shard_map/ppermute | solution.py:298
  49.3 4.8 %collective-permute-start.12 = (f32[8,128]{1,0:T(8,128)S(1)}, f32[8,128]{1,0:T(8,128)S(1)}, u32[]{:S(2)}, u32[]{:S(2)}) collective-permute-start(f32[8,128]{1,0:T(8,128)S(1)} %add.70), channel_id=1, source_target_pairs={{0,13},{1,12},{2,15},{3,14},{4,9},{5,8},{6,11},{7,10},{8,5},{9,4},... | collective-permute-start | bytes 12296 | tf_op jit(solution)/shard_map/ppermute | solution.py:298

commit v3 on v2

--- a/solution.py
+++ b/solution.py
@@ -12,7 +12,10 @@
 
 
 def part_sum(x):
-    return jnp.sum(x, axis=0)
+    parts = [x[i] for i in range(len(x))]
+    while len(parts) > 1:
+        parts = [sum(parts[i + 1 : i + 2], parts[i]) for i in range(0, len(parts), 2)]
+    return parts[0]
 
 
 def both(half):
@@ -44,8 +47,9 @@
 
     rate_ref[...] = column((grow - 1.0) / states)
     slope_ref[...] = column(decay * toward * grow / states)
-    grad_ref[...] = jnp.zeros_like(grad_ref)
-    curve_ref[...] = jnp.zeros_like(curve_ref)
+    unused = jnp.zeros((grad_ref.shape[0] - branches * ROWS, LANES), F32)
+    grad_ref[branches * ROWS :, :] = unused
+    curve_ref[branches * ROWS :, :] = unused
     raw = weight_ref[...].astype(F32)
     quarter = [raw[:, part * LANES : (part + 1) * LANES] for part in range(4)]
     weight = jnp.concatenate(quarter + quarter, axis=0)
@@ -130,8 +134,9 @@
     dseed = -(dtotal * seed) * seed
 
     def record(at, grad, curve):
-        grad_ref[pl.ds(at, 1), :] = jnp.sum(weight * grad, axis=0, keepdims=True)
-        curve_ref[pl.ds(at, 1), :] = jnp.sum(weight * curve, axis=0, keepdims=True)
+        here = pl.ds(pl.multiple_of(at * ROWS, ROWS), ROWS)
+        grad_ref[here, :] = weight * grad
+        curve_ref[here, :] = weight * curve
 
     def down(at, ybar, dybar):
         half, dhalf = part_sum(ybar), part_sum(dybar)
@@ -177,8 +182,12 @@
     lax.fori_loop(0, tips >> cut, descend, 0)
 
     scale = decay * grow / states
-    grad = jnp.sum(jnp.transpose(grad_ref[...]), axis=0, keepdims=True)[:, :branches] * scale
-    curve = jnp.sum(jnp.transpose(curve_ref[...]), axis=0, keepdims=True)[:, :branches] * scale
+
+    def over_sites(ref):
+        rows = part_sum([ref[pl.ds(part, LANES, ROWS), :] for part in range(ROWS)])
+        return jnp.sum(jnp.transpose(rows), axis=0, keepdims=True)[:, :branches] * scale
+
+    grad, curve = over_sites(grad_ref), over_sites(curve_ref)
     curve = curve + decay * toward * grad
     out_ref[...] = jnp.zeros_like(out_ref)
     out_ref[0:1, :branches] = grad
@@ -213,8 +222,8 @@
             pltpu.VMEM((cut, *vec), F32),
             pltpu.VMEM((cut, *vec), F32),
             pltpu.VMEM((cut, ROWS, LANES), F32),
-            pltpu.VMEM((LANES, LANES), F32),
-            pltpu.VMEM((LANES, LANES), F32),
+            pltpu.VMEM((LANES * ROWS, LANES), F32),
+            pltpu.VMEM((LANES * ROWS, LANES), F32),
         ],
         compiler_params=pltpu.CompilerParams(vmem_limit_bytes=32 * 1024 * 1024),
         name="prune",
@@ -287,13 +296,14 @@
 
 def total_over_sites(part):
     peers = lax.axis_size("sites")
-    rounds, bit = [[1], [3]], 4
-    while bit < peers:
-        if 2 * bit < peers:
-            rounds.append([bit + 1, 2 * bit + 1, 3 * bit + 1])
-        else:
-            rounds.append([bit + 1])
-        bit *= 4
+    steps, bit = [2, peers - 4], 4
+    while bit < peers // 2:
+        steps.append(bit)
+        bit *= 2
+    rounds = [[1]]
+    for first in range(0, len(steps), 2):
+        pair = steps[first : first + 2]
+        rounds.append([step + 1 for step in ([*pair, pair[0] ^ pair[1]] if len(pair) > 1 else pair)])
     for apart in rounds:
         got = [lax.ppermute(part, "sites", [(i, i ^ step) for i in range(peers)]) for step in apart]
         part = part + got[0]

time: 54.9 us -> 52.5 us (0.956)
  waiting for transfers between devices: 20.4 us -> 18.2 us
    ppermute x5, waiting for transfers between devices: 7.15 us -> 4.88 us  [total_over_sites(): lax.ppermute(part, 'sites', [(i, i ^ step) for i in range(peers)])]
  transfers between devices with their start and end apart: 13 -> 13, of which waited for: 9 -> 9; matrix products, arithmetic and copies ran while one was open for 3% -> 4% of each run, Pallas kernels for 0% -> 0%
where the time goes in v3:
time: 52.5 us; the launch traced here: 52.3 us
  starting transfers between devices  25.4 us (48%)
  waiting for transfers between devices  18.2 us (35%)
  Pallas kernels  3.84 us (7%)
  local copies, waits for them, and re-layouts  3.56 us (7%)
  between operations  0.81 us (2%)
  other arithmetic  0.54 us (1%)
    ppermute x7, starting transfers between devices, exchange_pairs(): lax.ppermute(cut(probs, 2 * deep * (chip ^ apart), 2 * deep), 'sites', swap)  15.6 us
    ppermute x7, waiting for transfers between devices, exchange_pairs(): lax.ppermute(cut(probs, 2 * deep * (chip ^ apart), 2 * deep), 'sites', swap)  12.1 us
    ppermute x5, starting transfers between devices, total_over_sites(): lax.ppermute(part, 'sites', [(i, i ^ step) for i in range(peers)])  9.73 us
    ppermute x5, waiting for transfers between devices, total_over_sites(): lax.ppermute(part, 'sites', [(i, i ^ step) for i in range(peers)])  4.88 us
    pallas_call x1, Pallas kernels, prune(): pl.pallas_call(functools.partial(prune_kernel, unpack=unpack, held=len(pi...  3.84 us
    dynamic_slice x2, local copies, waits for them, and re-layouts, cut(): return lax.dynamic_slice(block, (0, first, 0), (states, count, LANES))  2.54 us
    ppermute x1, waiting for transfers between devices, exchange_pairs(): lax.ppermute(jnp.stack(give), 'sites', [(i, i ^ 1) for i in range(peers)])  1.18 us
  transfers between devices with their start and end apart: 13, of which 9 were waited for; matrix products, arithmetic and copies ran while one was open for 4% of the time, Pallas kernels for 0%

profile of v3, /device:TPU:0, one launch (start us, length us, event | category | flops | bytes accessed | tf_op | source)
XLA Modules:
  0.0 52.3 jit_solution(5390785744921119742)
XLA Ops:
  0.7 1.6 %constant_dynamic-slice_fusion = (bf16[20,32,128]{2,1,0:T(8,128)(2,1)S(1)}, bf16[20,32,128]{2,1,0:T(8,128)(2,1)S(1)}, bf16[20,32,128]{2,1,0:T(8,128)(2,1)S(1)}, ...) fusion(bf16[20,256,128]{2,1,0:T(8,128)(2,1)} %bitcast.34, ...), kind=kLoop, calls=%fused_computation.9 | loop fusion | bytes 2293788 | tf_op jit(solution)/shard_map/dynamic_slice | solution.py:284
  2.3 0.0 copy-start
  2.3 0.0 copy-start.1
  2.3 0.0 copy-start.2
  2.4 0.0 copy-start.3
  2.4 4.1 %collective-permute-start = (bf16[20,32,128]{2,1,0:T(8,128)(2,1)S(1)}, bf16[20,32,128]{2,1,0:T(8,128)(2,1)S(1)}, u32[]{:S(2)}, u32[]{:S(2)}) collective-permute-start(bf16[20,32,128]{2,1,0:T(8,128)(2,1)S(1)} %get-tuple-element.8), channel_id=1, source_target_pairs={{0,8},{1,9},{2,10},{3,11},{4,12},{5,13},{6,14},{7,15},{8,0},{9,1},... | collective-permute-start | bytes 491528 | tf_op jit(solution)/shard_map/ppermute | solution.py:291
  6.5 1.6 %collective-permute-start.1 = (bf16[20,32,128]{2,1,0:T(8,128)(2,1)S(1)}, bf16[20,32,128]{2,1,0:T(8,128)(2,1)S(1)}, u32[]{:S(2)}, u32[]{:S(2)}) collective-permute-start(bf16[20,32,128]{2,1,0:T(8,128)(2,1)S(1)} %get-tuple-element.7), channel_id=1, source_target_pairs={{0,4},{1,5},{2,6},{3,7},{4,0},{5,1},{6,2},{7,3},{8,12},{9,13},{10,... | collective-permute-start | bytes 491528 | tf_op jit(solution)/shard_map/ppermute | solution.py:291
  8.0 1.3 %collective-permute-start.2 = (bf16[20,32,128]{2,1,0:T(8,128)(2,1)S(1)}, bf16[20,32,128]{2,1,0:T(8,128)(2,1)S(1)}, u32[]{:S(2)}, u32[]{:S(2)}) collective-permute-start(bf16[20,32,128]{2,1,0:T(8,128)(2,1)S(1)} %get-tuple-element.6), channel_id=1, source_target_pairs={{0,10},{1,11},{2,8},{3,9},{4,14},{5,15},{6,12},{7,13},{8,2},{9,3},... | collective-permute-start | bytes 491528 | tf_op jit(solution)/shard_map/ppermute | solution.py:291
  9.3 0.1 collective-permute-start.3
  9.5 3.9 %collective-permute-start.4 = (bf16[20,32,128]{2,1,0:T(8,128)(2,1)S(1)}, bf16[20,32,128]{2,1,0:T(8,128)(2,1)S(1)}, u32[]{:S(2)}, u32[]{:S(2)}) collective-permute-start(bf16[20,32,128]{2,1,0:T(8,128)(2,1)S(1)} %get-tuple-element.4), channel_id=1, source_target_pairs={{0,12},{1,13},{2,14},{3,15},{4,8},{5,9},{6,10},{7,11},{8,4},{9,5},... | collective-permute-start | bytes 491528 | tf_op jit(solution)/shard_map/ppermute | solution.py:291
  13.3 0.9 %bitcast_dynamic-update-slice_fusion.7 = bf16[8,20,16,128]{3,2,1,0:T(8,128)(2,1)S(1)} fusion(bf16[20,256,128]{2,1,0:T(8,128)(2,1)} %bitcast.35, s32[]{:T(128)S(6)} %select_n.56), kind=kLoop, calls=%fused_computation.7 | loop fusion | bytes 163844
  14.2 1.7 %collective-permute-done.refs_4_ = bf16[20,32,128]{2,1,0:T(8,128)(2,1)S(1)} collective-permute-done((bf16[20,32,128]{2,1,0:T(8,128)(2,1)S(1)}, bf16[20,32,128]{2,1,0:T(8,128)(2,1)S(1)}, u32[]{:S(2)}, u32[]{:S(2)}) %collective-permute-start) | collective-permute-done | bytes 163872 | tf_op jit(solution)/shard_map/ppermute | solution.py:291
  15.9 3.5 %collective-permute-start.5 = (bf16[20,32,128]{2,1,0:T(8,128)(2,1)S(1)}, bf16[20,32,128]{2,1,0:T(8,128)(2,1)S(1)}, u32[]{:S(2)}, u32[]{:S(2)}) collective-permute-start(bf16[20,32,128]{2,1,0:T(8,128)(2,1)S(1)} %get-tuple-element.3), channel_id=1, source_target_pairs={{0,2},{1,3},{2,0},{3,1},{4,6},{5,7},{6,4},{7,5},{8,10},{9,11},{10,... | collective-permute-start | bytes 491528 | tf_op jit(solution)/shard_map/ppermute | solution.py:291
  19.4 0.0 collective-permute-done.1.refs_5_
  19.4 1.2 %collective-permute-start.6 = (bf16[20,32,128]{2,1,0:T(8,128)(2,1)S(1)}, bf16[20,32,128]{2,1,0:T(8,128)(2,1)S(1)}, u32[]{:S(2)}, u32[]{:S(2)}) collective-permute-start(bf16[20,32,128]{2,1,0:T(8,128)(2,1)S(1)} %get-tuple-element.2), channel_id=1, source_target_pairs={{0,14},{1,15},{2,12},{3,13},{4,10},{5,11},{6,8},{7,9},{8,6},{9,7},... | collective-permute-start | bytes 491528 | tf_op jit(solution)/shard_map/ppermute | solution.py:291
  20.6 3.3 %collective-permute-done.2.refs_6_ = bf16[20,32,128]{2,1,0:T(8,128)(2,1)S(1)} collective-permute-done((bf16[20,32,128]{2,1,0:T(8,128)(2,1)S(1)}, bf16[20,32,128]{2,1,0:T(8,128)(2,1)S(1)}, u32[]{:S(2)}, u32[]{:S(2)}) %collective-permute-start.2) | collective-permute-done | bytes 163872 | tf_op jit(solution)/shard_map/ppermute | solution.py:291
  23.9 0.0 collective-permute-done.3.refs_7_
  23.9 3.9 %collective-permute-done.4.refs_8_ = bf16[20,32,128]{2,1,0:T(8,128)(2,1)S(1)} collective-permute-done((bf16[20,32,128]{2,1,0:T(8,128)(2,1)S(1)}, bf16[20,32,128]{2,1,0:T(8,128)(2,1)S(1)}, u32[]{:S(2)}, u32[]{:S(2)}) %collective-permute-start.4) | collective-permute-done | bytes 163872 | tf_op jit(solution)/shard_map/ppermute | solution.py:291
  27.8 0.0 collective-permute-done.5.refs_9_
  27.9 3.3 %collective-permute-done.6.refs_10_ = bf16[20,32,128]{2,1,0:T(8,128)(2,1)S(1)} collective-permute-done((bf16[20,32,128]{2,1,0:T(8,128)(2,1)S(1)}, bf16[20,32,128]{2,1,0:T(8,128)(2,1)S(1)}, u32[]{:S(2)}, u32[]{:S(2)}) %collective-permute-start.6) | collective-permute-done | bytes 163872 | tf_op jit(solution)/shard_map/ppermute | solution.py:291
  31.1 0.1 collective-permute-start.7
  31.2 0.9 %constant_dynamic-slice_fusion.7.refs_3_ = bf16[20,16,128]{2,1,0:T(8,128)(2,1)S(1)} fusion(bf16[20,256,128]{2,1,0:T(8,128)(2,1)} %bitcast.36, s32[]{:T(128)S(6)} %select_n.47), kind=kLoop, calls=%fused_computation.16 | loop fusion | bytes 163844 | tf_op jit(solution)/shard_map/dynamic_slice | solution.py:284
  32.1 1.2 %collective-permute-done.7.refs_11_ = bf16[8,20,16,128]{3,2,1,0:T(8,128)(2,1)S(1)} collective-permute-done((bf16[8,20,16,128]{3,2,1,0:T(8,128)(2,1)S(1)}, bf16[8,20,16,128]{3,2,1,0:T(8,128)(2,1)S(1)}, u32[]{:S(2)}, u32[]{:S(2)}) %collective-permute-start.7) | collective-permute-done | bytes 655392 | tf_op jit(solution)/shard_map/ppermute | solution.py:293
  33.3 0.0 copy-done
  33.3 0.0 copy-done.1
  33.3 0.0 copy-done.2
  33.3 0.0 copy-done.3
  33.3 3.8 %prune.1 = f32[8,128]{1,0:T(8,128)S(1)} custom-call(s32[64]{0:T(128)S(1)} %copy-done.1, s32[1]{0:T(128)} %bitcast.me_ref, s32[1,512]{1,0:T(1,128)S(1)} %bitcast.31, f32[1,126]{1,0:T(1,128)S(1)} %bitcast.32, f32[1,126]{1,0:T(1,128)S(1)} %bitcast.33, bf16[20,16,128]{2,1,0:T(8,128)(2,1)S(1)} %constant_dynamic-slice_fusion.7.refs_3_, ...), custom_call_target="tpu_custom_call" | custom-call | tf_op jit(solution)/shard_map/prune/pallas_call | solution.py:207
  37.2 0.2 collective-permute-start.8
  37.4 1.0 %collective-permute-done.8 = f32[8,128]{1,0:T(8,128)S(1)} collective-permute-done((f32[8,128]{1,0:T(8,128)S(1)}, f32[8,128]{1,0:T(8,128)S(1)}, u32[]{:S(2)}, u32[]{:S(2)}) %collective-permute-start.8) | collective-permute-done | bytes 4128 | tf_op jit(solution)/shard_map/ppermute | solution.py:308
  38.4 1.6 %collective-permute-start.10 = (f32[8,128]{1,0:T(8,128)S(1)}, f32[8,128]{1,0:T(8,128)S(1)}, u32[]{:S(2)}, u32[]{:S(2)}) collective-permute-start(f32[8,128]{1,0:T(8,128)S(1)} %add.69), channel_id=1, source_target_pairs={{0,13},{1,12},{2,15},{3,14},{4,9},{5,8},{6,11},{7,10},{8,5},{9,4},... | collective-permute-start | bytes 12296 | tf_op jit(solution)/shard_map/ppermute | solution.py:308
  40.0 2.0 %collective-permute-start.11 = (f32[8,128]{1,0:T(8,128)S(1)}, f32[8,128]{1,0:T(8,128)S(1)}, u32[]{:S(2)}, u32[]{:S(2)}) collective-permute-start(f32[8,128]{1,0:T(8,128)S(1)} %add.69), channel_id=1, source_target_pairs={{0,15},{1,14},{2,13},{3,12},{4,11},{5,10},{6,9},{7,8},{8,7},{9,6},... | collective-permute-start | bytes 12296 | tf_op jit(solution)/shard_map/ppermute | solution.py:308
  41.9 1.2 %collective-permute-start.9 = (f32[8,128]{1,0:T(8,128)S(1)}, f32[8,128]{1,0:T(8,128)S(1)}, u32[]{:S(2)}, u32[]{:S(2)}) collective-permute-start(f32[8,128]{1,0:T(8,128)S(1)} %add.69), channel_id=1, source_target_pairs={{0,3},{1,2},{2,1},{3,0},{4,7},{5,6},{6,5},{7,4},{8,11},{9,10},{10,... | collective-permute-start | bytes 12296 | tf_op jit(solution)/shard_map/ppermute | solution.py:308
  43.2 0.1 collective-permute-done.10
  43.2 2.5 %collective-permute-done.11 = f32[8,128]{1,0:T(8,128)S(1)} collective-permute-done((f32[8,128]{1,0:T(8,128)S(1)}, f32[8,128]{1,0:T(8,128)S(1)}, u32[]{:S(2)}, u32[]{:S(2)}) %collective-permute-start.11) | collective-permute-done | bytes 4128 | tf_op jit(solution)/shard_map/ppermute | solution.py:308
  45.7 0.0 collective-permute-done.9
  45.7 4.8 %collective-permute-start.12 = (f32[8,128]{1,0:T(8,128)S(1)}, f32[8,128]{1,0:T(8,128)S(1)}, u32[]{:S(2)}, u32[]{:S(2)}) collective-permute-start(f32[8,128]{1,0:T(8,128)S(1)} %add_add_fusion), channel_id=1, source_target_pairs={{0,5},{1,4},{2,7},{3,6},{4,1},{5,0},{6,3},{7,2},{8,13},{9,12},{10,... | collective-permute-start | bytes 12296 | tf_op jit(solution)/shard_map/ppermute | solution.py:308
  50.5 1.3 %collective-permute-done.12 = f32[8,128]{1,0:T(8,128)S(1)} collective-permute-done((f32[8,128]{1,0:T(8,128)S(1)}, f32[8,128]{1,0:T(8,128)S(1)}, u32[]{:S(2)}, u32[]{:S(2)}) %collective-permute-start.12) | collective-permute-done | bytes 4128 | tf_op jit(solution)/shard_map/ppermute | solution.py:308
  51.8 0.5 %fusion = (f32[126]{0:T(128)}, f32[126]{0:T(128)}) fusion(f32[8,128]{1,0:T(8,128)S(1)} %add.73), kind=kLoop, calls=%fused_computation.20 | loop fusion | flops 378 | bytes 2520 | tf_op jit(solution)/shard_map/div | solution.py:327
  (10 shorter events, 0.1 us)
Async XLA Ops:
  2.3 31.0 %copy-start = (s32[512]{0:T(512)S(1)}, s32[512]{0:T(512)}, u32[]{:S(2)}) copy-start(s32[512]{0:T(512)} %param.7) | copy-start | bytes 6148
  2.3 31.0 %copy-start.1 = (s32[64]{0:T(128)S(1)}, s32[64]{0:T(128)}, u32[]{:S(2)}) copy-start(s32[64]{0:T(128)} %order_ref.1) | copy-start | bytes 772
  2.3 31.0 %copy-start.2 = (f32[126]{0:T(128)S(1)}, f32[126]{0:T(128)}, u32[]{:S(2)}) copy-start(f32[126]{0:T(128)} %param.8) | copy-start | bytes 1516
  2.4 31.0 %copy-start.3 = (f32[126]{0:T(128)S(1)}, f32[126]{0:T(128)}, u32[]{:S(2)}) copy-start(f32[126]{0:T(128)} %param.9) | copy-start | bytes 1516
  2.4 13.6 %collective-permute-start = (bf16[20,32,128]{2,1,0:T(8,128)(2,1)S(1)}, bf16[20,32,128]{2,1,0:T(8,128)(2,1)S(1)}, u32[]{:S(2)}, u32[]{:S(2)}) collective-permute-start(bf16[20,32,128]{2,1,0:T(8,128)(2,1)S(1)} %get-tuple-element.8), channel_id=1, source_target_pairs={{0,8},{1,9},{2,10},{3,11},{4,12},{5,13},{6,14},{7,15},{8,0},{9,1},... | collective-permute-start | bytes 491528 | tf_op jit(solution)/shard_map/ppermute | solution.py:291
  6.5 12.9 %collective-permute-start.1 = (bf16[20,32,128]{2,1,0:T(8,128)(2,1)S(1)}, bf16[20,32,128]{2,1,0:T(8,128)(2,1)S(1)}, u32[]{:S(2)}, u32[]{:S(2)}) collective-permute-start(bf16[20,32,128]{2,1,0:T(8,128)(2,1)S(1)} %get-tuple-element.7), channel_id=1, source_target_pairs={{0,4},{1,5},{2,6},{3,7},{4,0},{5,1},{6,2},{7,3},{8,12},{9,13},{10,... | collective-permute-start | bytes 491528 | tf_op jit(solution)/shard_map/ppermute | solution.py:291
  8.0 15.8 %collective-permute-start.2 = (bf16[20,32,128]{2,1,0:T(8,128)(2,1)S(1)}, bf16[20,32,128]{2,1,0:T(8,128)(2,1)S(1)}, u32[]{:S(2)}, u32[]{:S(2)}) collective-permute-start(bf16[20,32,128]{2,1,0:T(8,128)(2,1)S(1)} %get-tuple-element.6), channel_id=1, source_target_pairs={{0,10},{1,11},{2,8},{3,9},{4,14},{5,15},{6,12},{7,13},{8,2},{9,3},... | collective-permute-start | bytes 491528 | tf_op jit(solution)/shard_map/ppermute | solution.py:291
  9.3 14.5 %collective-permute-start.3 = (bf16[20,32,128]{2,1,0:T(8,128)(2,1)S(1)}, bf16[20,32,128]{2,1,0:T(8,128)(2,1)S(1)}, u32[]{:S(2)}, u32[]{:S(2)}) collective-permute-start(bf16[20,32,128]{2,1,0:T(8,128)(2,1)S(1)} %get-tuple-element.5), channel_id=1, source_target_pairs={{0,6},{1,7},{2,4},{3,5},{4,2},{5,3},{6,0},{7,1},{8,14},{9,15},{10,... | collective-permute-start | bytes 491528 | tf_op jit(solution)/shard_map/ppermute | solution.py:291
  9.5 18.3 %collective-permute-start.4 = (bf16[20,32,128]{2,1,0:T(8,128)(2,1)S(1)}, bf16[20,32,128]{2,1,0:T(8,128)(2,1)S(1)}, u32[]{:S(2)}, u32[]{:S(2)}) collective-permute-start(bf16[20,32,128]{2,1,0:T(8,128)(2,1)S(1)} %get-tuple-element.4), channel_id=1, source_target_pairs={{0,12},{1,13},{2,14},{3,15},{4,8},{5,9},{6,10},{7,11},{8,4},{9,5},... | collective-permute-start | bytes 491528 | tf_op jit(solution)/shard_map/ppermute | solution.py:291
  15.9 11.9 %collective-permute-start.5 = (bf16[20,32,128]{2,1,0:T(8,128)(2,1)S(1)}, bf16[20,32,128]{2,1,0:T(8,128)(2,1)S(1)}, u32[]{:S(2)}, u32[]{:S(2)}) collective-permute-start(bf16[20,32,128]{2,1,0:T(8,128)(2,1)S(1)} %get-tuple-element.3), channel_id=1, source_target_pairs={{0,2},{1,3},{2,0},{3,1},{4,6},{5,7},{6,4},{7,5},{8,10},{9,11},{10,... | collective-permute-start | bytes 491528 | tf_op jit(solution)/shard_map/ppermute | solution.py:291
  19.4 11.7 %collective-permute-start.6 = (bf16[20,32,128]{2,1,0:T(8,128)(2,1)S(1)}, bf16[20,32,128]{2,1,0:T(8,128)(2,1)S(1)}, u32[]{:S(2)}, u32[]{:S(2)}) collective-permute-start(bf16[20,32,128]{2,1,0:T(8,128)(2,1)S(1)} %get-tuple-element.2), channel_id=1, source_target_pairs={{0,14},{1,15},{2,12},{3,13},{4,10},{5,11},{6,8},{7,9},{8,6},{9,7},... | collective-permute-start | bytes 491528 | tf_op jit(solution)/shard_map/ppermute | solution.py:291
  31.1 2.2 %collective-permute-start.7 = (bf16[8,20,16,128]{3,2,1,0:T(8,128)(2,1)S(1)}, bf16[8,20,16,128]{3,2,1,0:T(8,128)(2,1)S(1)}, u32[]{:S(2)}, u32[]{:S(2)}) collective-permute-start(bf16[8,20,16,128]{3,2,1,0:T(8,128)(2,1)S(1)} %bitcast_dynamic-update-slice_fusion), channel_id=1, source_target_pairs={{0,1},{1,0},{2,3},{3,2},{4,5},{5,4},{6,7},{7,6},{8,9},{9,8},{10,11... | collective-permute-start | bytes 1966088 | tf_op jit(solution)/shard_map/ppermute | solution.py:293
  37.2 1.2 %collective-permute-start.8 = (f32[8,128]{1,0:T(8,128)S(1)}, f32[8,128]{1,0:T(8,128)S(1)}, u32[]{:S(2)}, u32[]{:S(2)}) collective-permute-start(f32[8,128]{1,0:T(8,128)S(1)} %prune.1), channel_id=1, source_target_pairs={{0,1},{1,0},{2,3},{3,2},{4,5},{5,4},{6,7},{7,6},{8,9},{9,8},{10,11... | collective-permute-start | bytes 12296 | tf_op jit(solution)/shard_map/ppermute | solution.py:308
  38.4 4.8 %collective-permute-start.10 = (f32[8,128]{1,0:T(8,128)S(1)}, f32[8,128]{1,0:T(8,128)S(1)}, u32[]{:S(2)}, u32[]{:S(2)}) collective-permute-start(f32[8,128]{1,0:T(8,128)S(1)} %add.69), channel_id=1, source_target_pairs={{0,13},{1,12},{2,15},{3,14},{4,9},{5,8},{6,11},{7,10},{8,5},{9,4},... | collective-permute-start | bytes 12296 | tf_op jit(solution)/shard_map/ppermute | solution.py:308
  40.0 5.7 %collective-permute-start.11 = (f32[8,128]{1,0:T(8,128)S(1)}, f32[8,128]{1,0:T(8,128)S(1)}, u32[]{:S(2)}, u32[]{:S(2)}) collective-permute-start(f32[8,128]{1,0:T(8,128)S(1)} %add.69), channel_id=1, source_target_pairs={{0,15},{1,14},{2,13},{3,12},{4,11},{5,10},{6,9},{7,8},{8,7},{9,6},... | collective-permute-start | bytes 12296 | tf_op jit(solution)/shard_map/ppermute | solution.py:308
  41.9 3.8 %collective-permute-start.9 = (f32[8,128]{1,0:T(8,128)S(1)}, f32[8,128]{1,0:T(8,128)S(1)}, u32[]{:S(2)}, u32[]{:S(2)}) collective-permute-start(f32[8,128]{1,0:T(8,128)S(1)} %add.69), channel_id=1, source_target_pairs={{0,3},{1,2},{2,1},{3,0},{4,7},{5,6},{6,5},{7,4},{8,11},{9,10},{10,... | collective-permute-start | bytes 12296 | tf_op jit(solution)/shard_map/ppermute | solution.py:308
  45.7 6.1 %collective-permute-start.12 = (f32[8,128]{1,0:T(8,128)S(1)}, f32[8,128]{1,0:T(8,128)S(1)}, u32[]{:S(2)}, u32[]{:S(2)}) collective-permute-start(f32[8,128]{1,0:T(8,128)S(1)} %add_add_fusion), channel_id=1, source_target_pairs={{0,5},{1,4},{2,7},{3,6},{4,1},{5,0},{6,3},{7,2},{8,13},{9,12},{10,... | collective-permute-start | bytes 12296 | tf_op jit(solution)/shard_map/ppermute | solution.py:308

commit v4 on v3

--- a/solution.py
+++ b/solution.py
@@ -273,25 +273,54 @@
     return [arrived.reshape(peers, -1, LANES)], unpack_plain
 
 
-def exchange_pairs(probs):
+def cut_kernel(me_ref, probs_ref, after_ref, *refs, firsts):
+    out_refs, sems = refs[:-1], refs[-1]
+    me = me_ref[0]
+    copies = []
+    for number, (out_ref, first) in enumerate(zip(out_refs, firsts)):
+        count = out_ref.shape[1]
+        start = pl.multiple_of(first(me), count)
+        copies.append(pltpu.make_async_copy(probs_ref.at[:, pl.ds(start, count), :], out_ref, sems.at[number]))
+    for copy in copies:
+        copy.start()
+    for copy in copies:
+        copy.wait()
+
+
+def cut(probs, me, firsts, counts, after):
+    vm = pl.BlockSpec(memory_space=pltpu.VMEM)
+    return pl.pallas_call(
+        functools.partial(cut_kernel, firsts=firsts),
+        in_specs=[pl.BlockSpec(memory_space=pltpu.SMEM), pl.BlockSpec(memory_space=pltpu.HBM), pl.BlockSpec(memory_space=pl.ANY)],
+        out_specs=[vm] * len(counts),
+        out_shape=[jax.ShapeDtypeStruct((probs.shape[0], count, LANES), probs.dtype) for count in counts],
+        scratch_shapes=[pltpu.SemaphoreType.DMA((len(counts),))],
+        compiler_params=pltpu.CompilerParams(vmem_limit_bytes=16 * 1024 * 1024),
+        name="cut",
+    )(me.reshape(1), pltpu.with_memory_space_constraint(probs, pltpu.HBM), after)
+
+
+def exchange_pairs(probs, me):
     peers = lax.axis_size("sites")
-    chips, me = peers // 2, lax.axis_index("sites")
-    chip, core = me // 2, me % 2
+    chips = peers // 2
+    core = me % 2
     states, rows, _ = probs.shape
     deep = rows // peers
-
-    def cut(block, first, count):
-        return lax.dynamic_slice(block, (0, first, 0), (states, count, LANES))
-
     far, near = range(chips // 2, chips), [*range(2, chips // 2), 1]
     order = [far[0], *(apart for pair in zip(near, far[1:]) for apart in pair)]
+    firsts = [lambda me, apart=apart: (((me // 2) ^ apart) * (2 * deep)) for apart in order]
+    firsts += [lambda me: me * deep, lambda me: (me ^ 1) * deep]
+    counts = [2 * deep] * len(order) + [deep] * 2
+    head = cut(probs, me, firsts[:1], counts[:1], me.reshape(1))
+    *tail, own, spare = cut(probs, me, firsts[1:], counts[1:], head[0])
+    sent = [*head, *tail]
     got = []
-    for apart in order:
-        swap = [(i, i ^ (2 * apart)) for i in range(peers)]
-        got.append(lax.ppermute(cut(probs, 2 * deep * (chip ^ apart), 2 * deep), "sites", swap))
-    give = [cut(probs, deep * (me ^ 1), deep)] + [cut(block, deep * (1 - core), deep) for block in got]
+    for apart, block in zip(order, sent):
+        got.append(lax.ppermute(block, "sites", [(i, i ^ (2 * apart)) for i in range(peers)]))
+    other = deep * (1 - core)
+    give = [spare] + [lax.dynamic_slice(block, (0, other, 0), (states, deep, LANES)) for block in got]
     take = lax.ppermute(jnp.stack(give), "sites", [(i, i ^ 1) for i in range(peers)])
-    return [cut(probs, deep * me, deep), *got, take], functools.partial(unpack_pairs, order=order)
+    return [own, *got, take], functools.partial(unpack_pairs, order=order)
 
 
 def total_over_sites(part):
@@ -318,7 +347,7 @@
     probs = by_tile(tip_probs)
     if 4 * each % 16 == 0:
         me = lax.axis_index("sites").astype(jnp.int32)
-        pieces, unpack = exchange_pairs(probs)
+        pieces, unpack = exchange_pairs(probs, me)
     else:
         me = jnp.zeros((), jnp.int32)
         pieces, unpack = exchange_plain(probs)

time: 52.5 us -> 50.8 us (0.968)
  local copies, waits for them, and re-layouts: 3.56 us -> 0.13 us
  Pallas kernels: 3.84 us -> 6.19 us
  starting transfers between devices: 25.4 us -> 24.4 us
    dynamic_slice x2 -> x0, local copies, waits for them, and re-layouts: 2.54 us -> none  [cut(): return lax.dynamic_slice(block, (0, first, 0), (states, count, LANES))]
    pallas_call x0 -> x2, Pallas kernels: none -> 2.34 us  [cut(): pl.pallas_call(functools.partial(cut_kernel, firsts=firsts), in_specs=[pl...]
    ppermute x1, waiting for transfers between devices: 1.18 us -> 2.08 us  [exchange_pairs(): lax.ppermute(jnp.stack(give), 'sites', [(i, i ^ 1) for i in range(peers)])]
    unnamed x15, local copies, waits for them, and re-layouts: 1.01 us -> 0.12 us
    ppermute x5, starting transfers between devices: 9.73 us -> 9.07 us  [total_over_sites(): lax.ppermute(part, 'sites', [(i, i ^ step) for i in range(peers)])]
    ppermute x5, waiting for transfers between devices: 4.88 us -> 4.28 us  [total_over_sites(): lax.ppermute(part, 'sites', [(i, i ^ step) for i in range(peers)])]
  transfers between devices with their start and end apart: 13 -> 13, of which waited for: 9 -> 10; matrix products, arithmetic and copies ran while one was open for 4% -> 0% of each run, Pallas kernels for 0% -> 3%
where the time goes in v4:
time: 50.8 us; the launch traced here: 50.6 us
  starting transfers between devices  24.4 us (48%)
  waiting for transfers between devices  18.6 us (37%)
  Pallas kernels  6.19 us (12%)
  between operations  0.75 us (1%)
  other arithmetic  0.54 us (1%)
    ppermute x7, starting transfers between devices, exchange_pairs(): lax.ppermute(block, 'sites', [(i, i ^ 2 * apart) for i in range(peers)])  15.2 us
    ppermute x7, waiting for transfers between devices, exchange_pairs(): lax.ppermute(block, 'sites', [(i, i ^ 2 * apart) for i in range(peers)])  12.3 us
    ppermute x5, starting transfers between devices, total_over_sites(): lax.ppermute(part, 'sites', [(i, i ^ step) for i in range(peers)])  9.07 us
    ppermute x5, waiting for transfers between devices, total_over_sites(): lax.ppermute(part, 'sites', [(i, i ^ step) for i in range(peers)])  4.28 us
    pallas_call x1, Pallas kernels, prune(): pl.pallas_call(functools.partial(prune_kernel, unpack=unpack, held=len(pi...  3.85 us
    pallas_call x2, Pallas kernels, cut(): pl.pallas_call(functools.partial(cut_kernel, firsts=firsts), in_specs=[pl...  2.34 us
    ppermute x1, waiting for transfers between devices, exchange_pairs(): lax.ppermute(jnp.stack(give), 'sites', [(i, i ^ 1) for i in range(peers)])  2.08 us
  transfers between devices with their start and end apart: 13, of which 10 were waited for; matrix products, arithmetic and copies ran while one was open for 0% of the time, Pallas kernels for 3%

profile of v4, /device:TPU:0, one launch (start us, length us, event | category | flops | bytes accessed | tf_op | source)
XLA Modules:
  0.0 50.6 jit_solution(709404198006353948)
XLA Ops:
  0.6 0.9 %cut.2.after_ref = bf16[20,32,128]{2,1,0:T(8,128)(2,1)S(1)} custom-call(s32[1]{0:T(128)} %bitcast.me_ref.after_ref, bf16[20,256,128]{2,1,0:T(8,128)(2,1)} %bitcast.34, s32[1]{0:T(128)} %bitcast.me_ref.after_ref), custom_call_target="tpu_custom_call" | custom-call | tf_op jit(solution)/shard_map/cut/pallas_call | solution.py:292
  1.6 0.0 copy-start
  1.6 0.0 copy-start.1
  1.6 0.0 copy-start.2
  1.6 0.0 copy-start.3
  1.6 4.1 %collective-permute-start = (bf16[20,32,128]{2,1,0:T(8,128)(2,1)S(1)}, bf16[20,32,128]{2,1,0:T(8,128)(2,1)S(1)}, u32[]{:S(2)}, u32[]{:S(2)}) collective-permute-start(bf16[20,32,128]{2,1,0:T(8,128)(2,1)S(1)} %cut.2.after_ref), channel_id=1, source_target_pairs={{0,8},{1,9},{2,10},{3,11},{4,12},{5,13},{6,14},{7,15},{8,0},{9,1},... | collective-permute-start | bytes 491528 | tf_op jit(solution)/shard_map/ppermute | solution.py:319
  5.7 1.4 %cut.3 = (bf16[20,32,128]{2,1,0:T(8,128)(2,1)S(1)}, bf16[20,32,128]{2,1,0:T(8,128)(2,1)S(1)}, bf16[20,32,128]{2,1,0:T(8,128)(2,1)S(1)}, bf16[20,32,128]{2,1,0:T(...) custom-call(s32[1]{0:T(128)} %bitcast.me_ref.after_ref, ...), custom_call_target="tpu_custom_call" | custom-call | tf_op jit(solution)/shard_map/cut/pallas_call | solution.py:292
  7.1 1.6 %collective-permute-start.1 = (bf16[20,32,128]{2,1,0:T(8,128)(2,1)S(1)}, bf16[20,32,128]{2,1,0:T(8,128)(2,1)S(1)}, u32[]{:S(2)}, u32[]{:S(2)}) collective-permute-start(bf16[20,32,128]{2,1,0:T(8,128)(2,1)S(1)} %get-tuple-element.11), channel_id=1, source_target_pairs={{0,4},{1,5},{2,6},{3,7},{4,0},{5,1},{6,2},{7,3},{8,12},{9,13},{10,... | collective-permute-start | bytes 491528 | tf_op jit(solution)/shard_map/ppermute | solution.py:319
  8.8 1.3 %collective-permute-start.2 = (bf16[20,32,128]{2,1,0:T(8,128)(2,1)S(1)}, bf16[20,32,128]{2,1,0:T(8,128)(2,1)S(1)}, u32[]{:S(2)}, u32[]{:S(2)}) collective-permute-start(bf16[20,32,128]{2,1,0:T(8,128)(2,1)S(1)} %get-tuple-element.12), channel_id=1, source_target_pairs={{0,10},{1,11},{2,8},{3,9},{4,14},{5,15},{6,12},{7,13},{8,2},{9,3},... | collective-permute-start | bytes 491528 | tf_op jit(solution)/shard_map/ppermute | solution.py:319
  10.1 0.1 collective-permute-start.3
  10.2 3.9 %collective-permute-start.4 = (bf16[20,32,128]{2,1,0:T(8,128)(2,1)S(1)}, bf16[20,32,128]{2,1,0:T(8,128)(2,1)S(1)}, u32[]{:S(2)}, u32[]{:S(2)}) collective-permute-start(bf16[20,32,128]{2,1,0:T(8,128)(2,1)S(1)} %get-tuple-element.14), channel_id=1, source_target_pairs={{0,12},{1,13},{2,14},{3,15},{4,8},{5,9},{6,10},{7,11},{8,4},{9,5},... | collective-permute-start | bytes 491528 | tf_op jit(solution)/shard_map/ppermute | solution.py:319
  14.1 1.1 %collective-permute-done.refs_4_ = bf16[20,32,128]{2,1,0:T(8,128)(2,1)S(1)} collective-permute-done((bf16[20,32,128]{2,1,0:T(8,128)(2,1)S(1)}, bf16[20,32,128]{2,1,0:T(8,128)(2,1)S(1)}, u32[]{:S(2)}, u32[]{:S(2)}) %collective-permute-start) | collective-permute-done | bytes 163872 | tf_op jit(solution)/shard_map/ppermute | solution.py:319
  15.2 3.5 %collective-permute-start.5 = (bf16[20,32,128]{2,1,0:T(8,128)(2,1)S(1)}, bf16[20,32,128]{2,1,0:T(8,128)(2,1)S(1)}, u32[]{:S(2)}, u32[]{:S(2)}) collective-permute-start(bf16[20,32,128]{2,1,0:T(8,128)(2,1)S(1)} %get-tuple-element.15), channel_id=1, source_target_pairs={{0,2},{1,3},{2,0},{3,1},{4,6},{5,7},{6,4},{7,5},{8,10},{9,11},{10,... | collective-permute-start | bytes 491528 | tf_op jit(solution)/shard_map/ppermute | solution.py:319
  18.7 0.0 collective-permute-done.1.refs_5_
  18.7 0.7 %collective-permute-start.6 = (bf16[20,32,128]{2,1,0:T(8,128)(2,1)S(1)}, bf16[20,32,128]{2,1,0:T(8,128)(2,1)S(1)}, u32[]{:S(2)}, u32[]{:S(2)}) collective-permute-start(bf16[20,32,128]{2,1,0:T(8,128)(2,1)S(1)} %get-tuple-element.16), channel_id=1, source_target_pairs={{0,14},{1,15},{2,12},{3,13},{4,10},{5,11},{6,8},{7,9},{8,6},{9,7},... | collective-permute-start | bytes 491528 | tf_op jit(solution)/shard_map/ppermute | solution.py:319
  19.4 3.4 %collective-permute-done.2.refs_6_ = bf16[20,32,128]{2,1,0:T(8,128)(2,1)S(1)} collective-permute-done((bf16[20,32,128]{2,1,0:T(8,128)(2,1)S(1)}, bf16[20,32,128]{2,1,0:T(8,128)(2,1)S(1)}, u32[]{:S(2)}, u32[]{:S(2)}) %collective-permute-start.2) | collective-permute-done | bytes 163872 | tf_op jit(solution)/shard_map/ppermute | solution.py:319
  22.8 1.2 %collective-permute-done.3.refs_7_ = bf16[20,32,128]{2,1,0:T(8,128)(2,1)S(1)} collective-permute-done((bf16[20,32,128]{2,1,0:T(8,128)(2,1)S(1)}, bf16[20,32,128]{2,1,0:T(8,128)(2,1)S(1)}, u32[]{:S(2)}, u32[]{:S(2)}) %collective-permute-start.3) | collective-permute-done | bytes 163872 | tf_op jit(solution)/shard_map/ppermute | solution.py:319
  24.1 3.2 %collective-permute-done.4.refs_8_ = bf16[20,32,128]{2,1,0:T(8,128)(2,1)S(1)} collective-permute-done((bf16[20,32,128]{2,1,0:T(8,128)(2,1)S(1)}, bf16[20,32,128]{2,1,0:T(8,128)(2,1)S(1)}, u32[]{:S(2)}, u32[]{:S(2)}) %collective-permute-start.4) | collective-permute-done | bytes 163872 | tf_op jit(solution)/shard_map/ppermute | solution.py:319
  27.3 0.0 collective-permute-done.5.refs_9_
  27.3 3.4 %collective-permute-done.6.refs_10_ = bf16[20,32,128]{2,1,0:T(8,128)(2,1)S(1)} collective-permute-done((bf16[20,32,128]{2,1,0:T(8,128)(2,1)S(1)}, bf16[20,32,128]{2,1,0:T(8,128)(2,1)S(1)}, u32[]{:S(2)}, u32[]{:S(2)}) %collective-permute-start.6) | collective-permute-done | bytes 163872 | tf_op jit(solution)/shard_map/ppermute | solution.py:319
  30.7 0.1 collective-permute-start.7
  30.8 2.1 %collective-permute-done.7.refs_11_ = bf16[8,20,16,128]{3,2,1,0:T(8,128)(2,1)S(1)} collective-permute-done((bf16[8,20,16,128]{3,2,1,0:T(8,128)(2,1)S(1)}, bf16[8,20,16,128]{3,2,1,0:T(8,128)(2,1)S(1)}, u32[]{:S(2)}, u32[]{:S(2)}) %collective-permute-start.7) | collective-permute-done | bytes 655392 | tf_op jit(solution)/shard_map/ppermute | solution.py:322
  32.9 0.0 copy-done
  32.9 0.0 copy-done.1
  32.9 0.0 copy-done.2
  32.9 0.0 copy-done.3
  32.9 3.8 %prune.1 = f32[8,128]{1,0:T(8,128)S(1)} custom-call(s32[64]{0:T(128)S(1)} %copy-done.1, s32[1]{0:T(128)} %bitcast.me_ref.after_ref, s32[1,512]{1,0:T(1,128)S(1)} %bitcast.31, f32[1,126]{1,0:T(1,128)S(1)} %bitcast.32, f32[1,126]{1,0:T(1,128)S(1)} %bitcast.33, bf16[20,16,128]{2,1,0:T(8,128)(2,1)S(1)} %get-tuple-element.10.refs_3_, ...), custom_call_target="tpu_custom_call" | custom-call | tf_op jit(solution)/shard_map/prune/pallas_call | solution.py:207
  36.7 0.2 collective-permute-start.8
  36.9 1.0 %collective-permute-done.8 = f32[8,128]{1,0:T(8,128)S(1)} collective-permute-done((f32[8,128]{1,0:T(8,128)S(1)}, f32[8,128]{1,0:T(8,128)S(1)}, u32[]{:S(2)}, u32[]{:S(2)}) %collective-permute-start.8) | collective-permute-done | bytes 4128 | tf_op jit(solution)/shard_map/ppermute | solution.py:337
  38.0 1.9 %collective-permute-start.11 = (f32[8,128]{1,0:T(8,128)S(1)}, f32[8,128]{1,0:T(8,128)S(1)}, u32[]{:S(2)}, u32[]{:S(2)}) collective-permute-start(f32[8,128]{1,0:T(8,128)S(1)} %add.32), channel_id=1, source_target_pairs={{0,15},{1,14},{2,13},{3,12},{4,11},{5,10},{6,9},{7,8},{8,7},{9,6},... | collective-permute-start | bytes 12296 | tf_op jit(solution)/shard_map/ppermute | solution.py:337
  39.8 1.6 %collective-permute-start.10 = (f32[8,128]{1,0:T(8,128)S(1)}, f32[8,128]{1,0:T(8,128)S(1)}, u32[]{:S(2)}, u32[]{:S(2)}) collective-permute-start(f32[8,128]{1,0:T(8,128)S(1)} %add.32), channel_id=1, source_target_pairs={{0,13},{1,12},{2,15},{3,14},{4,9},{5,8},{6,11},{7,10},{8,5},{9,4},... | collective-permute-start | bytes 12296 | tf_op jit(solution)/shard_map/ppermute | solution.py:337
  41.4 1.3 %collective-permute-start.9 = (f32[8,128]{1,0:T(8,128)S(1)}, f32[8,128]{1,0:T(8,128)S(1)}, u32[]{:S(2)}, u32[]{:S(2)}) collective-permute-start(f32[8,128]{1,0:T(8,128)S(1)} %add.32), channel_id=1, source_target_pairs={{0,3},{1,2},{2,1},{3,0},{4,7},{5,6},{6,5},{7,4},{8,11},{9,10},{10,... | collective-permute-start | bytes 12296 | tf_op jit(solution)/shard_map/ppermute | solution.py:337
  42.7 0.9 %collective-permute-done.11 = f32[8,128]{1,0:T(8,128)S(1)} collective-permute-done((f32[8,128]{1,0:T(8,128)S(1)}, f32[8,128]{1,0:T(8,128)S(1)}, u32[]{:S(2)}, u32[]{:S(2)}) %collective-permute-start.11) | collective-permute-done | bytes 4128 | tf_op jit(solution)/shard_map/ppermute | solution.py:337
  43.7 1.0 %collective-permute-done.10 = f32[8,128]{1,0:T(8,128)S(1)} collective-permute-done((f32[8,128]{1,0:T(8,128)S(1)}, f32[8,128]{1,0:T(8,128)S(1)}, u32[]{:S(2)}, u32[]{:S(2)}) %collective-permute-start.10) | collective-permute-done | bytes 4128 | tf_op jit(solution)/shard_map/ppermute | solution.py:337
  44.7 0.0 collective-permute-done.9
  44.7 4.1 %collective-permute-start.12 = (f32[8,128]{1,0:T(8,128)S(1)}, f32[8,128]{1,0:T(8,128)S(1)}, u32[]{:S(2)}, u32[]{:S(2)}) collective-permute-start(f32[8,128]{1,0:T(8,128)S(1)} %add_add_fusion), channel_id=1, source_target_pairs={{0,5},{1,4},{2,7},{3,6},{4,1},{5,0},{6,3},{7,2},{8,13},{9,12},{10,... | collective-permute-start | bytes 12296 | tf_op jit(solution)/shard_map/ppermute | solution.py:337
  48.8 1.3 %collective-permute-done.12 = f32[8,128]{1,0:T(8,128)S(1)} collective-permute-done((f32[8,128]{1,0:T(8,128)S(1)}, f32[8,128]{1,0:T(8,128)S(1)}, u32[]{:S(2)}, u32[]{:S(2)}) %collective-permute-start.12) | collective-permute-done | bytes 4128 | tf_op jit(solution)/shard_map/ppermute | solution.py:337
  50.1 0.5 %fusion = (f32[126]{0:T(128)}, f32[126]{0:T(128)}) fusion(f32[8,128]{1,0:T(8,128)S(1)} %add.36), kind=kLoop, calls=%fused_computation.12 | loop fusion | flops 378 | bytes 2520 | tf_op jit(solution)/shard_map/div | solution.py:356
  (11 shorter events, 0.1 us)
Async XLA Ops:
  1.6 31.3 %copy-start = (s32[512]{0:T(512)S(1)}, s32[512]{0:T(512)}, u32[]{:S(2)}) copy-start(s32[512]{0:T(512)} %param.7) | copy-start | bytes 6148
  1.6 31.3 %copy-start.1 = (s32[64]{0:T(128)S(1)}, s32[64]{0:T(128)}, u32[]{:S(2)}) copy-start(s32[64]{0:T(128)} %order_ref.1) | copy-start | bytes 772
  1.6 31.3 %copy-start.2 = (f32[126]{0:T(128)S(1)}, f32[126]{0:T(128)}, u32[]{:S(2)}) copy-start(f32[126]{0:T(128)} %param.8) | copy-start | bytes 1516
  1.6 31.3 %copy-start.3 = (f32[126]{0:T(128)S(1)}, f32[126]{0:T(128)}, u32[]{:S(2)}) copy-start(f32[126]{0:T(128)} %param.9) | copy-start | bytes 1516
  1.6 13.6 %collective-permute-start = (bf16[20,32,128]{2,1,0:T(8,128)(2,1)S(1)}, bf16[20,32,128]{2,1,0:T(8,128)(2,1)S(1)}, u32[]{:S(2)}, u32[]{:S(2)}) collective-permute-start(bf16[20,32,128]{2,1,0:T(8,128)(2,1)S(1)} %cut.2.after_ref), channel_id=1, source_target_pairs={{0,8},{1,9},{2,10},{3,11},{4,12},{5,13},{6,14},{7,15},{8,0},{9,1},... | collective-permute-start | bytes 491528 | tf_op jit(solution)/shard_map/ppermute | solution.py:319
  7.1 11.5 %collective-permute-start.1 = (bf16[20,32,128]{2,1,0:T(8,128)(2,1)S(1)}, bf16[20,32,128]{2,1,0:T(8,128)(2,1)S(1)}, u32[]{:S(2)}, u32[]{:S(2)}) collective-permute-start(bf16[20,32,128]{2,1,0:T(8,128)(2,1)S(1)} %get-tuple-element.11), channel_id=1, source_target_pairs={{0,4},{1,5},{2,6},{3,7},{4,0},{5,1},{6,2},{7,3},{8,12},{9,13},{10,... | collective-permute-start | bytes 491528 | tf_op jit(solution)/shard_map/ppermute | solution.py:319
  8.8 14.0 %collective-permute-start.2 = (bf16[20,32,128]{2,1,0:T(8,128)(2,1)S(1)}, bf16[20,32,128]{2,1,0:T(8,128)(2,1)S(1)}, u32[]{:S(2)}, u32[]{:S(2)}) collective-permute-start(bf16[20,32,128]{2,1,0:T(8,128)(2,1)S(1)} %get-tuple-element.12), channel_id=1, source_target_pairs={{0,10},{1,11},{2,8},{3,9},{4,14},{5,15},{6,12},{7,13},{8,2},{9,3},... | collective-permute-start | bytes 491528 | tf_op jit(solution)/shard_map/ppermute | solution.py:319
  10.1 14.0 %collective-permute-start.3 = (bf16[20,32,128]{2,1,0:T(8,128)(2,1)S(1)}, bf16[20,32,128]{2,1,0:T(8,128)(2,1)S(1)}, u32[]{:S(2)}, u32[]{:S(2)}) collective-permute-start(bf16[20,32,128]{2,1,0:T(8,128)(2,1)S(1)} %get-tuple-element.13), channel_id=1, source_target_pairs={{0,6},{1,7},{2,4},{3,5},{4,2},{5,3},{6,0},{7,1},{8,14},{9,15},{10,... | collective-permute-start | bytes 491528 | tf_op jit(solution)/shard_map/ppermute | solution.py:319
  10.2 17.1 %collective-permute-start.4 = (bf16[20,32,128]{2,1,0:T(8,128)(2,1)S(1)}, bf16[20,32,128]{2,1,0:T(8,128)(2,1)S(1)}, u32[]{:S(2)}, u32[]{:S(2)}) collective-permute-start(bf16[20,32,128]{2,1,0:T(8,128)(2,1)S(1)} %get-tuple-element.14), channel_id=1, source_target_pairs={{0,12},{1,13},{2,14},{3,15},{4,8},{5,9},{6,10},{7,11},{8,4},{9,5},... | collective-permute-start | bytes 491528 | tf_op jit(solution)/shard_map/ppermute | solution.py:319
  15.2 12.1 %collective-permute-start.5 = (bf16[20,32,128]{2,1,0:T(8,128)(2,1)S(1)}, bf16[20,32,128]{2,1,0:T(8,128)(2,1)S(1)}, u32[]{:S(2)}, u32[]{:S(2)}) collective-permute-start(bf16[20,32,128]{2,1,0:T(8,128)(2,1)S(1)} %get-tuple-element.15), channel_id=1, source_target_pairs={{0,2},{1,3},{2,0},{3,1},{4,6},{5,7},{6,4},{7,5},{8,10},{9,11},{10,... | collective-permute-start | bytes 491528 | tf_op jit(solution)/shard_map/ppermute | solution.py:319
  18.7 12.0 %collective-permute-start.6 = (bf16[20,32,128]{2,1,0:T(8,128)(2,1)S(1)}, bf16[20,32,128]{2,1,0:T(8,128)(2,1)S(1)}, u32[]{:S(2)}, u32[]{:S(2)}) collective-permute-start(bf16[20,32,128]{2,1,0:T(8,128)(2,1)S(1)} %get-tuple-element.16), channel_id=1, source_target_pairs={{0,14},{1,15},{2,12},{3,13},{4,10},{5,11},{6,8},{7,9},{8,6},{9,7},... | collective-permute-start | bytes 491528 | tf_op jit(solution)/shard_map/ppermute | solution.py:319
  30.7 2.2 %collective-permute-start.7 = (bf16[8,20,16,128]{3,2,1,0:T(8,128)(2,1)S(1)}, bf16[8,20,16,128]{3,2,1,0:T(8,128)(2,1)S(1)}, u32[]{:S(2)}, u32[]{:S(2)}) collective-permute-start(bf16[8,20,16,128]{3,2,1,0:T(8,128)(2,1)S(1)} %bitcast_dynamic-update-slice_fusion), channel_id=1, source_target_pairs={{0,1},{1,0},{2,3},{3,2},{4,5},{5,4},{6,7},{7,6},{8,9},{9,8},{10,11... | collective-permute-start | bytes 1966088 | tf_op jit(solution)/shard_map/ppermute | solution.py:322
  36.7 1.2 %collective-permute-start.8 = (f32[8,128]{1,0:T(8,128)S(1)}, f32[8,128]{1,0:T(8,128)S(1)}, u32[]{:S(2)}, u32[]{:S(2)}) collective-permute-start(f32[8,128]{1,0:T(8,128)S(1)} %prune.1), channel_id=1, source_target_pairs={{0,1},{1,0},{2,3},{3,2},{4,5},{5,4},{6,7},{7,6},{8,9},{9,8},{10,11... | collective-permute-start | bytes 12296 | tf_op jit(solution)/shard_map/ppermute | solution.py:337
  38.0 5.7 %collective-permute-start.11 = (f32[8,128]{1,0:T(8,128)S(1)}, f32[8,128]{1,0:T(8,128)S(1)}, u32[]{:S(2)}, u32[]{:S(2)}) collective-permute-start(f32[8,128]{1,0:T(8,128)S(1)} %add.32), channel_id=1, source_target_pairs={{0,15},{1,14},{2,13},{3,12},{4,11},{5,10},{6,9},{7,8},{8,7},{9,6},... | collective-permute-start | bytes 12296 | tf_op jit(solution)/shard_map/ppermute | solution.py:337
  39.8 4.8 %collective-permute-start.10 = (f32[8,128]{1,0:T(8,128)S(1)}, f32[8,128]{1,0:T(8,128)S(1)}, u32[]{:S(2)}, u32[]{:S(2)}) collective-permute-start(f32[8,128]{1,0:T(8,128)S(1)} %add.32), channel_id=1, source_target_pairs={{0,13},{1,12},{2,15},{3,14},{4,9},{5,8},{6,11},{7,10},{8,5},{9,4},... | collective-permute-start | bytes 12296 | tf_op jit(solution)/shard_map/ppermute | solution.py:337
  41.4 3.3 %collective-permute-start.9 = (f32[8,128]{1,0:T(8,128)S(1)}, f32[8,128]{1,0:T(8,128)S(1)}, u32[]{:S(2)}, u32[]{:S(2)}) collective-permute-start(f32[8,128]{1,0:T(8,128)S(1)} %add.32), channel_id=1, source_target_pairs={{0,3},{1,2},{2,1},{3,0},{4,7},{5,6},{6,5},{7,4},{8,11},{9,10},{10,... | collective-permute-start | bytes 12296 | tf_op jit(solution)/shard_map/ppermute | solution.py:337
  44.7 5.4 %collective-permute-start.12 = (f32[8,128]{1,0:T(8,128)S(1)}, f32[8,128]{1,0:T(8,128)S(1)}, u32[]{:S(2)}, u32[]{:S(2)}) collective-permute-start(f32[8,128]{1,0:T(8,128)S(1)} %add_add_fusion), channel_id=1, source_target_pairs={{0,5},{1,4},{2,7},{3,6},{4,1},{5,0},{6,3},{7,2},{8,13},{9,12},{10,... | collective-permute-start | bytes 12296 | tf_op jit(solution)/shard_map/ppermute | solution.py:337

commit v5 on v4

--- a/solution.py
+++ b/solution.py
@@ -244,7 +244,7 @@
 
 
 def unpack_pairs(piece_refs, wide_ref, me, rows, order):
-    own, *got, take = piece_refs
+    own, *got, take, take_last = piece_refs
     deep = own.shape[1]
     here = pl.ds(pl.multiple_of(lax.rem(me, 2) * deep, deep), deep)
 
@@ -255,7 +255,8 @@
     put(1, take[0])
     for number, (apart, block) in enumerate(zip(order, got), 1):
         put(2 * apart, block[:, here, :])
-        put(2 * apart + 1, take[number])
+        late = number - take.shape[0]
+        put(2 * apart + 1, take_last[late] if late >= 0 else take[number])
 
 
 def by_tile(tip_probs):
@@ -319,8 +320,10 @@
         got.append(lax.ppermute(block, "sites", [(i, i ^ (2 * apart)) for i in range(peers)]))
     other = deep * (1 - core)
     give = [spare] + [lax.dynamic_slice(block, (0, other, 0), (states, deep, LANES)) for block in got]
-    take = lax.ppermute(jnp.stack(give), "sites", [(i, i ^ 1) for i in range(peers)])
-    return [own, *got, take], functools.partial(unpack_pairs, order=order)
+    cores = [(i, i ^ 1) for i in range(peers)]
+    take = lax.ppermute(jnp.stack(give[:-2]), "sites", cores)
+    take_last = lax.ppermute(jnp.stack(give[-2:]), "sites", cores)
+    return [own, *got, take, take_last], functools.partial(unpack_pairs, order=order)
 
 
 def total_over_sites(part):
@@ -332,7 +335,7 @@
     rounds = [[1]]
     for first in range(0, len(steps), 2):
         pair = steps[first : first + 2]
-        rounds.append([step + 1 for step in ([*pair, pair[0] ^ pair[1]] if len(pair) > 1 else pair)])
+        rounds.append([step + 1 for step in ([pair[0], pair[0] ^ pair[1], pair[1]] if len(pair) > 1 else pair)])
     for apart in rounds:
         got = [lax.ppermute(part, "sites", [(i, i ^ step) for i in range(peers)]) for step in apart]
         part = part + got[0]

time: 50.8 us -> 50.1 us (0.986)
    ppermute x1 -> x2, waiting for transfers between devices: 2.08 us -> 1.38 us  [the longest x1 1.38 us: exchange_pairs(): take_last = lax.ppermute(jnp.stack(give[-2:]), 'sites', cores)]
    ppermute x5, starting transfers between devices: 9.07 us -> 8.5 us  [total_over_sites(): lax.ppermute(part, 'sites', [(i, i ^ step) for i in range(peers)])]
    ppermute x5, waiting for transfers between devices: 4.28 us -> 4.85 us  [total_over_sites(): lax.ppermute(part, 'sites', [(i, i ^ step) for i in range(peers)])]
  transfers between devices with their start and end apart: 13 -> 14, of which waited for: 10 -> 10; matrix products, arithmetic and copies ran while one was open for 0% -> 0% of each run, Pallas kernels for 3% -> 3%
where the time goes in v5:
time: 50.1 us; the launch traced here: 50 us
  starting transfers between devices  23.9 us (48%)
  waiting for transfers between devices  18.5 us (37%)
  Pallas kernels  6.18 us (12%)
  between operations  0.77 us (2%)
  other arithmetic  0.56 us (1%)
    ppermute x7, starting transfers between devices, exchange_pairs(): lax.ppermute(block, 'sites', [(i, i ^ 2 * apart) for i in range(peers)])  15.2 us
    ppermute x7, waiting for transfers between devices, exchange_pairs(): lax.ppermute(block, 'sites', [(i, i ^ 2 * apart) for i in range(peers)])  12.2 us
    ppermute x5, starting transfers between devices, total_over_sites(): lax.ppermute(part, 'sites', [(i, i ^ step) for i in range(peers)])  8.5 us
    ppermute x5, waiting for transfers between devices, total_over_sites(): lax.ppermute(part, 'sites', [(i, i ^ step) for i in range(peers)])  4.85 us
    pallas_call x1, Pallas kernels, prune(): pl.pallas_call(functools.partial(prune_kernel, unpack=unpack, held=len(pi...  3.84 us
    pallas_call x2, Pallas kernels, cut(): pl.pallas_call(functools.partial(cut_kernel, firsts=firsts), in_specs=[pl...  2.34 us
    ppermute x1, waiting for transfers between devices, exchange_pairs(): take_last = lax.ppermute(jnp.stack(give[-2:]), 'sites', cores)  1.38 us
  transfers between devices with their start and end apart: 14, of which 10 were waited for; matrix products, arithmetic and copies ran while one was open for 0% of the time, Pallas kernels for 3%

profile of v5, /device:TPU:0, one launch (start us, length us, event | category | flops | bytes accessed | tf_op | source)
XLA Modules:
  0.0 50.0 jit_solution(15535001674425662625)
XLA Ops:
  0.6 0.9 %cut.2.after_ref = bf16[20,32,128]{2,1,0:T(8,128)(2,1)S(1)} custom-call(s32[1]{0:T(128)} %bitcast.me_ref.after_ref, bf16[20,256,128]{2,1,0:T(8,128)(2,1)} %bitcast.34, s32[1]{0:T(128)} %bitcast.me_ref.after_ref), custom_call_target="tpu_custom_call" | custom-call | tf_op jit(solution)/shard_map/cut/pallas_call | solution.py:293
  1.6 0.0 copy-start
  1.6 0.0 copy-start.1
  1.6 0.0 copy-start.2
  1.6 0.0 copy-start.3
  1.6 4.1 %collective-permute-start = (bf16[20,32,128]{2,1,0:T(8,128)(2,1)S(1)}, bf16[20,32,128]{2,1,0:T(8,128)(2,1)S(1)}, u32[]{:S(2)}, u32[]{:S(2)}) collective-permute-start(bf16[20,32,128]{2,1,0:T(8,128)(2,1)S(1)} %cut.2.after_ref), channel_id=1, source_target_pairs={{0,8},{1,9},{2,10},{3,11},{4,12},{5,13},{6,14},{7,15},{8,0},{9,1},... | collective-permute-start | bytes 491528 | tf_op jit(solution)/shard_map/ppermute | solution.py:320
  5.7 1.4 %cut.3 = (bf16[20,32,128]{2,1,0:T(8,128)(2,1)S(1)}, bf16[20,32,128]{2,1,0:T(8,128)(2,1)S(1)}, bf16[20,32,128]{2,1,0:T(8,128)(2,1)S(1)}, bf16[20,32,128]{2,1,0:T(...) custom-call(s32[1]{0:T(128)} %bitcast.me_ref.after_ref, ...), custom_call_target="tpu_custom_call" | custom-call | tf_op jit(solution)/shard_map/cut/pallas_call | solution.py:293
  7.1 1.6 %collective-permute-start.1 = (bf16[20,32,128]{2,1,0:T(8,128)(2,1)S(1)}, bf16[20,32,128]{2,1,0:T(8,128)(2,1)S(1)}, u32[]{:S(2)}, u32[]{:S(2)}) collective-permute-start(bf16[20,32,128]{2,1,0:T(8,128)(2,1)S(1)} %get-tuple-element.11), channel_id=1, source_target_pairs={{0,4},{1,5},{2,6},{3,7},{4,0},{5,1},{6,2},{7,3},{8,12},{9,13},{10,... | collective-permute-start | bytes 491528 | tf_op jit(solution)/shard_map/ppermute | solution.py:320
  8.8 1.3 %collective-permute-start.2 = (bf16[20,32,128]{2,1,0:T(8,128)(2,1)S(1)}, bf16[20,32,128]{2,1,0:T(8,128)(2,1)S(1)}, u32[]{:S(2)}, u32[]{:S(2)}) collective-permute-start(bf16[20,32,128]{2,1,0:T(8,128)(2,1)S(1)} %get-tuple-element.12), channel_id=1, source_target_pairs={{0,10},{1,11},{2,8},{3,9},{4,14},{5,15},{6,12},{7,13},{8,2},{9,3},... | collective-permute-start | bytes 491528 | tf_op jit(solution)/shard_map/ppermute | solution.py:320
  10.1 0.1 collective-permute-start.3
  10.2 3.9 %collective-permute-start.4 = (bf16[20,32,128]{2,1,0:T(8,128)(2,1)S(1)}, bf16[20,32,128]{2,1,0:T(8,128)(2,1)S(1)}, u32[]{:S(2)}, u32[]{:S(2)}) collective-permute-start(bf16[20,32,128]{2,1,0:T(8,128)(2,1)S(1)} %get-tuple-element.14), channel_id=1, source_target_pairs={{0,12},{1,13},{2,14},{3,15},{4,8},{5,9},{6,10},{7,11},{8,4},{9,5},... | collective-permute-start | bytes 491528 | tf_op jit(solution)/shard_map/ppermute | solution.py:320
  14.1 1.1 %collective-permute-done.refs_4_ = bf16[20,32,128]{2,1,0:T(8,128)(2,1)S(1)} collective-permute-done((bf16[20,32,128]{2,1,0:T(8,128)(2,1)S(1)}, bf16[20,32,128]{2,1,0:T(8,128)(2,1)S(1)}, u32[]{:S(2)}, u32[]{:S(2)}) %collective-permute-start) | collective-permute-done | bytes 163872 | tf_op jit(solution)/shard_map/ppermute | solution.py:320
  15.2 3.5 %collective-permute-start.5 = (bf16[20,32,128]{2,1,0:T(8,128)(2,1)S(1)}, bf16[20,32,128]{2,1,0:T(8,128)(2,1)S(1)}, u32[]{:S(2)}, u32[]{:S(2)}) collective-permute-start(bf16[20,32,128]{2,1,0:T(8,128)(2,1)S(1)} %get-tuple-element.15), channel_id=1, source_target_pairs={{0,2},{1,3},{2,0},{3,1},{4,6},{5,7},{6,4},{7,5},{8,10},{9,11},{10,... | collective-permute-start | bytes 491528 | tf_op jit(solution)/shard_map/ppermute | solution.py:320
  18.7 0.0 collective-permute-done.1.refs_5_
  18.7 0.7 %collective-permute-start.6 = (bf16[20,32,128]{2,1,0:T(8,128)(2,1)S(1)}, bf16[20,32,128]{2,1,0:T(8,128)(2,1)S(1)}, u32[]{:S(2)}, u32[]{:S(2)}) collective-permute-start(bf16[20,32,128]{2,1,0:T(8,128)(2,1)S(1)} %get-tuple-element.16), channel_id=1, source_target_pairs={{0,14},{1,15},{2,12},{3,13},{4,10},{5,11},{6,8},{7,9},{8,6},{9,7},... | collective-permute-start | bytes 491528 | tf_op jit(solution)/shard_map/ppermute | solution.py:320
  19.4 3.4 %collective-permute-done.2.refs_6_ = bf16[20,32,128]{2,1,0:T(8,128)(2,1)S(1)} collective-permute-done((bf16[20,32,128]{2,1,0:T(8,128)(2,1)S(1)}, bf16[20,32,128]{2,1,0:T(8,128)(2,1)S(1)}, u32[]{:S(2)}, u32[]{:S(2)}) %collective-permute-start.2) | collective-permute-done | bytes 163872 | tf_op jit(solution)/shard_map/ppermute | solution.py:320
  22.8 1.2 %collective-permute-done.3.refs_7_ = bf16[20,32,128]{2,1,0:T(8,128)(2,1)S(1)} collective-permute-done((bf16[20,32,128]{2,1,0:T(8,128)(2,1)S(1)}, bf16[20,32,128]{2,1,0:T(8,128)(2,1)S(1)}, u32[]{:S(2)}, u32[]{:S(2)}) %collective-permute-start.3) | collective-permute-done | bytes 163872 | tf_op jit(solution)/shard_map/ppermute | solution.py:320
  24.1 3.2 %collective-permute-done.4.refs_8_ = bf16[20,32,128]{2,1,0:T(8,128)(2,1)S(1)} collective-permute-done((bf16[20,32,128]{2,1,0:T(8,128)(2,1)S(1)}, bf16[20,32,128]{2,1,0:T(8,128)(2,1)S(1)}, u32[]{:S(2)}, u32[]{:S(2)}) %collective-permute-start.4) | collective-permute-done | bytes 163872 | tf_op jit(solution)/shard_map/ppermute | solution.py:320
  27.3 0.1 collective-permute-start.7
  27.3 3.3 %collective-permute-done.6.refs_10_ = bf16[20,32,128]{2,1,0:T(8,128)(2,1)S(1)} collective-permute-done((bf16[20,32,128]{2,1,0:T(8,128)(2,1)S(1)}, bf16[20,32,128]{2,1,0:T(8,128)(2,1)S(1)}, u32[]{:S(2)}, u32[]{:S(2)}) %collective-permute-start.6) | collective-permute-done | bytes 163872 | tf_op jit(solution)/shard_map/ppermute | solution.py:320
  30.7 0.0 collective-permute-done.5.refs_9_
  30.7 0.1 collective-permute-start.8
  30.8 1.4 %collective-permute-done.8.refs_12_ = bf16[2,20,16,128]{3,2,1,0:T(8,128)(2,1)S(1)} collective-permute-done((bf16[2,20,16,128]{3,2,1,0:T(8,128)(2,1)S(1)}, bf16[2,20,16,128]{3,2,1,0:T(8,128)(2,1)S(1)}, u32[]{:S(2)}, u32[]{:S(2)}) %collective-permute-start.8) | collective-permute-done | bytes 163872 | tf_op jit(solution)/shard_map/ppermute | solution.py:325
  32.2 0.0 collective-permute-done.7.refs_11_
  32.2 0.0 copy-done
  32.2 0.0 copy-done.1
  32.2 0.0 copy-done.2
  32.2 0.0 copy-done.3
  32.2 3.8 %prune.1 = f32[8,128]{1,0:T(8,128)S(1)} custom-call(s32[64]{0:T(128)S(1)} %copy-done.1, s32[1]{0:T(128)} %bitcast.me_ref.after_ref, s32[1,512]{1,0:T(1,128)S(1)} %bitcast.31, f32[1,126]{1,0:T(1,128)S(1)} %bitcast.32, f32[1,126]{1,0:T(1,128)S(1)} %bitcast.33, bf16[20,16,128]{2,1,0:T(8,128)(2,1)S(1)} %get-tuple-element.10.refs_3_, ...), custom_call_target="tpu_custom_call" | custom-call | tf_op jit(solution)/shard_map/prune/pallas_call | solution.py:207
  36.1 0.2 collective-permute-start.9
  36.3 1.0 %collective-permute-done.9 = f32[8,128]{1,0:T(8,128)S(1)} collective-permute-done((f32[8,128]{1,0:T(8,128)S(1)}, f32[8,128]{1,0:T(8,128)S(1)}, u32[]{:S(2)}, u32[]{:S(2)}) %collective-permute-start.9) | collective-permute-done | bytes 4128 | tf_op jit(solution)/shard_map/ppermute | solution.py:340
  37.3 2.4 %collective-permute-start.11 = (f32[8,128]{1,0:T(8,128)S(1)}, f32[8,128]{1,0:T(8,128)S(1)}, u32[]{:S(2)}, u32[]{:S(2)}) collective-permute-start(f32[8,128]{1,0:T(8,128)S(1)} %add.32), channel_id=1, source_target_pairs={{0,15},{1,14},{2,13},{3,12},{4,11},{5,10},{6,9},{7,8},{8,7},{9,6},... | collective-permute-start | bytes 12296 | tf_op jit(solution)/shard_map/ppermute | solution.py:340
  39.7 1.0 %collective-permute-start.12 = (f32[8,128]{1,0:T(8,128)S(1)}, f32[8,128]{1,0:T(8,128)S(1)}, u32[]{:S(2)}, u32[]{:S(2)}) collective-permute-start(f32[8,128]{1,0:T(8,128)S(1)} %add.32), channel_id=1, source_target_pairs={{0,13},{1,12},{2,15},{3,14},{4,9},{5,8},{6,11},{7,10},{8,5},{9,4},... | collective-permute-start | bytes 12296 | tf_op jit(solution)/shard_map/ppermute | solution.py:340
  40.7 1.3 %collective-permute-start.10 = (f32[8,128]{1,0:T(8,128)S(1)}, f32[8,128]{1,0:T(8,128)S(1)}, u32[]{:S(2)}, u32[]{:S(2)}) collective-permute-start(f32[8,128]{1,0:T(8,128)S(1)} %add.32), channel_id=1, source_target_pairs={{0,3},{1,2},{2,1},{3,0},{4,7},{5,6},{6,5},{7,4},{8,11},{9,10},{10,... | collective-permute-start | bytes 12296 | tf_op jit(solution)/shard_map/ppermute | solution.py:340
  42.1 0.9 %collective-permute-done.11 = f32[8,128]{1,0:T(8,128)S(1)} collective-permute-done((f32[8,128]{1,0:T(8,128)S(1)}, f32[8,128]{1,0:T(8,128)S(1)}, u32[]{:S(2)}, u32[]{:S(2)}) %collective-permute-start.11) | collective-permute-done | bytes 4128 | tf_op jit(solution)/shard_map/ppermute | solution.py:340
  43.0 1.5 %collective-permute-done.12 = f32[8,128]{1,0:T(8,128)S(1)} collective-permute-done((f32[8,128]{1,0:T(8,128)S(1)}, f32[8,128]{1,0:T(8,128)S(1)}, u32[]{:S(2)}, u32[]{:S(2)}) %collective-permute-start.12) | collective-permute-done | bytes 4128 | tf_op jit(solution)/shard_map/ppermute | solution.py:340
  44.6 0.0 collective-permute-done.10
  44.6 3.5 %collective-permute-start.13 = (f32[8,128]{1,0:T(8,128)S(1)}, f32[8,128]{1,0:T(8,128)S(1)}, u32[]{:S(2)}, u32[]{:S(2)}) collective-permute-start(f32[8,128]{1,0:T(8,128)S(1)} %add_add_fusion), channel_id=1, source_target_pairs={{0,5},{1,4},{2,7},{3,6},{4,1},{5,0},{6,3},{7,2},{8,13},{9,12},{10,... | collective-permute-start | bytes 12296 | tf_op jit(solution)/shard_map/ppermute | solution.py:340
  48.1 1.3 %collective-permute-done.13 = f32[8,128]{1,0:T(8,128)S(1)} collective-permute-done((f32[8,128]{1,0:T(8,128)S(1)}, f32[8,128]{1,0:T(8,128)S(1)}, u32[]{:S(2)}, u32[]{:S(2)}) %collective-permute-start.13) | collective-permute-done | bytes 4128 | tf_op jit(solution)/shard_map/ppermute | solution.py:340
  49.4 0.5 %fusion = (f32[126]{0:T(128)}, f32[126]{0:T(128)}) fusion(f32[8,128]{1,0:T(8,128)S(1)} %add.36), kind=kLoop, calls=%fused_computation.13 | loop fusion | flops 378 | bytes 2520 | tf_op jit(solution)/shard_map/div | solution.py:359
  (12 shorter events, 0.1 us)
Async XLA Ops:
  1.6 30.6 %copy-start = (s32[512]{0:T(512)S(1)}, s32[512]{0:T(512)}, u32[]{:S(2)}) copy-start(s32[512]{0:T(512)} %param.7) | copy-start | bytes 6148
  1.6 30.6 %copy-start.1 = (s32[64]{0:T(128)S(1)}, s32[64]{0:T(128)}, u32[]{:S(2)}) copy-start(s32[64]{0:T(128)} %order_ref.1) | copy-start | bytes 772
  1.6 30.6 %copy-start.2 = (f32[126]{0:T(128)S(1)}, f32[126]{0:T(128)}, u32[]{:S(2)}) copy-start(f32[126]{0:T(128)} %param.8) | copy-start | bytes 1516
  1.6 30.6 %copy-start.3 = (f32[126]{0:T(128)S(1)}, f32[126]{0:T(128)}, u32[]{:S(2)}) copy-start(f32[126]{0:T(128)} %param.9) | copy-start | bytes 1516
  1.6 13.6 %collective-permute-start = (bf16[20,32,128]{2,1,0:T(8,128)(2,1)S(1)}, bf16[20,32,128]{2,1,0:T(8,128)(2,1)S(1)}, u32[]{:S(2)}, u32[]{:S(2)}) collective-permute-start(bf16[20,32,128]{2,1,0:T(8,128)(2,1)S(1)} %cut.2.after_ref), channel_id=1, source_target_pairs={{0,8},{1,9},{2,10},{3,11},{4,12},{5,13},{6,14},{7,15},{8,0},{9,1},... | collective-permute-start | bytes 491528 | tf_op jit(solution)/shard_map/ppermute | solution.py:320
  7.1 11.5 %collective-permute-start.1 = (bf16[20,32,128]{2,1,0:T(8,128)(2,1)S(1)}, bf16[20,32,128]{2,1,0:T(8,128)(2,1)S(1)}, u32[]{:S(2)}, u32[]{:S(2)}) collective-permute-start(bf16[20,32,128]{2,1,0:T(8,128)(2,1)S(1)} %get-tuple-element.11), channel_id=1, source_target_pairs={{0,4},{1,5},{2,6},{3,7},{4,0},{5,1},{6,2},{7,3},{8,12},{9,13},{10,... | collective-permute-start | bytes 491528 | tf_op jit(solution)/shard_map/ppermute | solution.py:320
  8.8 14.0 %collective-permute-start.2 = (bf16[20,32,128]{2,1,0:T(8,128)(2,1)S(1)}, bf16[20,32,128]{2,1,0:T(8,128)(2,1)S(1)}, u32[]{:S(2)}, u32[]{:S(2)}) collective-permute-start(bf16[20,32,128]{2,1,0:T(8,128)(2,1)S(1)} %get-tuple-element.12), channel_id=1, source_target_pairs={{0,10},{1,11},{2,8},{3,9},{4,14},{5,15},{6,12},{7,13},{8,2},{9,3},... | collective-permute-start | bytes 491528 | tf_op jit(solution)/shard_map/ppermute | solution.py:320
  10.1 14.0 %collective-permute-start.3 = (bf16[20,32,128]{2,1,0:T(8,128)(2,1)S(1)}, bf16[20,32,128]{2,1,0:T(8,128)(2,1)S(1)}, u32[]{:S(2)}, u32[]{:S(2)}) collective-permute-start(bf16[20,32,128]{2,1,0:T(8,128)(2,1)S(1)} %get-tuple-element.13), channel_id=1, source_target_pairs={{0,6},{1,7},{2,4},{3,5},{4,2},{5,3},{6,0},{7,1},{8,14},{9,15},{10,... | collective-permute-start | bytes 491528 | tf_op jit(solution)/shard_map/ppermute | solution.py:320
  10.2 17.1 %collective-permute-start.4 = (bf16[20,32,128]{2,1,0:T(8,128)(2,1)S(1)}, bf16[20,32,128]{2,1,0:T(8,128)(2,1)S(1)}, u32[]{:S(2)}, u32[]{:S(2)}) collective-permute-start(bf16[20,32,128]{2,1,0:T(8,128)(2,1)S(1)} %get-tuple-element.14), channel_id=1, source_target_pairs={{0,12},{1,13},{2,14},{3,15},{4,8},{5,9},{6,10},{7,11},{8,4},{9,5},... | collective-permute-start | bytes 491528 | tf_op jit(solution)/shard_map/ppermute | solution.py:320
  15.2 15.5 %collective-permute-start.5 = (bf16[20,32,128]{2,1,0:T(8,128)(2,1)S(1)}, bf16[20,32,128]{2,1,0:T(8,128)(2,1)S(1)}, u32[]{:S(2)}, u32[]{:S(2)}) collective-permute-start(bf16[20,32,128]{2,1,0:T(8,128)(2,1)S(1)} %get-tuple-element.15), channel_id=1, source_target_pairs={{0,2},{1,3},{2,0},{3,1},{4,6},{5,7},{6,4},{7,5},{8,10},{9,11},{10,... | collective-permute-start | bytes 491528 | tf_op jit(solution)/shard_map/ppermute | solution.py:320
  18.7 12.0 %collective-permute-start.6 = (bf16[20,32,128]{2,1,0:T(8,128)(2,1)S(1)}, bf16[20,32,128]{2,1,0:T(8,128)(2,1)S(1)}, u32[]{:S(2)}, u32[]{:S(2)}) collective-permute-start(bf16[20,32,128]{2,1,0:T(8,128)(2,1)S(1)} %get-tuple-element.16), channel_id=1, source_target_pairs={{0,14},{1,15},{2,12},{3,13},{4,10},{5,11},{6,8},{7,9},{8,6},{9,7},... | collective-permute-start | bytes 491528 | tf_op jit(solution)/shard_map/ppermute | solution.py:320
  27.3 4.9 %collective-permute-start.7 = (bf16[6,20,16,128]{3,2,1,0:T(8,128)(2,1)S(1)}, bf16[6,20,16,128]{3,2,1,0:T(8,128)(2,1)S(1)}, u32[]{:S(2)}, u32[]{:S(2)}) collective-permute-start(bf16[6,20,16,128]{3,2,1,0:T(8,128)(2,1)S(1)} %bitcast_dynamic-update-slice_fusion), channel_id=1, source_target_pairs={{0,1},{1,0},{2,3},{3,2},{4,5},{5,4},{6,7},{7,6},{8,9},{9,8},{10,11... | collective-permute-start | bytes 1474568 | tf_op jit(solution)/shard_map/ppermute | solution.py:324
  30.7 1.5 %collective-permute-start.8 = (bf16[2,20,16,128]{3,2,1,0:T(8,128)(2,1)S(1)}, bf16[2,20,16,128]{3,2,1,0:T(8,128)(2,1)S(1)}, u32[]{:S(2)}, u32[]{:S(2)}) collective-permute-start(bf16[2,20,16,128]{3,2,1,0:T(8,128)(2,1)S(1)} %pad_maximum_fusion), channel_id=1, source_target_pairs={{0,1},{1,0},{2,3},{3,2},{4,5},{5,4},{6,7},{7,6},{8,9},{9,8},{10,11... | collective-permute-start | bytes 491528 | tf_op jit(solution)/shard_map/ppermute | solution.py:325
  36.1 1.2 %collective-permute-start.9 = (f32[8,128]{1,0:T(8,128)S(1)}, f32[8,128]{1,0:T(8,128)S(1)}, u32[]{:S(2)}, u32[]{:S(2)}) collective-permute-start(f32[8,128]{1,0:T(8,128)S(1)} %prune.1), channel_id=1, source_target_pairs={{0,1},{1,0},{2,3},{3,2},{4,5},{5,4},{6,7},{7,6},{8,9},{9,8},{10,11... | collective-permute-start | bytes 12296 | tf_op jit(solution)/shard_map/ppermute | solution.py:340
  37.3 5.7 %collective-permute-start.11 = (f32[8,128]{1,0:T(8,128)S(1)}, f32[8,128]{1,0:T(8,128)S(1)}, u32[]{:S(2)}, u32[]{:S(2)}) collective-permute-start(f32[8,128]{1,0:T(8,128)S(1)} %add.32), channel_id=1, source_target_pairs={{0,15},{1,14},{2,13},{3,12},{4,11},{5,10},{6,9},{7,8},{8,7},{9,6},... | collective-permute-start | bytes 12296 | tf_op jit(solution)/shard_map/ppermute | solution.py:340
  39.7 4.8 %collective-permute-start.12 = (f32[8,128]{1,0:T(8,128)S(1)}, f32[8,128]{1,0:T(8,128)S(1)}, u32[]{:S(2)}, u32[]{:S(2)}) collective-permute-start(f32[8,128]{1,0:T(8,128)S(1)} %add.32), channel_id=1, source_target_pairs={{0,13},{1,12},{2,15},{3,14},{4,9},{5,8},{6,11},{7,10},{8,5},{9,4},... | collective-permute-start | bytes 12296 | tf_op jit(solution)/shard_map/ppermute | solution.py:340
  40.7 3.8 %collective-permute-start.10 = (f32[8,128]{1,0:T(8,128)S(1)}, f32[8,128]{1,0:T(8,128)S(1)}, u32[]{:S(2)}, u32[]{:S(2)}) collective-permute-start(f32[8,128]{1,0:T(8,128)S(1)} %add.32), channel_id=1, source_target_pairs={{0,3},{1,2},{2,1},{3,0},{4,7},{5,6},{6,5},{7,4},{8,11},{9,10},{10,... | collective-permute-start | bytes 12296 | tf_op jit(solution)/shard_map/ppermute | solution.py:340
  44.6 4.8 %collective-permute-start.13 = (f32[8,128]{1,0:T(8,128)S(1)}, f32[8,128]{1,0:T(8,128)S(1)}, u32[]{:S(2)}, u32[]{:S(2)}) collective-permute-start(f32[8,128]{1,0:T(8,128)S(1)} %add_add_fusion), channel_id=1, source_target_pairs={{0,5},{1,4},{2,7},{3,6},{4,1},{5,0},{6,3},{7,2},{8,13},{9,12},{10,... | collective-permute-start | bytes 12296 | tf_op jit(solution)/shard_map/ppermute | solution.py:340

commit v6 on v4

--- a/solution.py
+++ b/solution.py
@@ -243,8 +243,8 @@
         wide_ref[number * rows : (number + 1) * rows, :] = pieces[number].astype(F32)
 
 
-def unpack_pairs(piece_refs, wide_ref, me, rows, order):
-    own, *got, take = piece_refs
+def unpack_pairs(piece_refs, wide_ref, me, rows, early, late):
+    own, first, *refs = piece_refs
     deep = own.shape[1]
     here = pl.ds(pl.multiple_of(lax.rem(me, 2) * deep, deep), deep)
 
@@ -252,10 +252,16 @@
         wide_ref[number * rows : (number + 1) * rows, :] = block.astype(F32).reshape(rows, LANES)
 
     put(0, own[...])
-    put(1, take[0])
-    for number, (apart, block) in enumerate(zip(order, got), 1):
+    put(1, first[0])
+    both_refs, late_refs, swapped_refs = refs[: len(early)], refs[len(early) :][: len(late)], refs[len(early) + len(late) :]
+    for apart, block in zip(early, both_refs):
         put(2 * apart, block[:, here, :])
-        put(2 * apart + 1, take[number])
+    for apart, block in zip(late, late_refs):
+        put(2 * apart, block[0])
+        put(2 * apart + 1, block[1])
+    for number, apart in enumerate(early):
+        block = swapped_refs[number // 2]
+        put(2 * apart + 1, block[number % 2])
 
 
 def by_tile(tip_probs):
@@ -277,10 +283,12 @@
     out_refs, sems = refs[:-1], refs[-1]
     me = me_ref[0]
     copies = []
-    for number, (out_ref, first) in enumerate(zip(out_refs, firsts)):
-        count = out_ref.shape[1]
-        start = pl.multiple_of(first(me), count)
-        copies.append(pltpu.make_async_copy(probs_ref.at[:, pl.ds(start, count), :], out_ref, sems.at[number]))
+    for out_ref, places in zip(out_refs, firsts):
+        for slot, first in enumerate(places):
+            count = out_ref.shape[2]
+            start = pl.multiple_of(first(me), count)
+            source = probs_ref.at[:, pl.ds(start, count), :]
+            copies.append(pltpu.make_async_copy(source, out_ref.at[slot], sems.at[len(copies)]))
     for copy in copies:
         copy.start()
     for copy in copies:
@@ -289,12 +297,20 @@
 
 def cut(probs, me, firsts, counts, after):
     vm = pl.BlockSpec(memory_space=pltpu.VMEM)
+    states = probs.shape[0]
     return pl.pallas_call(
         functools.partial(cut_kernel, firsts=firsts),
-        in_specs=[pl.BlockSpec(memory_space=pltpu.SMEM), pl.BlockSpec(memory_space=pltpu.HBM), pl.BlockSpec(memory_space=pl.ANY)],
+        in_specs=[
+            pl.BlockSpec(memory_space=pltpu.SMEM),
+            pl.BlockSpec(memory_space=pltpu.HBM),
+            pl.BlockSpec(memory_space=pl.ANY),
+        ],
         out_specs=[vm] * len(counts),
-        out_shape=[jax.ShapeDtypeStruct((probs.shape[0], count, LANES), probs.dtype) for count in counts],
-        scratch_shapes=[pltpu.SemaphoreType.DMA((len(counts),))],
+        out_shape=[
+            jax.ShapeDtypeStruct((len(places), states, count, LANES), probs.dtype)
+            for places, count in zip(firsts, counts)
+        ],
+        scratch_shapes=[pltpu.SemaphoreType.DMA((sum(len(places) for places in firsts),))],
         compiler_params=pltpu.CompilerParams(vmem_limit_bytes=16 * 1024 * 1024),
         name="cut",
     )(me.reshape(1), pltpu.with_memory_space_constraint(probs, pltpu.HBM), after)
@@ -308,19 +324,36 @@
     deep = rows // peers
     far, near = range(chips // 2, chips), [*range(2, chips // 2), 1]
     order = [far[0], *(apart for pair in zip(near, far[1:]) for apart in pair)]
-    firsts = [lambda me, apart=apart: (((me // 2) ^ apart) * (2 * deep)) for apart in order]
-    firsts += [lambda me: me * deep, lambda me: (me ^ 1) * deep]
-    counts = [2 * deep] * len(order) + [deep] * 2
+    early, late = order[:-1], order[-1:]
+
+    def chip_first(apart):
+        return lambda me: ((me // 2) ^ apart) * (2 * deep)
+
+    def core_first(step):
+        return lambda me: (me ^ step) * deep
+
+    firsts = [[chip_first(apart)] for apart in early]
+    counts = [2 * deep] * len(early)
     head = cut(probs, me, firsts[:1], counts[:1], me.reshape(1))
-    *tail, own, spare = cut(probs, me, firsts[1:], counts[1:], head[0])
-    sent = [*head, *tail]
-    got = []
-    for apart, block in zip(order, sent):
-        got.append(lax.ppermute(block, "sites", [(i, i ^ (2 * apart)) for i in range(peers)]))
+    firsts += [[core_first(1), *(core_first(2 * apart + 1) for apart in late)]]
+    firsts += [[core_first(2 * apart)] for apart in late]
+    firsts += [[core_first(0)]]
+    counts += [deep] * (len(late) + 2)
+    tail = cut(probs, me, firsts[1:], counts[1:], head[0])
+    sent = [*head, *tail[: len(early) - 1]]
+    give, *mine, own = tail[len(early) - 1 :]
+
+    def swap(block, step):
+        return lax.ppermute(block, "sites", [(i, i ^ step) for i in range(peers)])
+
+    first = swap(give, 1)
+    got = [swap(block[0], 2 * apart) for apart, block in zip(early, sent)]
+    for number, apart in enumerate(late):
+        got.append(swap(jnp.concatenate([mine[number], first[number + 1 : number + 2]], axis=0), 2 * apart))
     other = deep * (1 - core)
-    give = [spare] + [lax.dynamic_slice(block, (0, other, 0), (states, deep, LANES)) for block in got]
-    take = lax.ppermute(jnp.stack(give), "sites", [(i, i ^ 1) for i in range(peers)])
-    return [own, *got, take], functools.partial(unpack_pairs, order=order)
+    give = [lax.dynamic_slice(block, (0, other, 0), (states, deep, LANES)) for block in got[: len(early)]]
+    swapped = [swap(jnp.stack(give[at : at + 2]), 1) for at in range(0, len(give), 2)]
+    return [own[0], first, *got, *swapped], functools.partial(unpack_pairs, early=early, late=late)
 
 
 def total_over_sites(part):

time: 50.8 us -> 49.1 us (0.967)
  starting transfers between devices: 24.4 us -> 21.3 us
  waiting for transfers between devices: 18.6 us -> 19.9 us
    ppermute x5, starting transfers between devices: 9.07 us -> 6.67 us  [total_over_sites(): lax.ppermute(part, 'sites', [(i, i ^ step) for i in range(peers)])]
    ppermute x8 -> x11, waiting for transfers between devices: 14.3 us -> 15.1 us  [swap(): return lax.ppermute(block, 'sites', [(i, i ^ step) for i in range(peers)])]
    ppermute x8 -> x11, starting transfers between devices: 15.3 us -> 14.7 us  [swap(): return lax.ppermute(block, 'sites', [(i, i ^ step) for i in range(peers)])]
    ppermute x5, waiting for transfers between devices: 4.28 us -> 4.79 us  [total_over_sites(): lax.ppermute(part, 'sites', [(i, i ^ step) for i in range(peers)])]
  transfers between devices with their start and end apart: 13 -> 16, of which waited for: 10 -> 9; matrix products, arithmetic and copies ran while one was open for 0% -> 0% of each run, Pallas kernels for 3% -> 3%
where the time goes in v6:
time: 49.1 us; the launch traced here: 48.9 us
  starting transfers between devices  21.3 us (43%)
  waiting for transfers between devices  19.9 us (41%)
  Pallas kernels  6.2 us (13%)
  between operations  0.78 us (2%)
  other arithmetic  0.61 us (1%)
    ppermute x11, waiting for transfers between devices, swap(): return lax.ppermute(block, 'sites', [(i, i ^ step) for i in range(peers)])  15.1 us
    ppermute x11, starting transfers between devices, swap(): return lax.ppermute(block, 'sites', [(i, i ^ step) for i in range(peers)])  14.7 us
    ppermute x5, starting transfers between devices, total_over_sites(): lax.ppermute(part, 'sites', [(i, i ^ step) for i in range(peers)])  6.67 us
    ppermute x5, waiting for transfers between devices, total_over_sites(): lax.ppermute(part, 'sites', [(i, i ^ step) for i in range(peers)])  4.79 us
    pallas_call x1, Pallas kernels, prune(): pl.pallas_call(functools.partial(prune_kernel, unpack=unpack, held=len(pi...  3.85 us
    pallas_call x2, Pallas kernels, cut(): pl.pallas_call(functools.partial(cut_kernel, firsts=firsts), in_specs=[pl...  2.35 us
  transfers between devices with their start and end apart: 16, of which 9 were waited for; matrix products, arithmetic and copies ran while one was open for 0% of the time, Pallas kernels for 3%

profile of v6, /device:TPU:0, one launch (start us, length us, event | category | flops | bytes accessed | tf_op | source)
XLA Modules:
  0.0 48.9 jit_solution(16500493981998911140)
XLA Ops:
  0.6 0.9 %cut.2.after_ref = bf16[1,20,32,128]{3,2,1,0:T(8,128)(2,1)S(1)} custom-call(s32[1]{0:T(128)} %bitcast.me_ref.after_ref, bf16[20,256,128]{2,1,0:T(8,128)(2,1)} %bitcast.44, s32[1]{0:T(128)} %bitcast.me_ref.after_ref), custom_call_target="tpu_custom_call" | custom-call | tf_op jit(solution)/shard_map/cut/pallas_call | solution.py:301
  1.6 4.1 %collective-permute-start.1 = (bf16[20,32,128]{2,1,0:T(8,128)(2,1)S(1)}, bf16[20,32,128]{2,1,0:T(8,128)(2,1)S(1)}, u32[]{:S(2)}, u32[]{:S(2)}) collective-permute-start(bf16[20,32,128]{2,1,0:T(8,128)(2,1)S(1)} %bitcast.34), channel_id=1, source_target_pairs={{0,8},{1,9},{2,10},{3,11},{4,12},{5,13},{6,14},{7,15},{8,0},{9,1},... | collective-permute-start | bytes 491528 | tf_op jit(solution)/shard_map/ppermute | solution.py:347
  5.7 1.4 %cut.3 = (bf16[1,20,32,128]{3,2,1,0:T(8,128)(2,1)S(1)}, bf16[1,20,32,128]{3,2,1,0:T(8,128)(2,1)S(1)}, bf16[1,20,32,128]{3,2,1,0:T(8,128)(2,1)S(1)}, bf16[1,20,32...) custom-call(s32[1]{0:T(128)} %bitcast.me_ref.after_ref, ...), custom_call_target="tpu_custom_call" | custom-call | tf_op jit(solution)/shard_map/cut/pallas_call | solution.py:301
  7.1 0.0 copy-start
  7.1 0.0 copy-start.1
  7.1 0.0 copy-start.2
  7.1 0.0 copy-start.3
  7.2 0.1 collective-permute-start
  7.2 1.6 %collective-permute-start.2 = (bf16[20,32,128]{2,1,0:T(8,128)(2,1)S(1)}, bf16[20,32,128]{2,1,0:T(8,128)(2,1)S(1)}, u32[]{:S(2)}, u32[]{:S(2)}) collective-permute-start(bf16[20,32,128]{2,1,0:T(8,128)(2,1)S(1)} %bitcast.43), channel_id=1, source_target_pairs={{0,4},{1,5},{2,6},{3,7},{4,0},{5,1},{6,2},{7,3},{8,12},{9,13},{10,... | collective-permute-start | bytes 491528 | tf_op jit(solution)/shard_map/ppermute | solution.py:347
  8.9 1.3 %collective-permute-start.3 = (bf16[20,32,128]{2,1,0:T(8,128)(2,1)S(1)}, bf16[20,32,128]{2,1,0:T(8,128)(2,1)S(1)}, u32[]{:S(2)}, u32[]{:S(2)}) collective-permute-start(bf16[20,32,128]{2,1,0:T(8,128)(2,1)S(1)} %bitcast.42), channel_id=1, source_target_pairs={{0,10},{1,11},{2,8},{3,9},{4,14},{5,15},{6,12},{7,13},{8,2},{9,3},... | collective-permute-start | bytes 491528 | tf_op jit(solution)/shard_map/ppermute | solution.py:347
  10.2 0.1 collective-permute-start.4
  10.3 3.2 %collective-permute-done.1.refs_5_ = bf16[20,32,128]{2,1,0:T(8,128)(2,1)S(1)} collective-permute-done((bf16[20,32,128]{2,1,0:T(8,128)(2,1)S(1)}, bf16[20,32,128]{2,1,0:T(8,128)(2,1)S(1)}, u32[]{:S(2)}, u32[]{:S(2)}) %collective-permute-start.1) | collective-permute-done | bytes 163872 | tf_op jit(solution)/shard_map/ppermute | solution.py:347
  13.5 3.9 %collective-permute-start.5 = (bf16[20,32,128]{2,1,0:T(8,128)(2,1)S(1)}, bf16[20,32,128]{2,1,0:T(8,128)(2,1)S(1)}, u32[]{:S(2)}, u32[]{:S(2)}) collective-permute-start(bf16[20,32,128]{2,1,0:T(8,128)(2,1)S(1)} %bitcast.40), channel_id=1, source_target_pairs={{0,12},{1,13},{2,14},{3,15},{4,8},{5,9},{6,10},{7,11},{8,4},{9,5},... | collective-permute-start | bytes 491528 | tf_op jit(solution)/shard_map/ppermute | solution.py:347
  17.4 0.0 collective-permute-done.refs_4_
  17.4 1.6 %collective-permute-start.6 = (bf16[20,32,128]{2,1,0:T(8,128)(2,1)S(1)}, bf16[20,32,128]{2,1,0:T(8,128)(2,1)S(1)}, u32[]{:S(2)}, u32[]{:S(2)}) collective-permute-start(bf16[20,32,128]{2,1,0:T(8,128)(2,1)S(1)} %bitcast.39), channel_id=1, source_target_pairs={{0,2},{1,3},{2,0},{3,1},{4,6},{5,7},{6,4},{7,5},{8,10},{9,11},{10,... | collective-permute-start | bytes 491528 | tf_op jit(solution)/shard_map/ppermute | solution.py:347
  19.0 0.0 collective-permute-done.2.refs_6_
  19.0 1.4 %collective-permute-start.7 = (bf16[2,20,16,128]{3,2,1,0:T(8,128)(2,1)S(1)}, bf16[2,20,16,128]{3,2,1,0:T(8,128)(2,1)S(1)}, u32[]{:S(2)}, u32[]{:S(2)}) collective-permute-start(bf16[2,20,16,128]{3,2,1,0:T(8,128)(2,1)S(1)} %pad_maximum_fusion), channel_id=1, source_target_pairs={{0,14},{1,15},{2,12},{3,13},{4,10},{5,11},{6,8},{7,9},{8,6},{9,7},... | collective-permute-start | bytes 491528 | tf_op jit(solution)/shard_map/ppermute | solution.py:347
  20.4 2.0 %collective-permute-done.3.refs_7_ = bf16[20,32,128]{2,1,0:T(8,128)(2,1)S(1)} collective-permute-done((bf16[20,32,128]{2,1,0:T(8,128)(2,1)S(1)}, bf16[20,32,128]{2,1,0:T(8,128)(2,1)S(1)}, u32[]{:S(2)}, u32[]{:S(2)}) %collective-permute-start.3) | collective-permute-done | bytes 163872 | tf_op jit(solution)/shard_map/ppermute | solution.py:347
  22.4 0.0 collective-permute-start.8
  22.4 8.8 %collective-permute-done.4.refs_8_ = bf16[20,32,128]{2,1,0:T(8,128)(2,1)S(1)} collective-permute-done((bf16[20,32,128]{2,1,0:T(8,128)(2,1)S(1)}, bf16[20,32,128]{2,1,0:T(8,128)(2,1)S(1)}, u32[]{:S(2)}, u32[]{:S(2)}) %collective-permute-start.4) | collective-permute-done | bytes 163872 | tf_op jit(solution)/shard_map/ppermute | solution.py:347
  31.3 0.1 collective-permute-start.9
  31.4 0.0 collective-permute-done.5.refs_9_
  31.4 0.0 collective-permute-done.6.refs_10_
  31.5 0.5 %collective-permute-start.10 = (bf16[2,20,16,128]{3,2,1,0:T(8,128)(2,1)S(1)}, bf16[2,20,16,128]{3,2,1,0:T(8,128)(2,1)S(1)}, u32[]{:S(2)}, u32[]{:S(2)}) collective-permute-start(bf16[2,20,16,128]{3,2,1,0:T(8,128)(2,1)S(1)} %pad_maximum_fusion.3), channel_id=1, source_target_pairs={{0,1},{1,0},{2,3},{3,2},{4,5},{5,4},{6,7},{7,6},{8,9},{9,8},{10,11... | collective-permute-start | bytes 491528 | tf_op jit(solution)/shard_map/ppermute | solution.py:347
  32.0 0.0 collective-permute-done.7.refs_11_
  32.0 0.0 collective-permute-done.8.refs_12_
  32.0 0.7 %collective-permute-done.9.refs_13_ = bf16[2,20,16,128]{3,2,1,0:T(8,128)(2,1)S(1)} collective-permute-done((bf16[2,20,16,128]{3,2,1,0:T(8,128)(2,1)S(1)}, bf16[2,20,16,128]{3,2,1,0:T(8,128)(2,1)S(1)}, u32[]{:S(2)}, u32[]{:S(2)}) %collective-permute-start.9) | collective-permute-done | bytes 163872 | tf_op jit(solution)/shard_map/ppermute | solution.py:347
  32.7 0.3 collective-permute-done.10.refs_14_
  33.0 0.0 copy-done
  33.0 0.0 copy-done.1
  33.0 0.0 copy-done.2
  33.0 0.0 copy-done.3
  33.0 3.9 %prune.1 = f32[8,128]{1,0:T(8,128)S(1)} custom-call(s32[64]{0:T(128)S(1)} %copy-done.1, s32[1]{0:T(128)} %bitcast.me_ref.after_ref, s32[1,512]{1,0:T(1,128)S(1)} %bitcast.36, f32[1,126]{1,0:T(1,128)S(1)} %bitcast.37, f32[1,126]{1,0:T(1,128)S(1)} %bitcast.38, bf16[20,16,128]{2,1,0:T(8,128)(2,1)S(1)} %bitcast.35, ...), custom_call_target="tpu_custom_call" | custom-call | tf_op jit(solution)/shard_map/prune/pallas_call | solution.py:207
  36.9 0.4 collective-permute-start.11
  37.3 0.8 %collective-permute-done.11 = f32[8,128]{1,0:T(8,128)S(1)} collective-permute-done((f32[8,128]{1,0:T(8,128)S(1)}, f32[8,128]{1,0:T(8,128)S(1)}, u32[]{:S(2)}, u32[]{:S(2)}) %collective-permute-start.11) | collective-permute-done | bytes 4128 | tf_op jit(solution)/shard_map/ppermute | solution.py:370
  38.2 2.3 %collective-permute-start.14 = (f32[8,128]{1,0:T(8,128)S(1)}, f32[8,128]{1,0:T(8,128)S(1)}, u32[]{:S(2)}, u32[]{:S(2)}) collective-permute-start(f32[8,128]{1,0:T(8,128)S(1)} %add.31), channel_id=1, source_target_pairs={{0,15},{1,14},{2,13},{3,12},{4,11},{5,10},{6,9},{7,8},{8,7},{9,6},... | collective-permute-start | bytes 12296 | tf_op jit(solution)/shard_map/ppermute | solution.py:370
  40.4 1.1 %collective-permute-start.13 = (f32[8,128]{1,0:T(8,128)S(1)}, f32[8,128]{1,0:T(8,128)S(1)}, u32[]{:S(2)}, u32[]{:S(2)}) collective-permute-start(f32[8,128]{1,0:T(8,128)S(1)} %add.31), channel_id=1, source_target_pairs={{0,13},{1,12},{2,15},{3,14},{4,9},{5,8},{6,11},{7,10},{8,5},{9,4},... | collective-permute-start | bytes 12296 | tf_op jit(solution)/shard_map/ppermute | solution.py:370
  41.5 1.6 %collective-permute-start.12 = (f32[8,128]{1,0:T(8,128)S(1)}, f32[8,128]{1,0:T(8,128)S(1)}, u32[]{:S(2)}, u32[]{:S(2)}) collective-permute-start(f32[8,128]{1,0:T(8,128)S(1)} %add.31), channel_id=1, source_target_pairs={{0,3},{1,2},{2,1},{3,0},{4,7},{5,6},{6,5},{7,4},{8,11},{9,10},{10,... | collective-permute-start | bytes 12296 | tf_op jit(solution)/shard_map/ppermute | solution.py:370
  43.1 0.8 %collective-permute-done.14 = f32[8,128]{1,0:T(8,128)S(1)} collective-permute-done((f32[8,128]{1,0:T(8,128)S(1)}, f32[8,128]{1,0:T(8,128)S(1)}, u32[]{:S(2)}, u32[]{:S(2)}) %collective-permute-start.14) | collective-permute-done | bytes 4128 | tf_op jit(solution)/shard_map/ppermute | solution.py:370
  43.9 1.4 %collective-permute-done.13 = f32[8,128]{1,0:T(8,128)S(1)} collective-permute-done((f32[8,128]{1,0:T(8,128)S(1)}, f32[8,128]{1,0:T(8,128)S(1)}, u32[]{:S(2)}, u32[]{:S(2)}) %collective-permute-start.13) | collective-permute-done | bytes 4128 | tf_op jit(solution)/shard_map/ppermute | solution.py:370
  45.3 0.0 collective-permute-done.12
  45.3 1.3 %collective-permute-start.15 = (f32[8,128]{1,0:T(8,128)S(1)}, f32[8,128]{1,0:T(8,128)S(1)}, u32[]{:S(2)}, u32[]{:S(2)}) collective-permute-start(f32[8,128]{1,0:T(8,128)S(1)} %add_add_fusion), channel_id=1, source_target_pairs={{0,5},{1,4},{2,7},{3,6},{4,1},{5,0},{6,3},{7,2},{8,13},{9,12},{10,... | collective-permute-start | bytes 12296 | tf_op jit(solution)/shard_map/ppermute | solution.py:370
  46.6 1.8 %collective-permute-done.15 = f32[8,128]{1,0:T(8,128)S(1)} collective-permute-done((f32[8,128]{1,0:T(8,128)S(1)}, f32[8,128]{1,0:T(8,128)S(1)}, u32[]{:S(2)}, u32[]{:S(2)}) %collective-permute-start.15) | collective-permute-done | bytes 4128 | tf_op jit(solution)/shard_map/ppermute | solution.py:370
  48.4 0.5 %fusion = (f32[126]{0:T(128)}, f32[126]{0:T(128)}) fusion(f32[8,128]{1,0:T(8,128)S(1)} %add.35), kind=kLoop, calls=%fused_computation.14 | loop fusion | flops 378 | bytes 2520 | tf_op jit(solution)/shard_map/div | solution.py:389
  (14 shorter events, 0.1 us)
Async XLA Ops:
  1.6 11.9 %collective-permute-start.1 = (bf16[20,32,128]{2,1,0:T(8,128)(2,1)S(1)}, bf16[20,32,128]{2,1,0:T(8,128)(2,1)S(1)}, u32[]{:S(2)}, u32[]{:S(2)}) collective-permute-start(bf16[20,32,128]{2,1,0:T(8,128)(2,1)S(1)} %bitcast.34), channel_id=1, source_target_pairs={{0,8},{1,9},{2,10},{3,11},{4,12},{5,13},{6,14},{7,15},{8,0},{9,1},... | collective-permute-start | bytes 491528 | tf_op jit(solution)/shard_map/ppermute | solution.py:347
  7.1 25.9 %copy-start = (s32[512]{0:T(512)S(1)}, s32[512]{0:T(512)}, u32[]{:S(2)}) copy-start(s32[512]{0:T(512)} %param.7) | copy-start | bytes 6148
  7.1 25.9 %copy-start.1 = (s32[64]{0:T(128)S(1)}, s32[64]{0:T(128)}, u32[]{:S(2)}) copy-start(s32[64]{0:T(128)} %order_ref.1) | copy-start | bytes 772
  7.1 25.9 %copy-start.2 = (f32[126]{0:T(128)S(1)}, f32[126]{0:T(128)}, u32[]{:S(2)}) copy-start(f32[126]{0:T(128)} %param.8) | copy-start | bytes 1516
  7.1 25.9 %copy-start.3 = (f32[126]{0:T(128)S(1)}, f32[126]{0:T(128)}, u32[]{:S(2)}) copy-start(f32[126]{0:T(128)} %param.9) | copy-start | bytes 1516
  7.2 10.2 %collective-permute-start = (bf16[2,20,16,128]{3,2,1,0:T(8,128)(2,1)S(1)}, bf16[2,20,16,128]{3,2,1,0:T(8,128)(2,1)S(1)}, u32[]{:S(2)}, u32[]{:S(2)}) collective-permute-start(bf16[2,20,16,128]{3,2,1,0:T(8,128)(2,1)S(1)} %get-tuple-element.11), channel_id=1, source_target_pairs={{0,1},{1,0},{2,3},{3,2},{4,5},{5,4},{6,7},{7,6},{8,9},{9,8},{10,11... | collective-permute-start | bytes 491528 | tf_op jit(solution)/shard_map/ppermute | solution.py:347
  7.2 11.8 %collective-permute-start.2 = (bf16[20,32,128]{2,1,0:T(8,128)(2,1)S(1)}, bf16[20,32,128]{2,1,0:T(8,128)(2,1)S(1)}, u32[]{:S(2)}, u32[]{:S(2)}) collective-permute-start(bf16[20,32,128]{2,1,0:T(8,128)(2,1)S(1)} %bitcast.43), channel_id=1, source_target_pairs={{0,4},{1,5},{2,6},{3,7},{4,0},{5,1},{6,2},{7,3},{8,12},{9,13},{10,... | collective-permute-start | bytes 491528 | tf_op jit(solution)/shard_map/ppermute | solution.py:347
  8.9 13.5 %collective-permute-start.3 = (bf16[20,32,128]{2,1,0:T(8,128)(2,1)S(1)}, bf16[20,32,128]{2,1,0:T(8,128)(2,1)S(1)}, u32[]{:S(2)}, u32[]{:S(2)}) collective-permute-start(bf16[20,32,128]{2,1,0:T(8,128)(2,1)S(1)} %bitcast.42), channel_id=1, source_target_pairs={{0,10},{1,11},{2,8},{3,9},{4,14},{5,15},{6,12},{7,13},{8,2},{9,3},... | collective-permute-start | bytes 491528 | tf_op jit(solution)/shard_map/ppermute | solution.py:347
  10.2 21.1 %collective-permute-start.4 = (bf16[20,32,128]{2,1,0:T(8,128)(2,1)S(1)}, bf16[20,32,128]{2,1,0:T(8,128)(2,1)S(1)}, u32[]{:S(2)}, u32[]{:S(2)}) collective-permute-start(bf16[20,32,128]{2,1,0:T(8,128)(2,1)S(1)} %bitcast.41), channel_id=1, source_target_pairs={{0,6},{1,7},{2,4},{3,5},{4,2},{5,3},{6,0},{7,1},{8,14},{9,15},{10,... | collective-permute-start | bytes 491528 | tf_op jit(solution)/shard_map/ppermute | solution.py:347
  13.5 17.9 %collective-permute-start.5 = (bf16[20,32,128]{2,1,0:T(8,128)(2,1)S(1)}, bf16[20,32,128]{2,1,0:T(8,128)(2,1)S(1)}, u32[]{:S(2)}, u32[]{:S(2)}) collective-permute-start(bf16[20,32,128]{2,1,0:T(8,128)(2,1)S(1)} %bitcast.40), channel_id=1, source_target_pairs={{0,12},{1,13},{2,14},{3,15},{4,8},{5,9},{6,10},{7,11},{8,4},{9,5},... | collective-permute-start | bytes 491528 | tf_op jit(solution)/shard_map/ppermute | solution.py:347
  17.4 14.0 %collective-permute-start.6 = (bf16[20,32,128]{2,1,0:T(8,128)(2,1)S(1)}, bf16[20,32,128]{2,1,0:T(8,128)(2,1)S(1)}, u32[]{:S(2)}, u32[]{:S(2)}) collective-permute-start(bf16[20,32,128]{2,1,0:T(8,128)(2,1)S(1)} %bitcast.39), channel_id=1, source_target_pairs={{0,2},{1,3},{2,0},{3,1},{4,6},{5,7},{6,4},{7,5},{8,10},{9,11},{10,... | collective-permute-start | bytes 491528 | tf_op jit(solution)/shard_map/ppermute | solution.py:347
  19.0 13.0 %collective-permute-start.7 = (bf16[2,20,16,128]{3,2,1,0:T(8,128)(2,1)S(1)}, bf16[2,20,16,128]{3,2,1,0:T(8,128)(2,1)S(1)}, u32[]{:S(2)}, u32[]{:S(2)}) collective-permute-start(bf16[2,20,16,128]{3,2,1,0:T(8,128)(2,1)S(1)} %pad_maximum_fusion), channel_id=1, source_target_pairs={{0,14},{1,15},{2,12},{3,13},{4,10},{5,11},{6,8},{7,9},{8,6},{9,7},... | collective-permute-start | bytes 491528 | tf_op jit(solution)/shard_map/ppermute | solution.py:347
  22.4 9.6 %collective-permute-start.8 = (bf16[2,20,16,128]{3,2,1,0:T(8,128)(2,1)S(1)}, bf16[2,20,16,128]{3,2,1,0:T(8,128)(2,1)S(1)}, u32[]{:S(2)}, u32[]{:S(2)}) collective-permute-start(bf16[2,20,16,128]{3,2,1,0:T(8,128)(2,1)S(1)} %pad_maximum_fusion.1), channel_id=1, source_target_pairs={{0,1},{1,0},{2,3},{3,2},{4,5},{5,4},{6,7},{7,6},{8,9},{9,8},{10,11... | collective-permute-start | bytes 491528 | tf_op jit(solution)/shard_map/ppermute | solution.py:347
  31.3 1.5 %collective-permute-start.9 = (bf16[2,20,16,128]{3,2,1,0:T(8,128)(2,1)S(1)}, bf16[2,20,16,128]{3,2,1,0:T(8,128)(2,1)S(1)}, u32[]{:S(2)}, u32[]{:S(2)}) collective-permute-start(bf16[2,20,16,128]{3,2,1,0:T(8,128)(2,1)S(1)} %pad_maximum_fusion.2), channel_id=1, source_target_pairs={{0,1},{1,0},{2,3},{3,2},{4,5},{5,4},{6,7},{7,6},{8,9},{9,8},{10,11... | collective-permute-start | bytes 491528 | tf_op jit(solution)/shard_map/ppermute | solution.py:347
  31.5 1.6 %collective-permute-start.10 = (bf16[2,20,16,128]{3,2,1,0:T(8,128)(2,1)S(1)}, bf16[2,20,16,128]{3,2,1,0:T(8,128)(2,1)S(1)}, u32[]{:S(2)}, u32[]{:S(2)}) collective-permute-start(bf16[2,20,16,128]{3,2,1,0:T(8,128)(2,1)S(1)} %pad_maximum_fusion.3), channel_id=1, source_target_pairs={{0,1},{1,0},{2,3},{3,2},{4,5},{5,4},{6,7},{7,6},{8,9},{9,8},{10,11... | collective-permute-start | bytes 491528 | tf_op jit(solution)/shard_map/ppermute | solution.py:347
  36.9 1.3 %collective-permute-start.11 = (f32[8,128]{1,0:T(8,128)S(1)}, f32[8,128]{1,0:T(8,128)S(1)}, u32[]{:S(2)}, u32[]{:S(2)}) collective-permute-start(f32[8,128]{1,0:T(8,128)S(1)} %prune.1), channel_id=1, source_target_pairs={{0,1},{1,0},{2,3},{3,2},{4,5},{5,4},{6,7},{7,6},{8,9},{9,8},{10,11... | collective-permute-start | bytes 12296 | tf_op jit(solution)/shard_map/ppermute | solution.py:370
  38.2 5.7 %collective-permute-start.14 = (f32[8,128]{1,0:T(8,128)S(1)}, f32[8,128]{1,0:T(8,128)S(1)}, u32[]{:S(2)}, u32[]{:S(2)}) collective-permute-start(f32[8,128]{1,0:T(8,128)S(1)} %add.31), channel_id=1, source_target_pairs={{0,15},{1,14},{2,13},{3,12},{4,11},{5,10},{6,9},{7,8},{8,7},{9,6},... | collective-permute-start | bytes 12296 | tf_op jit(solution)/shard_map/ppermute | solution.py:370
  40.4 4.8 %collective-permute-start.13 = (f32[8,128]{1,0:T(8,128)S(1)}, f32[8,128]{1,0:T(8,128)S(1)}, u32[]{:S(2)}, u32[]{:S(2)}) collective-permute-start(f32[8,128]{1,0:T(8,128)S(1)} %add.31), channel_id=1, source_target_pairs={{0,13},{1,12},{2,15},{3,14},{4,9},{5,8},{6,11},{7,10},{8,5},{9,4},... | collective-permute-start | bytes 12296 | tf_op jit(solution)/shard_map/ppermute | solution.py:370
  41.5 3.8 %collective-permute-start.12 = (f32[8,128]{1,0:T(8,128)S(1)}, f32[8,128]{1,0:T(8,128)S(1)}, u32[]{:S(2)}, u32[]{:S(2)}) collective-permute-start(f32[8,128]{1,0:T(8,128)S(1)} %add.31), channel_id=1, source_target_pairs={{0,3},{1,2},{2,1},{3,0},{4,7},{5,6},{6,5},{7,4},{8,11},{9,10},{10,... | collective-permute-start | bytes 12296 | tf_op jit(solution)/shard_map/ppermute | solution.py:370
  45.3 3.1 %collective-permute-start.15 = (f32[8,128]{1,0:T(8,128)S(1)}, f32[8,128]{1,0:T(8,128)S(1)}, u32[]{:S(2)}, u32[]{:S(2)}) collective-permute-start(f32[8,128]{1,0:T(8,128)S(1)} %add_add_fusion), channel_id=1, source_target_pairs={{0,5},{1,4},{2,7},{3,6},{4,1},{5,0},{6,3},{7,2},{8,13},{9,12},{10,... | collective-permute-start | bytes 12296 | tf_op jit(solution)/shard_map/ppermute | solution.py:370

commit v7 on v6

--- a/solution.py
+++ b/solution.py
@@ -133,15 +133,18 @@
     seed = 1.0 / total
     dseed = -(dtotal * seed) * seed
 
-    def record(at, grad, curve):
-        here = pl.ds(pl.multiple_of(at * ROWS, ROWS), ROWS)
-        grad_ref[here, :] = weight * grad
-        curve_ref[here, :] = weight * curve
+    def record(row_at, total, dtotal, half, dhalf):
+        share = row(rate_ref, row_at) + 1.0 / states
+        both_totals = total * half
+        here = pl.ds(pl.multiple_of(row_at * ROWS, ROWS), ROWS)
+        grad_ref[here, :] = weight * (share * both_totals - 0.5)
+        change = total * dhalf if dtotal is None else dtotal * half + total * dhalf
+        curve_ref[here, :] = weight * (share * change + row(slope_ref, row_at) * both_totals)
 
     def down(at, ybar, dybar):
         half, dhalf = part_sum(ybar), part_sum(dybar)
         total, dtotal = sums_ref[at], dsums_ref[at - tips]
-        record(at, total * half, dtotal * half + total * dhalf)
+        record(at, total, dtotal, half, dhalf)
         full, dfull = both(half), both(dhalf)
         rate, slope = row(rate_ref, at), row(slope_ref, at)
         xbar = ybar + (rate * full)[None]
@@ -157,7 +160,7 @@
                 tip, mate = order_ref[child], order_ref[other]
                 total = sums_ref[child]
                 push = row(slope_ref, mate) * sums_ref[other]
-                record(tip, total * half, total * (dhalf + 0.5 * (push * zsum)))
+                record(tip, total, None, half, dhalf + 0.5 * (push * zsum))
                 continue
             at, mate = offsets[level - 1] + child, offsets[level - 1] + other
             yb, dyb = fetch(mate)
@@ -181,14 +184,11 @@
 
     lax.fori_loop(0, tips >> cut, descend, 0)
 
-    scale = decay * grow / states
-
     def over_sites(ref):
         rows = part_sum([ref[pl.ds(part, LANES, ROWS), :] for part in range(ROWS)])
-        return jnp.sum(jnp.transpose(rows), axis=0, keepdims=True)[:, :branches] * scale
+        return jnp.sum(jnp.transpose(rows), axis=0, keepdims=True)[:, :branches] * decay
 
     grad, curve = over_sites(grad_ref), over_sites(curve_ref)
-    curve = curve + decay * toward * grad
     out_ref[...] = jnp.zeros_like(out_ref)
     out_ref[0:1, :branches] = grad
     out_ref[1:2, :branches] = curve
@@ -386,7 +386,7 @@
         pieces, unpack = exchange_plain(probs)
     part = prune(pieces, me, unpack, leaf_order, site_weights, branch_length, direction, states, each)
     sums = total_over_sites(part)[:, :branches]
-    return sums[0] / sums[2] - states / (states - 1.0), sums[1] / sums[2]
+    return sums[0] / sums[2], sums[1] / sums[2]
 
 
 def solution(mesh):

time: 49.1 us -> 49.2 us (level)
  no operation moved by 1% of the time
where the time goes in v7:
time: 49.2 us; the launch traced here: 49.1 us
  starting transfers between devices  21.3 us (43%)
  waiting for transfers between devices  19.9 us (40%)
  Pallas kernels  6.35 us (13%)
  between operations  0.78 us (2%)
  other arithmetic  0.61 us (1%)
    ppermute x11, waiting for transfers between devices, swap(): return lax.ppermute(block, 'sites', [(i, i ^ step) for i in range(peers)])  15.1 us
    ppermute x11, starting transfers between devices, swap(): return lax.ppermute(block, 'sites', [(i, i ^ step) for i in range(peers)])  14.7 us
    ppermute x5, starting transfers between devices, total_over_sites(): lax.ppermute(part, 'sites', [(i, i ^ step) for i in range(peers)])  6.67 us
    ppermute x5, waiting for transfers between devices, total_over_sites(): lax.ppermute(part, 'sites', [(i, i ^ step) for i in range(peers)])  4.79 us
    pallas_call x1, Pallas kernels, prune(): pl.pallas_call(functools.partial(prune_kernel, unpack=unpack, held=len(pi...  4 us
    pallas_call x2, Pallas kernels, cut(): pl.pallas_call(functools.partial(cut_kernel, firsts=firsts), in_specs=[pl...  2.35 us
  transfers between devices with their start and end apart: 16, of which 9 were waited for; matrix products, arithmetic and copies ran while one was open for 0% of the time, Pallas kernels for 3%

profile of v7, /device:TPU:0, one launch (start us, length us, event | category | flops | bytes accessed | tf_op | source)
XLA Modules:
  0.0 49.1 jit_solution(2517548246589838598)
XLA Ops:
  0.6 0.9 %cut.2.after_ref = bf16[1,20,32,128]{3,2,1,0:T(8,128)(2,1)S(1)} custom-call(s32[1]{0:T(128)} %bitcast.me_ref.after_ref, bf16[20,256,128]{2,1,0:T(8,128)(2,1)} %bitcast.44, s32[1]{0:T(128)} %bitcast.me_ref.after_ref), custom_call_target="tpu_custom_call" | custom-call | tf_op jit(solution)/shard_map/cut/pallas_call | solution.py:301
  1.6 4.1 %collective-permute-start.1 = (bf16[20,32,128]{2,1,0:T(8,128)(2,1)S(1)}, bf16[20,32,128]{2,1,0:T(8,128)(2,1)S(1)}, u32[]{:S(2)}, u32[]{:S(2)}) collective-permute-start(bf16[20,32,128]{2,1,0:T(8,128)(2,1)S(1)} %bitcast.34), channel_id=1, source_target_pairs={{0,8},{1,9},{2,10},{3,11},{4,12},{5,13},{6,14},{7,15},{8,0},{9,1},... | collective-permute-start | bytes 491528 | tf_op jit(solution)/shard_map/ppermute | solution.py:347
  5.7 1.4 %cut.3 = (bf16[1,20,32,128]{3,2,1,0:T(8,128)(2,1)S(1)}, bf16[1,20,32,128]{3,2,1,0:T(8,128)(2,1)S(1)}, bf16[1,20,32,128]{3,2,1,0:T(8,128)(2,1)S(1)}, bf16[1,20,32...) custom-call(s32[1]{0:T(128)} %bitcast.me_ref.after_ref, ...), custom_call_target="tpu_custom_call" | custom-call | tf_op jit(solution)/shard_map/cut/pallas_call | solution.py:301
  7.1 0.0 copy-start
  7.1 0.0 copy-start.1
  7.1 0.0 copy-start.2
  7.1 0.0 copy-start.3
  7.2 0.1 collective-permute-start
  7.2 1.6 %collective-permute-start.2 = (bf16[20,32,128]{2,1,0:T(8,128)(2,1)S(1)}, bf16[20,32,128]{2,1,0:T(8,128)(2,1)S(1)}, u32[]{:S(2)}, u32[]{:S(2)}) collective-permute-start(bf16[20,32,128]{2,1,0:T(8,128)(2,1)S(1)} %bitcast.43), channel_id=1, source_target_pairs={{0,4},{1,5},{2,6},{3,7},{4,0},{5,1},{6,2},{7,3},{8,12},{9,13},{10,... | collective-permute-start | bytes 491528 | tf_op jit(solution)/shard_map/ppermute | solution.py:347
  8.9 1.3 %collective-permute-start.3 = (bf16[20,32,128]{2,1,0:T(8,128)(2,1)S(1)}, bf16[20,32,128]{2,1,0:T(8,128)(2,1)S(1)}, u32[]{:S(2)}, u32[]{:S(2)}) collective-permute-start(bf16[20,32,128]{2,1,0:T(8,128)(2,1)S(1)} %bitcast.42), channel_id=1, source_target_pairs={{0,10},{1,11},{2,8},{3,9},{4,14},{5,15},{6,12},{7,13},{8,2},{9,3},... | collective-permute-start | bytes 491528 | tf_op jit(solution)/shard_map/ppermute | solution.py:347
  10.2 0.1 collective-permute-start.4
  10.3 3.2 %collective-permute-done.1.refs_5_ = bf16[20,32,128]{2,1,0:T(8,128)(2,1)S(1)} collective-permute-done((bf16[20,32,128]{2,1,0:T(8,128)(2,1)S(1)}, bf16[20,32,128]{2,1,0:T(8,128)(2,1)S(1)}, u32[]{:S(2)}, u32[]{:S(2)}) %collective-permute-start.1) | collective-permute-done | bytes 163872 | tf_op jit(solution)/shard_map/ppermute | solution.py:347
  13.5 3.9 %collective-permute-start.5 = (bf16[20,32,128]{2,1,0:T(8,128)(2,1)S(1)}, bf16[20,32,128]{2,1,0:T(8,128)(2,1)S(1)}, u32[]{:S(2)}, u32[]{:S(2)}) collective-permute-start(bf16[20,32,128]{2,1,0:T(8,128)(2,1)S(1)} %bitcast.40), channel_id=1, source_target_pairs={{0,12},{1,13},{2,14},{3,15},{4,8},{5,9},{6,10},{7,11},{8,4},{9,5},... | collective-permute-start | bytes 491528 | tf_op jit(solution)/shard_map/ppermute | solution.py:347
  17.4 0.0 collective-permute-done.refs_4_
  17.4 1.6 %collective-permute-start.6 = (bf16[20,32,128]{2,1,0:T(8,128)(2,1)S(1)}, bf16[20,32,128]{2,1,0:T(8,128)(2,1)S(1)}, u32[]{:S(2)}, u32[]{:S(2)}) collective-permute-start(bf16[20,32,128]{2,1,0:T(8,128)(2,1)S(1)} %bitcast.39), channel_id=1, source_target_pairs={{0,2},{1,3},{2,0},{3,1},{4,6},{5,7},{6,4},{7,5},{8,10},{9,11},{10,... | collective-permute-start | bytes 491528 | tf_op jit(solution)/shard_map/ppermute | solution.py:347
  19.0 0.0 collective-permute-done.2.refs_6_
  19.0 1.4 %collective-permute-start.7 = (bf16[2,20,16,128]{3,2,1,0:T(8,128)(2,1)S(1)}, bf16[2,20,16,128]{3,2,1,0:T(8,128)(2,1)S(1)}, u32[]{:S(2)}, u32[]{:S(2)}) collective-permute-start(bf16[2,20,16,128]{3,2,1,0:T(8,128)(2,1)S(1)} %pad_maximum_fusion), channel_id=1, source_target_pairs={{0,14},{1,15},{2,12},{3,13},{4,10},{5,11},{6,8},{7,9},{8,6},{9,7},... | collective-permute-start | bytes 491528 | tf_op jit(solution)/shard_map/ppermute | solution.py:347
  20.4 2.0 %collective-permute-done.3.refs_7_ = bf16[20,32,128]{2,1,0:T(8,128)(2,1)S(1)} collective-permute-done((bf16[20,32,128]{2,1,0:T(8,128)(2,1)S(1)}, bf16[20,32,128]{2,1,0:T(8,128)(2,1)S(1)}, u32[]{:S(2)}, u32[]{:S(2)}) %collective-permute-start.3) | collective-permute-done | bytes 163872 | tf_op jit(solution)/shard_map/ppermute | solution.py:347
  22.4 0.0 collective-permute-start.8
  22.4 8.8 %collective-permute-done.4.refs_8_ = bf16[20,32,128]{2,1,0:T(8,128)(2,1)S(1)} collective-permute-done((bf16[20,32,128]{2,1,0:T(8,128)(2,1)S(1)}, bf16[20,32,128]{2,1,0:T(8,128)(2,1)S(1)}, u32[]{:S(2)}, u32[]{:S(2)}) %collective-permute-start.4) | collective-permute-done | bytes 163872 | tf_op jit(solution)/shard_map/ppermute | solution.py:347
  31.3 0.1 collective-permute-start.9
  31.4 0.0 collective-permute-done.5.refs_9_
  31.4 0.0 collective-permute-done.6.refs_10_
  31.5 0.5 %collective-permute-start.10 = (bf16[2,20,16,128]{3,2,1,0:T(8,128)(2,1)S(1)}, bf16[2,20,16,128]{3,2,1,0:T(8,128)(2,1)S(1)}, u32[]{:S(2)}, u32[]{:S(2)}) collective-permute-start(bf16[2,20,16,128]{3,2,1,0:T(8,128)(2,1)S(1)} %pad_maximum_fusion.3), channel_id=1, source_target_pairs={{0,1},{1,0},{2,3},{3,2},{4,5},{5,4},{6,7},{7,6},{8,9},{9,8},{10,11... | collective-permute-start | bytes 491528 | tf_op jit(solution)/shard_map/ppermute | solution.py:347
  32.0 0.0 collective-permute-done.7.refs_11_
  32.0 0.0 collective-permute-done.8.refs_12_
  32.0 0.7 %collective-permute-done.9.refs_13_ = bf16[2,20,16,128]{3,2,1,0:T(8,128)(2,1)S(1)} collective-permute-done((bf16[2,20,16,128]{3,2,1,0:T(8,128)(2,1)S(1)}, bf16[2,20,16,128]{3,2,1,0:T(8,128)(2,1)S(1)}, u32[]{:S(2)}, u32[]{:S(2)}) %collective-permute-start.9) | collective-permute-done | bytes 163872 | tf_op jit(solution)/shard_map/ppermute | solution.py:347
  32.7 0.3 collective-permute-done.10.refs_14_
  33.0 0.0 copy-done
  33.0 0.0 copy-done.1
  33.0 0.0 copy-done.2
  33.0 0.0 copy-done.3
  33.0 4.0 %prune.1 = f32[8,128]{1,0:T(8,128)S(1)} custom-call(s32[64]{0:T(128)S(1)} %copy-done.1, s32[1]{0:T(128)} %bitcast.me_ref.after_ref, s32[1,512]{1,0:T(1,128)S(1)} %bitcast.36, f32[1,126]{1,0:T(1,128)S(1)} %bitcast.37, f32[1,126]{1,0:T(1,128)S(1)} %bitcast.38, bf16[20,16,128]{2,1,0:T(8,128)(2,1)S(1)} %bitcast.35, ...), custom_call_target="tpu_custom_call" | custom-call | tf_op jit(solution)/shard_map/prune/pallas_call | solution.py:207
  37.0 0.4 collective-permute-start.11
  37.5 0.8 %collective-permute-done.11 = f32[8,128]{1,0:T(8,128)S(1)} collective-permute-done((f32[8,128]{1,0:T(8,128)S(1)}, f32[8,128]{1,0:T(8,128)S(1)}, u32[]{:S(2)}, u32[]{:S(2)}) %collective-permute-start.11) | collective-permute-done | bytes 4128 | tf_op jit(solution)/shard_map/ppermute | solution.py:370
  38.3 2.3 %collective-permute-start.14 = (f32[8,128]{1,0:T(8,128)S(1)}, f32[8,128]{1,0:T(8,128)S(1)}, u32[]{:S(2)}, u32[]{:S(2)}) collective-permute-start(f32[8,128]{1,0:T(8,128)S(1)} %add.29), channel_id=1, source_target_pairs={{0,15},{1,14},{2,13},{3,12},{4,11},{5,10},{6,9},{7,8},{8,7},{9,6},... | collective-permute-start | bytes 12296 | tf_op jit(solution)/shard_map/ppermute | solution.py:370
  40.6 1.1 %collective-permute-start.13 = (f32[8,128]{1,0:T(8,128)S(1)}, f32[8,128]{1,0:T(8,128)S(1)}, u32[]{:S(2)}, u32[]{:S(2)}) collective-permute-start(f32[8,128]{1,0:T(8,128)S(1)} %add.29), channel_id=1, source_target_pairs={{0,13},{1,12},{2,15},{3,14},{4,9},{5,8},{6,11},{7,10},{8,5},{9,4},... | collective-permute-start | bytes 12296 | tf_op jit(solution)/shard_map/ppermute | solution.py:370
  41.6 1.6 %collective-permute-start.12 = (f32[8,128]{1,0:T(8,128)S(1)}, f32[8,128]{1,0:T(8,128)S(1)}, u32[]{:S(2)}, u32[]{:S(2)}) collective-permute-start(f32[8,128]{1,0:T(8,128)S(1)} %add.29), channel_id=1, source_target_pairs={{0,3},{1,2},{2,1},{3,0},{4,7},{5,6},{6,5},{7,4},{8,11},{9,10},{10,... | collective-permute-start | bytes 12296 | tf_op jit(solution)/shard_map/ppermute | solution.py:370
  43.3 0.8 %collective-permute-done.14 = f32[8,128]{1,0:T(8,128)S(1)} collective-permute-done((f32[8,128]{1,0:T(8,128)S(1)}, f32[8,128]{1,0:T(8,128)S(1)}, u32[]{:S(2)}, u32[]{:S(2)}) %collective-permute-start.14) | collective-permute-done | bytes 4128 | tf_op jit(solution)/shard_map/ppermute | solution.py:370
  44.0 1.4 %collective-permute-done.13 = f32[8,128]{1,0:T(8,128)S(1)} collective-permute-done((f32[8,128]{1,0:T(8,128)S(1)}, f32[8,128]{1,0:T(8,128)S(1)}, u32[]{:S(2)}, u32[]{:S(2)}) %collective-permute-start.13) | collective-permute-done | bytes 4128 | tf_op jit(solution)/shard_map/ppermute | solution.py:370
  45.4 0.0 collective-permute-done.12
  45.4 1.3 %collective-permute-start.15 = (f32[8,128]{1,0:T(8,128)S(1)}, f32[8,128]{1,0:T(8,128)S(1)}, u32[]{:S(2)}, u32[]{:S(2)}) collective-permute-start(f32[8,128]{1,0:T(8,128)S(1)} %add_add_fusion), channel_id=1, source_target_pairs={{0,5},{1,4},{2,7},{3,6},{4,1},{5,0},{6,3},{7,2},{8,13},{9,12},{10,... | collective-permute-start | bytes 12296 | tf_op jit(solution)/shard_map/ppermute | solution.py:370
  46.7 1.8 %collective-permute-done.15 = f32[8,128]{1,0:T(8,128)S(1)} collective-permute-done((f32[8,128]{1,0:T(8,128)S(1)}, f32[8,128]{1,0:T(8,128)S(1)}, u32[]{:S(2)}, u32[]{:S(2)}) %collective-permute-start.15) | collective-permute-done | bytes 4128 | tf_op jit(solution)/shard_map/ppermute | solution.py:370
  48.5 0.5 %fusion.1 = (f32[126]{0:T(128)}, f32[126]{0:T(128)}) fusion(f32[8,128]{1,0:T(8,128)S(1)} %add.33), kind=kLoop, calls=%fused_computation.14 | loop fusion | flops 252 | bytes 2520 | tf_op jit(solution)/shard_map/div | solution.py:389
  (14 shorter events, 0.1 us)
Async XLA Ops:
  1.6 11.9 %collective-permute-start.1 = (bf16[20,32,128]{2,1,0:T(8,128)(2,1)S(1)}, bf16[20,32,128]{2,1,0:T(8,128)(2,1)S(1)}, u32[]{:S(2)}, u32[]{:S(2)}) collective-permute-start(bf16[20,32,128]{2,1,0:T(8,128)(2,1)S(1)} %bitcast.34), channel_id=1, source_target_pairs={{0,8},{1,9},{2,10},{3,11},{4,12},{5,13},{6,14},{7,15},{8,0},{9,1},... | collective-permute-start | bytes 491528 | tf_op jit(solution)/shard_map/ppermute | solution.py:347
  7.1 25.9 %copy-start = (s32[512]{0:T(512)S(1)}, s32[512]{0:T(512)}, u32[]{:S(2)}) copy-start(s32[512]{0:T(512)} %param.7) | copy-start | bytes 6148
  7.1 25.9 %copy-start.1 = (s32[64]{0:T(128)S(1)}, s32[64]{0:T(128)}, u32[]{:S(2)}) copy-start(s32[64]{0:T(128)} %order_ref.1) | copy-start | bytes 772
  7.1 25.9 %copy-start.2 = (f32[126]{0:T(128)S(1)}, f32[126]{0:T(128)}, u32[]{:S(2)}) copy-start(f32[126]{0:T(128)} %param.8) | copy-start | bytes 1516
  7.1 25.9 %copy-start.3 = (f32[126]{0:T(128)S(1)}, f32[126]{0:T(128)}, u32[]{:S(2)}) copy-start(f32[126]{0:T(128)} %param.9) | copy-start | bytes 1516
  7.2 10.2 %collective-permute-start = (bf16[2,20,16,128]{3,2,1,0:T(8,128)(2,1)S(1)}, bf16[2,20,16,128]{3,2,1,0:T(8,128)(2,1)S(1)}, u32[]{:S(2)}, u32[]{:S(2)}) collective-permute-start(bf16[2,20,16,128]{3,2,1,0:T(8,128)(2,1)S(1)} %get-tuple-element.11), channel_id=1, source_target_pairs={{0,1},{1,0},{2,3},{3,2},{4,5},{5,4},{6,7},{7,6},{8,9},{9,8},{10,11... | collective-permute-start | bytes 491528 | tf_op jit(solution)/shard_map/ppermute | solution.py:347
  7.2 11.8 %collective-permute-start.2 = (bf16[20,32,128]{2,1,0:T(8,128)(2,1)S(1)}, bf16[20,32,128]{2,1,0:T(8,128)(2,1)S(1)}, u32[]{:S(2)}, u32[]{:S(2)}) collective-permute-start(bf16[20,32,128]{2,1,0:T(8,128)(2,1)S(1)} %bitcast.43), channel_id=1, source_target_pairs={{0,4},{1,5},{2,6},{3,7},{4,0},{5,1},{6,2},{7,3},{8,12},{9,13},{10,... | collective-permute-start | bytes 491528 | tf_op jit(solution)/shard_map/ppermute | solution.py:347
  8.9 13.5 %collective-permute-start.3 = (bf16[20,32,128]{2,1,0:T(8,128)(2,1)S(1)}, bf16[20,32,128]{2,1,0:T(8,128)(2,1)S(1)}, u32[]{:S(2)}, u32[]{:S(2)}) collective-permute-start(bf16[20,32,128]{2,1,0:T(8,128)(2,1)S(1)} %bitcast.42), channel_id=1, source_target_pairs={{0,10},{1,11},{2,8},{3,9},{4,14},{5,15},{6,12},{7,13},{8,2},{9,3},... | collective-permute-start | bytes 491528 | tf_op jit(solution)/shard_map/ppermute | solution.py:347
  10.2 21.1 %collective-permute-start.4 = (bf16[20,32,128]{2,1,0:T(8,128)(2,1)S(1)}, bf16[20,32,128]{2,1,0:T(8,128)(2,1)S(1)}, u32[]{:S(2)}, u32[]{:S(2)}) collective-permute-start(bf16[20,32,128]{2,1,0:T(8,128)(2,1)S(1)} %bitcast.41), channel_id=1, source_target_pairs={{0,6},{1,7},{2,4},{3,5},{4,2},{5,3},{6,0},{7,1},{8,14},{9,15},{10,... | collective-permute-start | bytes 491528 | tf_op jit(solution)/shard_map/ppermute | solution.py:347
  13.5 17.9 %collective-permute-start.5 = (bf16[20,32,128]{2,1,0:T(8,128)(2,1)S(1)}, bf16[20,32,128]{2,1,0:T(8,128)(2,1)S(1)}, u32[]{:S(2)}, u32[]{:S(2)}) collective-permute-start(bf16[20,32,128]{2,1,0:T(8,128)(2,1)S(1)} %bitcast.40), channel_id=1, source_target_pairs={{0,12},{1,13},{2,14},{3,15},{4,8},{5,9},{6,10},{7,11},{8,4},{9,5},... | collective-permute-start | bytes 491528 | tf_op jit(solution)/shard_map/ppermute | solution.py:347
  17.4 14.0 %collective-permute-start.6 = (bf16[20,32,128]{2,1,0:T(8,128)(2,1)S(1)}, bf16[20,32,128]{2,1,0:T(8,128)(2,1)S(1)}, u32[]{:S(2)}, u32[]{:S(2)}) collective-permute-start(bf16[20,32,128]{2,1,0:T(8,128)(2,1)S(1)} %bitcast.39), channel_id=1, source_target_pairs={{0,2},{1,3},{2,0},{3,1},{4,6},{5,7},{6,4},{7,5},{8,10},{9,11},{10,... | collective-permute-start | bytes 491528 | tf_op jit(solution)/shard_map/ppermute | solution.py:347
  19.0 13.0 %collective-permute-start.7 = (bf16[2,20,16,128]{3,2,1,0:T(8,128)(2,1)S(1)}, bf16[2,20,16,128]{3,2,1,0:T(8,128)(2,1)S(1)}, u32[]{:S(2)}, u32[]{:S(2)}) collective-permute-start(bf16[2,20,16,128]{3,2,1,0:T(8,128)(2,1)S(1)} %pad_maximum_fusion), channel_id=1, source_target_pairs={{0,14},{1,15},{2,12},{3,13},{4,10},{5,11},{6,8},{7,9},{8,6},{9,7},... | collective-permute-start | bytes 491528 | tf_op jit(solution)/shard_map/ppermute | solution.py:347
  22.4 9.6 %collective-permute-start.8 = (bf16[2,20,16,128]{3,2,1,0:T(8,128)(2,1)S(1)}, bf16[2,20,16,128]{3,2,1,0:T(8,128)(2,1)S(1)}, u32[]{:S(2)}, u32[]{:S(2)}) collective-permute-start(bf16[2,20,16,128]{3,2,1,0:T(8,128)(2,1)S(1)} %pad_maximum_fusion.1), channel_id=1, source_target_pairs={{0,1},{1,0},{2,3},{3,2},{4,5},{5,4},{6,7},{7,6},{8,9},{9,8},{10,11... | collective-permute-start | bytes 491528 | tf_op jit(solution)/shard_map/ppermute | solution.py:347
  31.3 1.5 %collective-permute-start.9 = (bf16[2,20,16,128]{3,2,1,0:T(8,128)(2,1)S(1)}, bf16[2,20,16,128]{3,2,1,0:T(8,128)(2,1)S(1)}, u32[]{:S(2)}, u32[]{:S(2)}) collective-permute-start(bf16[2,20,16,128]{3,2,1,0:T(8,128)(2,1)S(1)} %pad_maximum_fusion.2), channel_id=1, source_target_pairs={{0,1},{1,0},{2,3},{3,2},{4,5},{5,4},{6,7},{7,6},{8,9},{9,8},{10,11... | collective-permute-start | bytes 491528 | tf_op jit(solution)/shard_map/ppermute | solution.py:347
  31.5 1.6 %collective-permute-start.10 = (bf16[2,20,16,128]{3,2,1,0:T(8,128)(2,1)S(1)}, bf16[2,20,16,128]{3,2,1,0:T(8,128)(2,1)S(1)}, u32[]{:S(2)}, u32[]{:S(2)}) collective-permute-start(bf16[2,20,16,128]{3,2,1,0:T(8,128)(2,1)S(1)} %pad_maximum_fusion.3), channel_id=1, source_target_pairs={{0,1},{1,0},{2,3},{3,2},{4,5},{5,4},{6,7},{7,6},{8,9},{9,8},{10,11... | collective-permute-start | bytes 491528 | tf_op jit(solution)/shard_map/ppermute | solution.py:347
  37.0 1.3 %collective-permute-start.11 = (f32[8,128]{1,0:T(8,128)S(1)}, f32[8,128]{1,0:T(8,128)S(1)}, u32[]{:S(2)}, u32[]{:S(2)}) collective-permute-start(f32[8,128]{1,0:T(8,128)S(1)} %prune.1), channel_id=1, source_target_pairs={{0,1},{1,0},{2,3},{3,2},{4,5},{5,4},{6,7},{7,6},{8,9},{9,8},{10,11... | collective-permute-start | bytes 12296 | tf_op jit(solution)/shard_map/ppermute | solution.py:370
  38.3 5.7 %collective-permute-start.14 = (f32[8,128]{1,0:T(8,128)S(1)}, f32[8,128]{1,0:T(8,128)S(1)}, u32[]{:S(2)}, u32[]{:S(2)}) collective-permute-start(f32[8,128]{1,0:T(8,128)S(1)} %add.29), channel_id=1, source_target_pairs={{0,15},{1,14},{2,13},{3,12},{4,11},{5,10},{6,9},{7,8},{8,7},{9,6},... | collective-permute-start | bytes 12296 | tf_op jit(solution)/shard_map/ppermute | solution.py:370
  40.6 4.8 %collective-permute-start.13 = (f32[8,128]{1,0:T(8,128)S(1)}, f32[8,128]{1,0:T(8,128)S(1)}, u32[]{:S(2)}, u32[]{:S(2)}) collective-permute-start(f32[8,128]{1,0:T(8,128)S(1)} %add.29), channel_id=1, source_target_pairs={{0,13},{1,12},{2,15},{3,14},{4,9},{5,8},{6,11},{7,10},{8,5},{9,4},... | collective-permute-start | bytes 12296 | tf_op jit(solution)/shard_map/ppermute | solution.py:370
  41.6 3.8 %collective-permute-start.12 = (f32[8,128]{1,0:T(8,128)S(1)}, f32[8,128]{1,0:T(8,128)S(1)}, u32[]{:S(2)}, u32[]{:S(2)}) collective-permute-start(f32[8,128]{1,0:T(8,128)S(1)} %add.29), channel_id=1, source_target_pairs={{0,3},{1,2},{2,1},{3,0},{4,7},{5,6},{6,5},{7,4},{8,11},{9,10},{10,... | collective-permute-start | bytes 12296 | tf_op jit(solution)/shard_map/ppermute | solution.py:370
  45.4 3.1 %collective-permute-start.15 = (f32[8,128]{1,0:T(8,128)S(1)}, f32[8,128]{1,0:T(8,128)S(1)}, u32[]{:S(2)}, u32[]{:S(2)}) collective-permute-start(f32[8,128]{1,0:T(8,128)S(1)} %add_add_fusion), channel_id=1, source_target_pairs={{0,5},{1,4},{2,7},{3,6},{4,1},{5,0},{6,3},{7,2},{8,13},{9,12},{10,... | collective-permute-start | bytes 12296 | tf_op jit(solution)/shard_map/ppermute | solution.py:370

commit v8 on v7

--- a/solution.py
+++ b/solution.py
@@ -28,7 +28,7 @@
     (weight_ref, length_ref, toward_ref), piece_refs = refs[:3], refs[3 : 3 + held]
     out_ref, wide_ref, *refs = refs[3 + held :]
     (
-        rate_ref, slope_ref, sums_ref, dsums_ref, y_ref, dy_ref, adj_ref, dadj_ref, norm_ref, grad_ref, curve_ref,
+        rate_ref, slope_ref, hold_ref, turn_ref, sums_ref, dsums_ref, y_ref, dy_ref, adj_ref, dadj_ref, norm_ref, grad_ref, curve_ref,
     ) = refs
     rows = states * 4
     me = me_ref[0]
@@ -47,6 +47,9 @@
 
     rate_ref[...] = column((grow - 1.0) / states)
     slope_ref[...] = column(decay * toward * grow / states)
+    share = (grow - 1.0) / states + 1.0 / states
+    hold_ref[...] = column(0.5 / share)
+    turn_ref[...] = column(decay * toward)
     unused = jnp.zeros((grad_ref.shape[0] - branches * ROWS, LANES), F32)
     grad_ref[branches * ROWS :, :] = unused
     curve_ref[branches * ROWS :, :] = unused
@@ -134,12 +137,11 @@
     dseed = -(dtotal * seed) * seed
 
     def record(row_at, total, dtotal, half, dhalf):
-        share = row(rate_ref, row_at) + 1.0 / states
         both_totals = total * half
         here = pl.ds(pl.multiple_of(row_at * ROWS, ROWS), ROWS)
-        grad_ref[here, :] = weight * (share * both_totals - 0.5)
+        grad_ref[here, :] = weight * (both_totals - row(hold_ref, row_at))
         change = total * dhalf if dtotal is None else dtotal * half + total * dhalf
-        curve_ref[here, :] = weight * (share * change + row(slope_ref, row_at) * both_totals)
+        curve_ref[here, :] = weight * (change + row(turn_ref, row_at) * both_totals)
 
     def down(at, ybar, dybar):
         half, dhalf = part_sum(ybar), part_sum(dybar)
@@ -186,7 +188,7 @@
 
     def over_sites(ref):
         rows = part_sum([ref[pl.ds(part, LANES, ROWS), :] for part in range(ROWS)])
-        return jnp.sum(jnp.transpose(rows), axis=0, keepdims=True)[:, :branches] * decay
+        return jnp.sum(jnp.transpose(rows), axis=0, keepdims=True)[:, :branches] * (decay * share)
 
     grad, curve = over_sites(grad_ref), over_sites(curve_ref)
     out_ref[...] = jnp.zeros_like(out_ref)
@@ -213,6 +215,8 @@
         out_shape=jax.ShapeDtypeStruct((ROWS, LANES), F32),
         scratch_shapes=[
             pltpu.VMEM((tips * states * 4, LANES), F32),
+            pltpu.VMEM((LANES, LANES), F32),
+            pltpu.VMEM((LANES, LANES), F32),
             pltpu.VMEM((LANES, LANES), F32),
             pltpu.VMEM((LANES, LANES), F32),
             pltpu.VMEM((branches, ROWS, LANES), F32),

time: 49.2 us -> 49.2 us (level)
  no operation moved by 1% of the time
where the time goes in v8:
time: 49.2 us; the launch traced here: 49 us
  starting transfers between devices  21.3 us (43%)
  waiting for transfers between devices  19.9 us (40%)
  Pallas kernels  6.34 us (13%)
  between operations  0.78 us (2%)
  other arithmetic  0.61 us (1%)
    ppermute x11, waiting for transfers between devices, swap(): return lax.ppermute(block, 'sites', [(i, i ^ step) for i in range(peers)])  15.1 us
    ppermute x11, starting transfers between devices, swap(): return lax.ppermute(block, 'sites', [(i, i ^ step) for i in range(peers)])  14.7 us
    ppermute x5, starting transfers between devices, total_over_sites(): lax.ppermute(part, 'sites', [(i, i ^ step) for i in range(peers)])  6.67 us
    ppermute x5, waiting for transfers between devices, total_over_sites(): lax.ppermute(part, 'sites', [(i, i ^ step) for i in range(peers)])  4.79 us
    pallas_call x1, Pallas kernels, prune(): pl.pallas_call(functools.partial(prune_kernel, unpack=unpack, held=len(pi...  3.99 us
    pallas_call x2, Pallas kernels, cut(): pl.pallas_call(functools.partial(cut_kernel, firsts=firsts), in_specs=[pl...  2.35 us
  transfers between devices with their start and end apart: 16, of which 9 were waited for; matrix products, arithmetic and copies ran while one was open for 0% of the time, Pallas kernels for 3%

profile of v8, /device:TPU:0, one launch (start us, length us, event | category | flops | bytes accessed | tf_op | source)
XLA Modules:
  0.0 49.0 jit_solution(3570920721224112194)
XLA Ops:
  0.6 0.9 %cut.2.after_ref = bf16[1,20,32,128]{3,2,1,0:T(8,128)(2,1)S(1)} custom-call(s32[1]{0:T(128)} %bitcast.me_ref.after_ref, bf16[20,256,128]{2,1,0:T(8,128)(2,1)} %bitcast.44, s32[1]{0:T(128)} %bitcast.me_ref.after_ref), custom_call_target="tpu_custom_call" | custom-call | tf_op jit(solution)/shard_map/cut/pallas_call | solution.py:305
  1.6 4.1 %collective-permute-start.1 = (bf16[20,32,128]{2,1,0:T(8,128)(2,1)S(1)}, bf16[20,32,128]{2,1,0:T(8,128)(2,1)S(1)}, u32[]{:S(2)}, u32[]{:S(2)}) collective-permute-start(bf16[20,32,128]{2,1,0:T(8,128)(2,1)S(1)} %bitcast.34), channel_id=1, source_target_pairs={{0,8},{1,9},{2,10},{3,11},{4,12},{5,13},{6,14},{7,15},{8,0},{9,1},... | collective-permute-start | bytes 491528 | tf_op jit(solution)/shard_map/ppermute | solution.py:351
  5.7 1.4 %cut.3 = (bf16[1,20,32,128]{3,2,1,0:T(8,128)(2,1)S(1)}, bf16[1,20,32,128]{3,2,1,0:T(8,128)(2,1)S(1)}, bf16[1,20,32,128]{3,2,1,0:T(8,128)(2,1)S(1)}, bf16[1,20,32...) custom-call(s32[1]{0:T(128)} %bitcast.me_ref.after_ref, ...), custom_call_target="tpu_custom_call" | custom-call | tf_op jit(solution)/shard_map/cut/pallas_call | solution.py:305
  7.1 0.0 copy-start
  7.1 0.0 copy-start.1
  7.1 0.0 copy-start.2
  7.1 0.0 copy-start.3
  7.2 0.1 collective-permute-start
  7.2 1.6 %collective-permute-start.2 = (bf16[20,32,128]{2,1,0:T(8,128)(2,1)S(1)}, bf16[20,32,128]{2,1,0:T(8,128)(2,1)S(1)}, u32[]{:S(2)}, u32[]{:S(2)}) collective-permute-start(bf16[20,32,128]{2,1,0:T(8,128)(2,1)S(1)} %bitcast.43), channel_id=1, source_target_pairs={{0,4},{1,5},{2,6},{3,7},{4,0},{5,1},{6,2},{7,3},{8,12},{9,13},{10,... | collective-permute-start | bytes 491528 | tf_op jit(solution)/shard_map/ppermute | solution.py:351
  8.9 1.3 %collective-permute-start.3 = (bf16[20,32,128]{2,1,0:T(8,128)(2,1)S(1)}, bf16[20,32,128]{2,1,0:T(8,128)(2,1)S(1)}, u32[]{:S(2)}, u32[]{:S(2)}) collective-permute-start(bf16[20,32,128]{2,1,0:T(8,128)(2,1)S(1)} %bitcast.42), channel_id=1, source_target_pairs={{0,10},{1,11},{2,8},{3,9},{4,14},{5,15},{6,12},{7,13},{8,2},{9,3},... | collective-permute-start | bytes 491528 | tf_op jit(solution)/shard_map/ppermute | solution.py:351
  10.2 0.1 collective-permute-start.4
  10.3 3.2 %collective-permute-done.1.refs_5_ = bf16[20,32,128]{2,1,0:T(8,128)(2,1)S(1)} collective-permute-done((bf16[20,32,128]{2,1,0:T(8,128)(2,1)S(1)}, bf16[20,32,128]{2,1,0:T(8,128)(2,1)S(1)}, u32[]{:S(2)}, u32[]{:S(2)}) %collective-permute-start.1) | collective-permute-done | bytes 163872 | tf_op jit(solution)/shard_map/ppermute | solution.py:351
  13.5 3.9 %collective-permute-start.5 = (bf16[20,32,128]{2,1,0:T(8,128)(2,1)S(1)}, bf16[20,32,128]{2,1,0:T(8,128)(2,1)S(1)}, u32[]{:S(2)}, u32[]{:S(2)}) collective-permute-start(bf16[20,32,128]{2,1,0:T(8,128)(2,1)S(1)} %bitcast.40), channel_id=1, source_target_pairs={{0,12},{1,13},{2,14},{3,15},{4,8},{5,9},{6,10},{7,11},{8,4},{9,5},... | collective-permute-start | bytes 491528 | tf_op jit(solution)/shard_map/ppermute | solution.py:351
  17.4 0.0 collective-permute-done.refs_4_
  17.4 1.6 %collective-permute-start.6 = (bf16[20,32,128]{2,1,0:T(8,128)(2,1)S(1)}, bf16[20,32,128]{2,1,0:T(8,128)(2,1)S(1)}, u32[]{:S(2)}, u32[]{:S(2)}) collective-permute-start(bf16[20,32,128]{2,1,0:T(8,128)(2,1)S(1)} %bitcast.39), channel_id=1, source_target_pairs={{0,2},{1,3},{2,0},{3,1},{4,6},{5,7},{6,4},{7,5},{8,10},{9,11},{10,... | collective-permute-start | bytes 491528 | tf_op jit(solution)/shard_map/ppermute | solution.py:351
  19.0 0.0 collective-permute-done.2.refs_6_
  19.0 1.4 %collective-permute-start.7 = (bf16[2,20,16,128]{3,2,1,0:T(8,128)(2,1)S(1)}, bf16[2,20,16,128]{3,2,1,0:T(8,128)(2,1)S(1)}, u32[]{:S(2)}, u32[]{:S(2)}) collective-permute-start(bf16[2,20,16,128]{3,2,1,0:T(8,128)(2,1)S(1)} %pad_maximum_fusion), channel_id=1, source_target_pairs={{0,14},{1,15},{2,12},{3,13},{4,10},{5,11},{6,8},{7,9},{8,6},{9,7},... | collective-permute-start | bytes 491528 | tf_op jit(solution)/shard_map/ppermute | solution.py:351
  20.4 2.0 %collective-permute-done.3.refs_7_ = bf16[20,32,128]{2,1,0:T(8,128)(2,1)S(1)} collective-permute-done((bf16[20,32,128]{2,1,0:T(8,128)(2,1)S(1)}, bf16[20,32,128]{2,1,0:T(8,128)(2,1)S(1)}, u32[]{:S(2)}, u32[]{:S(2)}) %collective-permute-start.3) | collective-permute-done | bytes 163872 | tf_op jit(solution)/shard_map/ppermute | solution.py:351
  22.4 0.0 collective-permute-start.8
  22.4 8.8 %collective-permute-done.4.refs_8_ = bf16[20,32,128]{2,1,0:T(8,128)(2,1)S(1)} collective-permute-done((bf16[20,32,128]{2,1,0:T(8,128)(2,1)S(1)}, bf16[20,32,128]{2,1,0:T(8,128)(2,1)S(1)}, u32[]{:S(2)}, u32[]{:S(2)}) %collective-permute-start.4) | collective-permute-done | bytes 163872 | tf_op jit(solution)/shard_map/ppermute | solution.py:351
  31.3 0.1 collective-permute-start.9
  31.4 0.0 collective-permute-done.5.refs_9_
  31.4 0.0 collective-permute-done.6.refs_10_
  31.5 0.5 %collective-permute-start.10 = (bf16[2,20,16,128]{3,2,1,0:T(8,128)(2,1)S(1)}, bf16[2,20,16,128]{3,2,1,0:T(8,128)(2,1)S(1)}, u32[]{:S(2)}, u32[]{:S(2)}) collective-permute-start(bf16[2,20,16,128]{3,2,1,0:T(8,128)(2,1)S(1)} %pad_maximum_fusion.3), channel_id=1, source_target_pairs={{0,1},{1,0},{2,3},{3,2},{4,5},{5,4},{6,7},{7,6},{8,9},{9,8},{10,11... | collective-permute-start | bytes 491528 | tf_op jit(solution)/shard_map/ppermute | solution.py:351
  32.0 0.0 collective-permute-done.7.refs_11_
  32.0 0.0 collective-permute-done.8.refs_12_
  32.0 0.7 %collective-permute-done.9.refs_13_ = bf16[2,20,16,128]{3,2,1,0:T(8,128)(2,1)S(1)} collective-permute-done((bf16[2,20,16,128]{3,2,1,0:T(8,128)(2,1)S(1)}, bf16[2,20,16,128]{3,2,1,0:T(8,128)(2,1)S(1)}, u32[]{:S(2)}, u32[]{:S(2)}) %collective-permute-start.9) | collective-permute-done | bytes 163872 | tf_op jit(solution)/shard_map/ppermute | solution.py:351
  32.7 0.3 collective-permute-done.10.refs_14_
  33.0 0.0 copy-done
  33.0 0.0 copy-done.1
  33.0 0.0 copy-done.2
  33.0 0.0 copy-done.3
  33.0 4.0 %prune.1 = f32[8,128]{1,0:T(8,128)S(1)} custom-call(s32[64]{0:T(128)S(1)} %copy-done.1, s32[1]{0:T(128)} %bitcast.me_ref.after_ref, s32[1,512]{1,0:T(1,128)S(1)} %bitcast.36, f32[1,126]{1,0:T(1,128)S(1)} %bitcast.37, f32[1,126]{1,0:T(1,128)S(1)} %bitcast.38, bf16[20,16,128]{2,1,0:T(8,128)(2,1)S(1)} %bitcast.35, ...), custom_call_target="tpu_custom_call" | custom-call | tf_op jit(solution)/shard_map/prune/pallas_call | solution.py:209
  37.0 0.4 collective-permute-start.11
  37.5 0.8 %collective-permute-done.11 = f32[8,128]{1,0:T(8,128)S(1)} collective-permute-done((f32[8,128]{1,0:T(8,128)S(1)}, f32[8,128]{1,0:T(8,128)S(1)}, u32[]{:S(2)}, u32[]{:S(2)}) %collective-permute-start.11) | collective-permute-done | bytes 4128 | tf_op jit(solution)/shard_map/ppermute | solution.py:374
  38.3 2.3 %collective-permute-start.14 = (f32[8,128]{1,0:T(8,128)S(1)}, f32[8,128]{1,0:T(8,128)S(1)}, u32[]{:S(2)}, u32[]{:S(2)}) collective-permute-start(f32[8,128]{1,0:T(8,128)S(1)} %add.29), channel_id=1, source_target_pairs={{0,15},{1,14},{2,13},{3,12},{4,11},{5,10},{6,9},{7,8},{8,7},{9,6},... | collective-permute-start | bytes 12296 | tf_op jit(solution)/shard_map/ppermute | solution.py:374
  40.6 1.1 %collective-permute-start.13 = (f32[8,128]{1,0:T(8,128)S(1)}, f32[8,128]{1,0:T(8,128)S(1)}, u32[]{:S(2)}, u32[]{:S(2)}) collective-permute-start(f32[8,128]{1,0:T(8,128)S(1)} %add.29), channel_id=1, source_target_pairs={{0,13},{1,12},{2,15},{3,14},{4,9},{5,8},{6,11},{7,10},{8,5},{9,4},... | collective-permute-start | bytes 12296 | tf_op jit(solution)/shard_map/ppermute | solution.py:374
  41.6 1.6 %collective-permute-start.12 = (f32[8,128]{1,0:T(8,128)S(1)}, f32[8,128]{1,0:T(8,128)S(1)}, u32[]{:S(2)}, u32[]{:S(2)}) collective-permute-start(f32[8,128]{1,0:T(8,128)S(1)} %add.29), channel_id=1, source_target_pairs={{0,3},{1,2},{2,1},{3,0},{4,7},{5,6},{6,5},{7,4},{8,11},{9,10},{10,... | collective-permute-start | bytes 12296 | tf_op jit(solution)/shard_map/ppermute | solution.py:374
  43.3 0.8 %collective-permute-done.14 = f32[8,128]{1,0:T(8,128)S(1)} collective-permute-done((f32[8,128]{1,0:T(8,128)S(1)}, f32[8,128]{1,0:T(8,128)S(1)}, u32[]{:S(2)}, u32[]{:S(2)}) %collective-permute-start.14) | collective-permute-done | bytes 4128 | tf_op jit(solution)/shard_map/ppermute | solution.py:374
  44.0 1.4 %collective-permute-done.13 = f32[8,128]{1,0:T(8,128)S(1)} collective-permute-done((f32[8,128]{1,0:T(8,128)S(1)}, f32[8,128]{1,0:T(8,128)S(1)}, u32[]{:S(2)}, u32[]{:S(2)}) %collective-permute-start.13) | collective-permute-done | bytes 4128 | tf_op jit(solution)/shard_map/ppermute | solution.py:374
  45.4 0.0 collective-permute-done.12
  45.4 1.3 %collective-permute-start.15 = (f32[8,128]{1,0:T(8,128)S(1)}, f32[8,128]{1,0:T(8,128)S(1)}, u32[]{:S(2)}, u32[]{:S(2)}) collective-permute-start(f32[8,128]{1,0:T(8,128)S(1)} %add_add_fusion), channel_id=1, source_target_pairs={{0,5},{1,4},{2,7},{3,6},{4,1},{5,0},{6,3},{7,2},{8,13},{9,12},{10,... | collective-permute-start | bytes 12296 | tf_op jit(solution)/shard_map/ppermute | solution.py:374
  46.7 1.8 %collective-permute-done.15 = f32[8,128]{1,0:T(8,128)S(1)} collective-permute-done((f32[8,128]{1,0:T(8,128)S(1)}, f32[8,128]{1,0:T(8,128)S(1)}, u32[]{:S(2)}, u32[]{:S(2)}) %collective-permute-start.15) | collective-permute-done | bytes 4128 | tf_op jit(solution)/shard_map/ppermute | solution.py:374
  48.5 0.5 %fusion.1 = (f32[126]{0:T(128)}, f32[126]{0:T(128)}) fusion(f32[8,128]{1,0:T(8,128)S(1)} %add.33), kind=kLoop, calls=%fused_computation.14 | loop fusion | flops 252 | bytes 2520 | tf_op jit(solution)/shard_map/div | solution.py:393
  (14 shorter events, 0.1 us)
Async XLA Ops:
  1.6 11.9 %collective-permute-start.1 = (bf16[20,32,128]{2,1,0:T(8,128)(2,1)S(1)}, bf16[20,32,128]{2,1,0:T(8,128)(2,1)S(1)}, u32[]{:S(2)}, u32[]{:S(2)}) collective-permute-start(bf16[20,32,128]{2,1,0:T(8,128)(2,1)S(1)} %bitcast.34), channel_id=1, source_target_pairs={{0,8},{1,9},{2,10},{3,11},{4,12},{5,13},{6,14},{7,15},{8,0},{9,1},... | collective-permute-start | bytes 491528 | tf_op jit(solution)/shard_map/ppermute | solution.py:351
  7.1 25.9 %copy-start = (s32[512]{0:T(512)S(1)}, s32[512]{0:T(512)}, u32[]{:S(2)}) copy-start(s32[512]{0:T(512)} %param.7) | copy-start | bytes 6148
  7.1 25.9 %copy-start.1 = (s32[64]{0:T(128)S(1)}, s32[64]{0:T(128)}, u32[]{:S(2)}) copy-start(s32[64]{0:T(128)} %order_ref.1) | copy-start | bytes 772
  7.1 25.9 %copy-start.2 = (f32[126]{0:T(128)S(1)}, f32[126]{0:T(128)}, u32[]{:S(2)}) copy-start(f32[126]{0:T(128)} %param.8) | copy-start | bytes 1516
  7.1 25.9 %copy-start.3 = (f32[126]{0:T(128)S(1)}, f32[126]{0:T(128)}, u32[]{:S(2)}) copy-start(f32[126]{0:T(128)} %param.9) | copy-start | bytes 1516
  7.2 10.2 %collective-permute-start = (bf16[2,20,16,128]{3,2,1,0:T(8,128)(2,1)S(1)}, bf16[2,20,16,128]{3,2,1,0:T(8,128)(2,1)S(1)}, u32[]{:S(2)}, u32[]{:S(2)}) collective-permute-start(bf16[2,20,16,128]{3,2,1,0:T(8,128)(2,1)S(1)} %get-tuple-element.11), channel_id=1, source_target_pairs={{0,1},{1,0},{2,3},{3,2},{4,5},{5,4},{6,7},{7,6},{8,9},{9,8},{10,11... | collective-permute-start | bytes 491528 | tf_op jit(solution)/shard_map/ppermute | solution.py:351
  7.2 11.8 %collective-permute-start.2 = (bf16[20,32,128]{2,1,0:T(8,128)(2,1)S(1)}, bf16[20,32,128]{2,1,0:T(8,128)(2,1)S(1)}, u32[]{:S(2)}, u32[]{:S(2)}) collective-permute-start(bf16[20,32,128]{2,1,0:T(8,128)(2,1)S(1)} %bitcast.43), channel_id=1, source_target_pairs={{0,4},{1,5},{2,6},{3,7},{4,0},{5,1},{6,2},{7,3},{8,12},{9,13},{10,... | collective-permute-start | bytes 491528 | tf_op jit(solution)/shard_map/ppermute | solution.py:351
  8.9 13.5 %collective-permute-start.3 = (bf16[20,32,128]{2,1,0:T(8,128)(2,1)S(1)}, bf16[20,32,128]{2,1,0:T(8,128)(2,1)S(1)}, u32[]{:S(2)}, u32[]{:S(2)}) collective-permute-start(bf16[20,32,128]{2,1,0:T(8,128)(2,1)S(1)} %bitcast.42), channel_id=1, source_target_pairs={{0,10},{1,11},{2,8},{3,9},{4,14},{5,15},{6,12},{7,13},{8,2},{9,3},... | collective-permute-start | bytes 491528 | tf_op jit(solution)/shard_map/ppermute | solution.py:351
  10.2 21.1 %collective-permute-start.4 = (bf16[20,32,128]{2,1,0:T(8,128)(2,1)S(1)}, bf16[20,32,128]{2,1,0:T(8,128)(2,1)S(1)}, u32[]{:S(2)}, u32[]{:S(2)}) collective-permute-start(bf16[20,32,128]{2,1,0:T(8,128)(2,1)S(1)} %bitcast.41), channel_id=1, source_target_pairs={{0,6},{1,7},{2,4},{3,5},{4,2},{5,3},{6,0},{7,1},{8,14},{9,15},{10,... | collective-permute-start | bytes 491528 | tf_op jit(solution)/shard_map/ppermute | solution.py:351
  13.5 17.9 %collective-permute-start.5 = (bf16[20,32,128]{2,1,0:T(8,128)(2,1)S(1)}, bf16[20,32,128]{2,1,0:T(8,128)(2,1)S(1)}, u32[]{:S(2)}, u32[]{:S(2)}) collective-permute-start(bf16[20,32,128]{2,1,0:T(8,128)(2,1)S(1)} %bitcast.40), channel_id=1, source_target_pairs={{0,12},{1,13},{2,14},{3,15},{4,8},{5,9},{6,10},{7,11},{8,4},{9,5},... | collective-permute-start | bytes 491528 | tf_op jit(solution)/shard_map/ppermute | solution.py:351
  17.4 14.0 %collective-permute-start.6 = (bf16[20,32,128]{2,1,0:T(8,128)(2,1)S(1)}, bf16[20,32,128]{2,1,0:T(8,128)(2,1)S(1)}, u32[]{:S(2)}, u32[]{:S(2)}) collective-permute-start(bf16[20,32,128]{2,1,0:T(8,128)(2,1)S(1)} %bitcast.39), channel_id=1, source_target_pairs={{0,2},{1,3},{2,0},{3,1},{4,6},{5,7},{6,4},{7,5},{8,10},{9,11},{10,... | collective-permute-start | bytes 491528 | tf_op jit(solution)/shard_map/ppermute | solution.py:351
  19.0 13.0 %collective-permute-start.7 = (bf16[2,20,16,128]{3,2,1,0:T(8,128)(2,1)S(1)}, bf16[2,20,16,128]{3,2,1,0:T(8,128)(2,1)S(1)}, u32[]{:S(2)}, u32[]{:S(2)}) collective-permute-start(bf16[2,20,16,128]{3,2,1,0:T(8,128)(2,1)S(1)} %pad_maximum_fusion), channel_id=1, source_target_pairs={{0,14},{1,15},{2,12},{3,13},{4,10},{5,11},{6,8},{7,9},{8,6},{9,7},... | collective-permute-start | bytes 491528 | tf_op jit(solution)/shard_map/ppermute | solution.py:351
  22.4 9.6 %collective-permute-start.8 = (bf16[2,20,16,128]{3,2,1,0:T(8,128)(2,1)S(1)}, bf16[2,20,16,128]{3,2,1,0:T(8,128)(2,1)S(1)}, u32[]{:S(2)}, u32[]{:S(2)}) collective-permute-start(bf16[2,20,16,128]{3,2,1,0:T(8,128)(2,1)S(1)} %pad_maximum_fusion.1), channel_id=1, source_target_pairs={{0,1},{1,0},{2,3},{3,2},{4,5},{5,4},{6,7},{7,6},{8,9},{9,8},{10,11... | collective-permute-start | bytes 491528 | tf_op jit(solution)/shard_map/ppermute | solution.py:351
  31.3 1.5 %collective-permute-start.9 = (bf16[2,20,16,128]{3,2,1,0:T(8,128)(2,1)S(1)}, bf16[2,20,16,128]{3,2,1,0:T(8,128)(2,1)S(1)}, u32[]{:S(2)}, u32[]{:S(2)}) collective-permute-start(bf16[2,20,16,128]{3,2,1,0:T(8,128)(2,1)S(1)} %pad_maximum_fusion.2), channel_id=1, source_target_pairs={{0,1},{1,0},{2,3},{3,2},{4,5},{5,4},{6,7},{7,6},{8,9},{9,8},{10,11... | collective-permute-start | bytes 491528 | tf_op jit(solution)/shard_map/ppermute | solution.py:351
  31.5 1.6 %collective-permute-start.10 = (bf16[2,20,16,128]{3,2,1,0:T(8,128)(2,1)S(1)}, bf16[2,20,16,128]{3,2,1,0:T(8,128)(2,1)S(1)}, u32[]{:S(2)}, u32[]{:S(2)}) collective-permute-start(bf16[2,20,16,128]{3,2,1,0:T(8,128)(2,1)S(1)} %pad_maximum_fusion.3), channel_id=1, source_target_pairs={{0,1},{1,0},{2,3},{3,2},{4,5},{5,4},{6,7},{7,6},{8,9},{9,8},{10,11... | collective-permute-start | bytes 491528 | tf_op jit(solution)/shard_map/ppermute | solution.py:351
  37.0 1.3 %collective-permute-start.11 = (f32[8,128]{1,0:T(8,128)S(1)}, f32[8,128]{1,0:T(8,128)S(1)}, u32[]{:S(2)}, u32[]{:S(2)}) collective-permute-start(f32[8,128]{1,0:T(8,128)S(1)} %prune.1), channel_id=1, source_target_pairs={{0,1},{1,0},{2,3},{3,2},{4,5},{5,4},{6,7},{7,6},{8,9},{9,8},{10,11... | collective-permute-start | bytes 12296 | tf_op jit(solution)/shard_map/ppermute | solution.py:374
  38.3 5.7 %collective-permute-start.14 = (f32[8,128]{1,0:T(8,128)S(1)}, f32[8,128]{1,0:T(8,128)S(1)}, u32[]{:S(2)}, u32[]{:S(2)}) collective-permute-start(f32[8,128]{1,0:T(8,128)S(1)} %add.29), channel_id=1, source_target_pairs={{0,15},{1,14},{2,13},{3,12},{4,11},{5,10},{6,9},{7,8},{8,7},{9,6},... | collective-permute-start | bytes 12296 | tf_op jit(solution)/shard_map/ppermute | solution.py:374
  40.6 4.8 %collective-permute-start.13 = (f32[8,128]{1,0:T(8,128)S(1)}, f32[8,128]{1,0:T(8,128)S(1)}, u32[]{:S(2)}, u32[]{:S(2)}) collective-permute-start(f32[8,128]{1,0:T(8,128)S(1)} %add.29), channel_id=1, source_target_pairs={{0,13},{1,12},{2,15},{3,14},{4,9},{5,8},{6,11},{7,10},{8,5},{9,4},... | collective-permute-start | bytes 12296 | tf_op jit(solution)/shard_map/ppermute | solution.py:374
  41.6 3.8 %collective-permute-start.12 = (f32[8,128]{1,0:T(8,128)S(1)}, f32[8,128]{1,0:T(8,128)S(1)}, u32[]{:S(2)}, u32[]{:S(2)}) collective-permute-start(f32[8,128]{1,0:T(8,128)S(1)} %add.29), channel_id=1, source_target_pairs={{0,3},{1,2},{2,1},{3,0},{4,7},{5,6},{6,5},{7,4},{8,11},{9,10},{10,... | collective-permute-start | bytes 12296 | tf_op jit(solution)/shard_map/ppermute | solution.py:374
  45.4 3.1 %collective-permute-start.15 = (f32[8,128]{1,0:T(8,128)S(1)}, f32[8,128]{1,0:T(8,128)S(1)}, u32[]{:S(2)}, u32[]{:S(2)}) collective-permute-start(f32[8,128]{1,0:T(8,128)S(1)} %add_add_fusion), channel_id=1, source_target_pairs={{0,5},{1,4},{2,7},{3,6},{4,1},{5,0},{6,3},{7,2},{8,13},{9,12},{10,... | collective-permute-start | bytes 12296 | tf_op jit(solution)/shard_map/ppermute | solution.py:374
